TPU v7x, 32 devices: a whole 2x2x4 slice. The times are simulated.
32 devices in a mesh: pipe: 4 (over y, x), dp: 2 (over core), tensor: 4 (over z).
Axes of the slice: x: 2, y: 2, z: 4, core: 2. Of those that a mesh axis runs over, the one named last changes fastest.
Arguments:
- raw_pages: bfloat16 [4, 2, 1200, 2048], P('pipe', 'dp', 'tensor'), may hold values from -40 to 40
- w_merge: float32 [2048, 1024], P(('pipe', 'dp', 'tensor')), may hold values from -0.125 to 0.125
- merge_gain: float32 [2048], P(('pipe', 'dp', 'tensor')), may hold values from 0.5 to 1.5
- merge_bias: float32 [2048], P(('pipe', 'dp', 'tensor')), may hold values from -1.5 to 1.5
- final_gain: float32 [1024], P(('pipe', 'dp', 'tensor')), may hold values from 0.2 to 2
- final_bias: float32 [1024], P(('pipe', 'dp', 'tensor')), may hold values from -3 to 3
- w_qkv: float32 [4, 1024, 3, 1024], P('pipe', 'dp', None, 'tensor'), may hold values from -0.1875 to 0.1875
- w_proj: float32 [4, 1024, 1024], P('pipe', 'tensor', 'dp'), may hold values from -0.75 to 0.75
- w_fc1: float32 [4, 1024, 4096], P('pipe', 'dp', 'tensor'), may hold values from -0.1875 to 0.1875
- w_fc2: float32 [4, 4096, 1024], P('pipe', 'tensor', 'dp'), may hold values from -0.1875 to 0.1875
- qv_bias: float32 [4, 2, 1024], P('pipe', None, 'tensor'), may hold values from -1.5 to 1.5
- fc1_bias: float32 [4, 4096], P('pipe'), may hold values from -1.5 to 1.5
- rel_table: float32 [4, 361, 32], P('pipe', None, 'tensor'), may hold values from -5 to 5
- ln_gain: float32 [4, 2, 1024], P('pipe'), may hold values from 0.5 to 1.5
- ln_bias: float32 [4, 2, 1024], P('pipe'), may hold values from -1.5 to 1.5
- out_bias: float32 [4, 2, 1024], P('pipe'), may hold values from -1.5 to 1.5
- cotangent: bfloat16 [4, 4, 2, 1200, 1024], P('pipe', None, 'dp', 'tensor'), may hold values from -6 to 6
Outputs:
- hidden_states: bfloat16 [4, 4, 2, 1200, 1024], P('pipe', None, 'dp', 'tensor')
- grad_raw: bfloat16 [4, 2, 1200, 2048], P('pipe', 'dp', 'tensor')
- grad_w_merge: float32 [2048, 1024], P(('pipe', 'dp', 'tensor'))
- grad_merge_gain: float32 [2048], P(('pipe', 'dp', 'tensor'))
- grad_merge_bias: float32 [2048], P(('pipe', 'dp', 'tensor'))
- grad_final_gain: float32 [1024], P(('pipe', 'dp', 'tensor'))
- grad_final_bias: float32 [1024], P(('pipe', 'dp', 'tensor'))
- grad_w_qkv: float32 [4, 1024, 3, 1024], P('pipe', 'dp', None, 'tensor')
- grad_w_proj: float32 [4, 1024, 1024], P('pipe', 'tensor', 'dp')
- grad_w_fc1: float32 [4, 1024, 4096], P('pipe', 'dp', 'tensor')
- grad_w_fc2: float32 [4, 4096, 1024], P('pipe', 'tensor', 'dp')
- grad_qv_bias: float32 [4, 2, 1024], P('pipe', None, 'tensor')
- grad_fc1_bias: float32 [4, 4096], P('pipe')
- grad_rel_table: float32 [4, 361, 32], P('pipe', None, 'tensor')
- grad_ln_gain: float32 [4, 2, 1024], P('pipe')
- grad_ln_bias: float32 [4, 2, 1024], P('pipe')
- grad_out_bias: float32 [4, 2, 1024], P('pipe')
All inputs are finite; a program needn't handle non-finite values.
Results may differ from a plain program's by a relative error of at most 0.029.
Values may be sent and summed in bfloat16 or wider, within the bound.
No kernel may reach another device: no remote copies, remote signals or barrier semaphores. Data moves between devices by JAX's collectives and lax.ppermute only.
A program may use at most 192 MiB of HBM per device.

v0:
```python
import jax
import jax.numpy as jnp
import numpy as np
from jax import lax
from jax.sharding import PartitionSpec as P

D = 1024
HEAD = 32
FF = 4096
WIN = 10
SHIFT = 5
WIN_ROWS = 4
WIN_COLS = 3


NORM_EPS = 1e-05


def shifted(value, axis, steps):
    count = lax.axis_size(axis)
    initial, last = (max(0, -steps), min(count, count - steps))
    return lax.ppermute(value, axis, [(source, source + steps) for source in range(initial, last)])


def rel_index(window):
    coords = np.stack(np.meshgrid(np.arange(window), np.arange(window), indexing="ij")).reshape(
        2, -1
    )
    offsets = coords[:, :, None] - coords[:, None, :]
    return ((offsets[0] + window - 1) * (2 * window - 1) + offsets[1] + window - 1).reshape(-1)


def shift_mask(grid_rows, grid_cols, window, shift_now):
    region = np.zeros((grid_rows, grid_cols), np.int64)
    region_id = 0
    for span_rows in (
        (0, grid_rows - window),
        (grid_rows - window, grid_rows - shift_now),
        (grid_rows - shift_now, grid_rows),
    ):
        for span_cols in (
            (0, grid_cols - window),
            (grid_cols - window, grid_cols - shift_now),
            (grid_cols - shift_now, grid_cols),
        ):
            region[span_rows[0] : span_rows[1], span_cols[0] : span_cols[1]] = region_id
            region_id += 1
    blocks = region.reshape(grid_rows // window, window, grid_cols // window, window).transpose(
        0, 2, 1, 3
    )
    blocks = blocks.reshape(-1, window * window)
    return np.where(blocks[:, :, None] == blocks[:, None, :], 0.0, -100.0).astype(np.float32)


def norm_stats(values):
    row_mean = jnp.mean(values, -1, keepdims=True)
    centred = values - row_mean
    rstd_rows = lax.rsqrt(jnp.mean(centred * centred, -1, keepdims=True) + NORM_EPS)
    return (centred * rstd_rows, rstd_rows)


def norm_back(normed, rstd_rows, grad_normed):
    return rstd_rows * (
        grad_normed
        - jnp.mean(grad_normed, -1, keepdims=True)
        - normed * jnp.mean(grad_normed * normed, -1, keepdims=True)
    )


def matmul(left, right):
    return jnp.dot(left, right, preferred_element_type=jnp.float32)


def matmul_tn(left, right):
    return lax.dot_general(
        left, right, (((0,), (0,)), ((), ())), preferred_element_type=jnp.float32
    )


def matmul_nt(left, right):
    return lax.dot_general(
        left, right, (((1,), (1,)), ((), ())), preferred_element_type=jnp.float32
    )


def gelu_exact(values):
    return jax.nn.gelu(values, approximate=False)


def roll_grid(flat_rows, amount):
    grid_view = flat_rows.reshape(WIN * WIN_ROWS, WIN * WIN_COLS, flat_rows.shape[-1])
    grid_view = jnp.roll(jnp.roll(grid_view, amount, 0), amount, 1)
    return grid_view.reshape(flat_rows.shape)


def split_heads(flat_rows):
    channels = flat_rows.shape[-1]
    grid_view = flat_rows.reshape(WIN_ROWS, WIN, WIN_COLS, WIN, channels).transpose(0, 2, 1, 3, 4)
    return grid_view.reshape(WIN_ROWS * WIN_COLS, WIN * WIN, channels // HEAD, HEAD)


def join_heads(blocks):
    channels = blocks.shape[2] * blocks.shape[3]
    grid_view = blocks.reshape(WIN_ROWS, WIN_COLS, WIN, WIN, channels).transpose(0, 2, 1, 3, 4)
    return grid_view.reshape(WIN * WIN_ROWS * WIN * WIN_COLS, channels)


def spread_rows(local_rows):
    return lax.all_gather(local_rows, "tensor", axis=0, tiled=True)


def collect_rows(left, product):
    return lax.psum_scatter(
        product(left).astype(jnp.bfloat16), "tensor", scatter_dimension=0, tiled=True
    ).astype(jnp.float32)


def on_device(
    raw_pages,
    w_merge,
    merge_gain,
    merge_bias,
    final_gain,
    final_bias,
    w_qkv,
    w_proj,
    w_fc1,
    w_fc2,
    qv_bias,
    fc1_bias,
    rel_table,
    ln_gain,
    ln_bias,
    out_bias,
    cotangent,
):
    section_now = lax.axis_index("pipe")
    section_count = lax.axis_size("pipe")
    amount = SHIFT * (section_now % 2)
    mask_weight = (section_now % 2).astype(jnp.float32)
    is_first = section_now == 0
    is_last = section_now == section_count - 1
    rows_here = raw_pages.shape[2]
    owned = raw_pages.shape[0]
    micro_count = cotangent.shape[1]
    scale_factor = HEAD ** (-0.5)
    merge_set = (
        lax.all_gather(w_merge.astype(jnp.bfloat16), ("pipe", "dp", "tensor"), axis=0, tiled=True),
        lax.all_gather(
            merge_gain.astype(jnp.bfloat16), ("pipe", "dp", "tensor"), axis=0, tiled=True
        ),
        lax.all_gather(
            merge_bias.astype(jnp.bfloat16), ("pipe", "dp", "tensor"), axis=0, tiled=True
        ),
        lax.all_gather(
            final_gain.astype(jnp.bfloat16), ("pipe", "dp", "tensor"), axis=0, tiled=True
        ),
        lax.all_gather(
            final_bias.astype(jnp.bfloat16), ("pipe", "dp", "tensor"), axis=0, tiled=True
        ),
    )
    merge_weight, merge_scale, merge_shift, final_scale, final_shift = merge_set
    merge_scale = merge_scale.astype(jnp.float32)
    merge_shift = merge_shift.astype(jnp.float32)
    final_scale = final_scale.astype(jnp.float32)
    final_shift = final_shift.astype(jnp.float32)
    raw_rows = raw_pages.reshape(owned * rows_here, raw_pages.shape[3]).astype(jnp.float32)
    raw_hat, raw_rstd = norm_stats(raw_rows)
    merged_in = (raw_hat * merge_scale + merge_shift).astype(jnp.bfloat16)
    merged = matmul(merged_in, merge_weight).astype(jnp.bfloat16).reshape(owned, rows_here, D)
    first_pages = lax.all_gather(merged, "pipe", axis=0, tiled=True)
    layer_set = (
        lax.all_gather(w_qkv[0].astype(jnp.bfloat16), "dp", axis=0, tiled=True),
        lax.all_gather(w_fc1[0].astype(jnp.bfloat16), "dp", axis=0, tiled=True),
        lax.all_gather(w_proj[0].astype(jnp.bfloat16), "dp", axis=1, tiled=True),
        lax.all_gather(w_fc2[0].astype(jnp.bfloat16), "dp", axis=1, tiled=True),
    )
    qkv_weight, fc1_local, proj_weight, fc2_local = layer_set
    hidden_local = fc1_local.shape[1]
    bias_start = lax.axis_index("tensor") * hidden_local
    fc1_used, fc2_used = (fc1_local, fc2_local)
    hidden_bias = lax.dynamic_slice_in_dim(fc1_bias[0], bias_start, hidden_local)
    query_bias = qv_bias[0, 0]
    value_bias = qv_bias[0, 1]
    table_here = rel_table[0]
    lookup = rel_index(WIN)
    mask_add = jnp.asarray(shift_mask(WIN * WIN_ROWS, WIN * WIN_COLS, WIN, SHIFT)) * mask_weight

    def expand(table_in):
        picked = jnp.take(table_in, lookup, axis=0)
        return picked.reshape(WIN * WIN, WIN * WIN, table_in.shape[1]).transpose(2, 0, 1)

    pos_bias = expand(table_here)

    def through_proj(piece_rows):
        return matmul(piece_rows, proj_weight)

    def through_qkv(piece_rows):
        return jnp.einsum("tce,dce->td", piece_rows, qkv_weight, preferred_element_type=jnp.float32)

    def through_fc2(piece_rows):
        return matmul(piece_rows, fc2_used)

    def through_fc1(piece_rows):
        return matmul_nt(piece_rows, fc1_used)

    def attend(stream):
        hat_attn, rstd_attn = norm_stats(stream)
        ready_attn = (hat_attn * ln_gain[0, 0] + ln_bias[0, 0]).astype(jnp.bfloat16)
        full_attn = spread_rows(ready_attn)
        moved = roll_grid(full_attn, -amount)
        qkv_out = jnp.einsum("td,dce->tce", moved, qkv_weight, preferred_element_type=jnp.float32)
        query_win = split_heads((qkv_out[:, 0] + query_bias).astype(jnp.bfloat16))
        key_win = split_heads(qkv_out[:, 1].astype(jnp.bfloat16))
        value_win = split_heads((qkv_out[:, 2] + value_bias).astype(jnp.bfloat16))
        scores = jnp.einsum(
            "nqhd,nkhd->nhqk", query_win, key_win, preferred_element_type=jnp.float32
        )
        scores = scores * scale_factor + pos_bias[None] + mask_add[:, None]
        weights_soft = jax.nn.softmax(scores, axis=-1)
        weights_low = weights_soft.astype(jnp.bfloat16)
        mixed = jnp.einsum(
            "nhqk,nkhd->nqhd", weights_low, value_win, preferred_element_type=jnp.float32
        ).astype(jnp.bfloat16)
        mixed_flat = roll_grid(join_heads(mixed), amount)
        branch = collect_rows(mixed_flat, through_proj)
        after_attn = stream + branch + out_bias[0, 0]
        return (
            after_attn,
            (
                hat_attn,
                rstd_attn,
                full_attn,
                query_win,
                key_win,
                value_win,
                weights_soft,
                weights_low,
                mixed_flat,
            ),
        )

    def feed(after_attn):
        hat_mlp, rstd_mlp = norm_stats(after_attn)
        ready_mlp = (hat_mlp * ln_gain[0, 1] + ln_bias[0, 1]).astype(jnp.bfloat16)
        source_rows = spread_rows(ready_mlp)
        hidden_pre = matmul(source_rows, fc1_used) + hidden_bias
        hidden_act = gelu_exact(hidden_pre).astype(jnp.bfloat16)
        branch = collect_rows(hidden_act, through_fc2)
        after_mlp = after_attn + branch + out_bias[0, 1]
        return (after_mlp, (hat_mlp, rstd_mlp, source_rows, hidden_pre, hidden_act))

    def finish(after_mlp):
        hat_final, rstd_final = norm_stats(after_mlp)
        return (hat_final * final_scale + final_shift, hat_final, rstd_final)

    def feed_back(grad_after, saved):
        hat_mlp, rstd_mlp, source_rows, hidden_pre, hidden_act = saved
        grad_rows = spread_rows(grad_after.astype(jnp.bfloat16))
        g_fc2 = matmul_tn(hidden_act, grad_rows)
        grad_act = matmul_nt(grad_rows, fc2_used)
        gelu_out, gelu_pull = jax.vjp(gelu_exact, hidden_pre)
        grad_pre = gelu_pull(grad_act)[0].astype(jnp.bfloat16)
        g_hidden_bias = jnp.sum(grad_pre.astype(jnp.float32), 0)
        g_fc1 = matmul_tn(source_rows, grad_pre)
        grad_ready = collect_rows(grad_pre, through_fc1)
        g_gain_mlp = jnp.sum(grad_ready * hat_mlp, 0)
        g_shift_mlp = jnp.sum(grad_ready, 0)
        grad_before = grad_after + norm_back(hat_mlp, rstd_mlp, grad_ready * ln_gain[0, 1])
        return (
            grad_before,
            (g_fc1, g_fc2, g_hidden_bias, g_gain_mlp, g_shift_mlp, jnp.sum(grad_after, 0)),
        )

    def attend_back(grad_after, saved):
        (
            hat_attn,
            rstd_attn,
            full_attn,
            query_win,
            key_win,
            value_win,
            weights_soft,
            weights_low,
            mixed_flat,
        ) = saved
        grad_rows = spread_rows(grad_after.astype(jnp.bfloat16))
        g_proj = matmul_tn(mixed_flat, grad_rows)
        grad_mixed = matmul_nt(grad_rows, proj_weight).astype(jnp.bfloat16)
        grad_mixed = split_heads(roll_grid(grad_mixed, -amount))
        grad_values = jnp.einsum(
            "nhqk,nqhd->nkhd", weights_low, grad_mixed, preferred_element_type=jnp.float32
        )
        grad_soft = jnp.einsum(
            "nqhd,nkhd->nhqk", grad_mixed, value_win, preferred_element_type=jnp.float32
        )
        grad_scores = weights_soft * (
            grad_soft - jnp.sum(grad_soft * weights_soft, -1, keepdims=True)
        )
        grad_scores = grad_scores.astype(jnp.bfloat16)
        table_out, table_pull = jax.vjp(expand, table_here)
        g_table = table_pull(jnp.sum(grad_scores.astype(jnp.float32), 0))[0]
        grad_query = (
            jnp.einsum("nhqk,nkhd->nqhd", grad_scores, key_win, preferred_element_type=jnp.float32)
            * scale_factor
        )
        grad_keys = (
            jnp.einsum(
                "nhqk,nqhd->nkhd", grad_scores, query_win, preferred_element_type=jnp.float32
            )
            * scale_factor
        )
        query_flat = join_heads(grad_query).astype(jnp.bfloat16)
        key_flat = join_heads(grad_keys).astype(jnp.bfloat16)
        value_flat = join_heads(grad_values).astype(jnp.bfloat16)
        g_query_bias = jnp.sum(query_flat.astype(jnp.float32), 0)
        g_value_bias = jnp.sum(value_flat.astype(jnp.float32), 0)
        local_width = query_flat.shape[1]
        grad_qkv = jnp.stack((query_flat, key_flat, value_flat), 1).reshape(
            query_flat.shape[0], 3 * local_width
        )
        grad_qkv = roll_grid(grad_qkv, amount).reshape(query_flat.shape[0], 3, local_width)
        g_qkv = jnp.einsum("td,tce->dce", full_attn, grad_qkv, preferred_element_type=jnp.float32)
        grad_ready = collect_rows(grad_qkv, through_qkv)
        g_gain_attn = jnp.sum(grad_ready * hat_attn, 0)
        g_shift_attn = jnp.sum(grad_ready, 0)
        grad_before = grad_after + norm_back(hat_attn, rstd_attn, grad_ready * ln_gain[0, 0])
        return (
            grad_before,
            (
                g_qkv,
                g_proj,
                g_query_bias,
                g_value_bias,
                g_table,
                g_gain_attn,
                g_shift_attn,
                jnp.sum(grad_after, 0),
            ),
        )

    def forward_tick(tick_now, state_in):
        incoming, kept, shown = state_in
        slot_now = tick_now - section_now
        is_valid = (slot_now >= 0) & (slot_now < micro_count)
        slot_index = jnp.clip(slot_now, 0, micro_count - 1)
        start_rows = lax.dynamic_index_in_dim(first_pages, slot_index, 0, keepdims=False)
        section_in = jnp.where(is_first, start_rows, incoming)
        after_attn, unused_attn = attend(section_in.astype(jnp.float32))
        after_mlp, unused_mlp = feed(after_attn)
        final_out, hat_final, rstd_final = finish(after_mlp)
        shown_val = jnp.where(is_last, final_out, after_mlp).astype(jnp.bfloat16)
        kept = jnp.where(
            is_valid, lax.dynamic_update_index_in_dim(kept, section_in, slot_index, 0), kept
        )
        shown = jnp.where(
            is_valid, lax.dynamic_update_index_in_dim(shown, shown_val, slot_index, 0), shown
        )
        outgoing = shifted(after_mlp.astype(jnp.bfloat16), "pipe", 1)
        return (outgoing, kept, shown)

    tick_count = micro_count + section_count - 1
    empty_rows = jnp.zeros((rows_here, D), jnp.bfloat16)
    empty_pages = jnp.zeros((micro_count, rows_here, D), jnp.bfloat16)
    state_out = lax.fori_loop(0, tick_count, forward_tick, (empty_rows, empty_pages, empty_pages))
    kept_inputs = state_out[1]
    shown_all = state_out[2]
    cot_pages = cotangent[0, :, 0]
    zero_width = jnp.zeros((D,), jnp.float32)
    sums_init = (
        jnp.zeros(qkv_weight.shape, jnp.float32),
        jnp.zeros(proj_weight.shape, jnp.float32),
        jnp.zeros(fc1_used.shape, jnp.float32),
        jnp.zeros(fc2_used.shape, jnp.float32),
        jnp.zeros(query_bias.shape, jnp.float32),
        jnp.zeros(value_bias.shape, jnp.float32),
        jnp.zeros(table_here.shape, jnp.float32),
        jnp.zeros((fc1_used.shape[1],), jnp.float32),
        zero_width,
        zero_width,
        zero_width,
        zero_width,
        zero_width,
        zero_width,
        zero_width,
        zero_width,
    )

    def backward_tick(tick_now, state_in):
        incoming, firsts, grad_sums = state_in
        slot_now = tick_now - (section_count - 1 - section_now)
        is_valid = (slot_now >= 0) & (slot_now < micro_count)
        slot_index = jnp.clip(slot_now, 0, micro_count - 1)
        valid_weight = is_valid.astype(jnp.float32)
        last_weight = valid_weight * is_last.astype(jnp.float32)
        section_in = lax.dynamic_index_in_dim(kept_inputs, slot_index, 0, keepdims=False).astype(
            jnp.float32
        )
        cot_here = lax.dynamic_index_in_dim(cot_pages, slot_index, 0, keepdims=False).astype(
            jnp.float32
        )
        after_attn, saved_attn = attend(section_in)
        after_mlp, saved_mlp = feed(after_attn)
        final_out, hat_final, rstd_final = finish(after_mlp)
        grad_final = norm_back(hat_final, rstd_final, cot_here * final_scale)
        grad_after = jnp.where(is_last, grad_final, cot_here + incoming.astype(jnp.float32))
        grad_mid, mlp_grads = feed_back(grad_after, saved_mlp)
        grad_in, attn_grads = attend_back(grad_mid, saved_attn)
        g_fc1, g_fc2, g_hidden_bias, g_gain_mlp, g_shift_mlp, g_out_mlp = mlp_grads
        (
            g_qkv,
            g_proj,
            g_query_bias,
            g_value_bias,
            g_table,
            g_gain_attn,
            g_shift_attn,
            g_out_attn,
        ) = attn_grads
        new_terms = (
            g_qkv,
            g_proj,
            g_fc1,
            g_fc2,
            g_query_bias,
            g_value_bias,
            g_table,
            g_hidden_bias,
            g_gain_attn,
            g_shift_attn,
            g_gain_mlp,
            g_shift_mlp,
            g_out_attn,
            g_out_mlp,
        )
        grad_sums_head = jax.tree.map(
            lambda total, term_now: total + term_now * valid_weight, grad_sums[:14], new_terms
        )
        final_terms = (
            grad_sums[14] + jnp.sum(cot_here * hat_final, 0) * last_weight,
            grad_sums[15] + jnp.sum(cot_here, 0) * last_weight,
        )
        grad_sums = tuple(grad_sums_head) + final_terms
        first_ok = is_valid & is_first
        firsts = jnp.where(
            first_ok, lax.dynamic_update_index_in_dim(firsts, grad_in, slot_index, 0), firsts
        )
        outgoing = shifted(grad_in.astype(jnp.bfloat16), "pipe", -1)
        return (outgoing, firsts, grad_sums)

    firsts_init = jnp.zeros((micro_count, rows_here, D), jnp.float32)
    back_out = lax.fori_loop(0, tick_count, backward_tick, (empty_rows, firsts_init, sums_init))
    firsts_all = back_out[1]
    (
        g_qkv,
        g_proj,
        g_fc1,
        g_fc2,
        g_query_bias,
        g_value_bias,
        g_table,
        g_hidden_bias,
        g_gain_attn,
        g_shift_attn,
        g_gain_mlp,
        g_shift_mlp,
        g_out_attn,
        g_out_mlp,
        g_final_scale,
        g_final_shift,
    ) = back_out[2]
    g_fc1_local, g_fc2_local = (g_fc1, g_fc2)
    full_bias_grad = lax.dynamic_update_slice_in_dim(
        jnp.zeros((FF,), jnp.float32), g_hidden_bias, bias_start, 0
    )
    layer_out = (
        lax.psum_scatter(g_qkv.astype(jnp.bfloat16), "dp", scatter_dimension=0, tiled=True).astype(
            jnp.float32
        ),
        lax.psum_scatter(
            g_fc1_local.astype(jnp.bfloat16), "dp", scatter_dimension=0, tiled=True
        ).astype(jnp.float32),
        lax.psum_scatter(g_proj.astype(jnp.bfloat16), "dp", scatter_dimension=1, tiled=True).astype(
            jnp.float32
        ),
        lax.psum_scatter(
            g_fc2_local.astype(jnp.bfloat16), "dp", scatter_dimension=1, tiled=True
        ).astype(jnp.float32),
    )
    head_out = lax.psum((jnp.stack((g_query_bias, g_value_bias))[None], g_table[None]), "dp")
    feature_out = lax.psum(
        (
            jnp.stack((g_gain_attn, g_gain_mlp))[None],
            jnp.stack((g_shift_attn, g_shift_mlp))[None],
            jnp.stack((g_out_attn, g_out_mlp))[None],
            full_bias_grad[None],
        ),
        ("dp", "tensor"),
    )
    own_grads = lax.psum_scatter(
        firsts_all.astype(jnp.bfloat16), "pipe", scatter_dimension=0, tiled=True
    )
    grad_merged = own_grads.reshape(owned * rows_here, D)
    g_merge = matmul_tn(merged_in, grad_merged)
    grad_unit = matmul_nt(grad_merged, merge_weight)
    g_merge_scale = jnp.sum(grad_unit * raw_hat, 0)
    g_merge_shift = jnp.sum(grad_unit, 0)
    grad_raw = (
        norm_back(raw_hat, raw_rstd, grad_unit * merge_scale)
        .reshape(raw_pages.shape)
        .astype(jnp.bfloat16)
    )
    merge_out = (
        lax.psum_scatter(g_merge, ("pipe", "dp", "tensor"), scatter_dimension=0, tiled=True),
        lax.psum_scatter(g_merge_scale, ("pipe", "dp", "tensor"), scatter_dimension=0, tiled=True),
        lax.psum_scatter(g_merge_shift, ("pipe", "dp", "tensor"), scatter_dimension=0, tiled=True),
        lax.psum_scatter(g_final_scale, ("pipe", "dp", "tensor"), scatter_dimension=0, tiled=True),
        lax.psum_scatter(g_final_shift, ("pipe", "dp", "tensor"), scatter_dimension=0, tiled=True),
    )
    return (
        shown_all[None, :, None],
        grad_raw,
        merge_out[0],
        merge_out[1],
        merge_out[2],
        merge_out[3],
        merge_out[4],
        layer_out[0][None],
        layer_out[2][None],
        layer_out[1][None],
        layer_out[3][None],
        head_out[0],
        feature_out[3],
        head_out[1],
        feature_out[0],
        feature_out[1],
        feature_out[2],
    )


def solution(mesh):
    return jax.shard_map(
        on_device,
        mesh=mesh,
        in_specs=(
            P("pipe", "dp", "tensor", None),
            P(("pipe", "dp", "tensor"), None),
            P(("pipe", "dp", "tensor")),
            P(("pipe", "dp", "tensor")),
            P(("pipe", "dp", "tensor")),
            P(("pipe", "dp", "tensor")),
            P("pipe", "dp", None, "tensor"),
            P("pipe", "tensor", "dp"),
            P("pipe", "dp", "tensor"),
            P("pipe", "tensor", "dp"),
            P("pipe", None, "tensor"),
            P("pipe", None),
            P("pipe", None, "tensor"),
            P("pipe", None, None),
            P("pipe", None, None),
            P("pipe", None, None),
            P("pipe", None, "dp", "tensor", None),
        ),
        out_specs=(
            P("pipe", None, "dp", "tensor", None),
            P("pipe", "dp", "tensor", None),
            P(("pipe", "dp", "tensor"), None),
            P(("pipe", "dp", "tensor")),
            P(("pipe", "dp", "tensor")),
            P(("pipe", "dp", "tensor")),
            P(("pipe", "dp", "tensor")),
            P("pipe", "dp", None, "tensor"),
            P("pipe", "tensor", "dp"),
            P("pipe", "dp", "tensor"),
            P("pipe", "tensor", "dp"),
            P("pipe", None, "tensor"),
            P("pipe", None),
            P("pipe", None, "tensor"),
            P("pipe", None, None),
            P("pipe", None, None),
            P("pipe", None, None),
        ),
        check_vma=False,
    )
```

profile of v0, /device:TPU:9, one launch (start us, length us, event | category | flops | bytes accessed | tf_op | source)
XLA Modules:
  0.0 7733.6 jit_solution(2000827746240504879)
XLA Ops:
  159.6 2256.0 %while.71 = (s32[]{:T(128)}, bf16[300,1024]{1,0:T(8,128)(2,1)}, bf16[4,300,1024]{2,1,0:T(8,128)(2,1)}, bf16[4,300,1024]{2,1,0:T(8,128)(2,1)}, pred[]{:T(512)}, /...) while((s32[]{:T(128)}, bf16[300,1024]{1,0:T(8,128)(2,1)}, ...), condition=%wide.region_13.18_spmd.clone, body=%wide.region_2.17_spmd.clone.sunk | while | flops 7798502400 | bytes 150908448 | solution.py:365
  356.3 52.6 all-gather.54.cloned.1.call-done
  675.8 52.6 all-gather.54.cloned.1.call-done
  995.3 52.6 all-gather.54.cloned.1.call-done
  1314.7 52.6 all-gather.54.cloned.1.call-done
  1634.2 52.6 all-gather.54.cloned.1.call-done
  1953.7 52.6 all-gather.54.cloned.1.call-done
  2273.1 52.6 all-gather.54.cloned.1.call-done
  2418.4 5026.3 %while.72 = (s32[]{:T(128)}, bf16[300,1024]{1,0:T(8,128)(2,1)}, bf16[4,300,1024]{2,1,0:T(8,128)(2,1)}, f32[1024,3,256]{2,0,1:T(8,128)}, f32[256,1024]{1,0:T(8,12...) while((s32[]{:T(128)}, bf16[300,1024]{1,0:T(8,128)(2,1)}, ...), condition=%wide.region_47.52_spmd.clone.clone, body=%wide.region_14.51_spmd.sunk.clone.clone.sunk | while | flops 23212531712 | bytes 535109024 | solution.py:452
  2600.7 52.6 all-gather.58.cloned.1.call-done
  3065.6 55.4 scatter_custom_fusion.6
  3315.3 52.6 all-gather.58.cloned.1.call-done
  3781.1 55.4 scatter_custom_fusion.6
  4030.8 52.6 all-gather.58.cloned.1.call-done
  4496.7 55.4 scatter_custom_fusion.6
  4746.3 52.6 all-gather.58.cloned.1.call-done
  5212.2 55.4 scatter_custom_fusion.6
  5461.8 52.6 all-gather.58.cloned.1.call-done
  5927.7 55.4 scatter_custom_fusion.6
  6177.4 52.6 all-gather.58.cloned.1.call-done
  6643.2 55.4 scatter_custom_fusion.6
  6892.9 52.6 all-gather.58.cloned.1.call-done
  7358.7 55.4 scatter_custom_fusion.6
  7597.9 128.6 %reduce-scatter.21.cloned.1.call-done = f32[64,1024]{1,0:T(8,128)} async-done(((f32[2048,1024]{1,0:T(8,128)}), f32[64,1024]{1,0:T(8,128)}) %reduce-scatter.21.cloned.1.call-update) | async-done | bytes 262160 | tf_op jit(solution)/shard_map/reduce_scatter | solution.py:514
  (2616 shorter events, 6402.7 us)
Async XLA Ops:
  187.1 221.8 %all-gather.54.cloned.1.call-start = ((), (), s32[]{:S(2)}) async-start(), calls=%async_computation.18 | async-start | bytes 3112960 | tf_op jit(solution)/shard_map/while/body/eval_jaxpr/all_gather | solution.py:109
  503.0 225.4 %all-gather.54.cloned.1.call-start = ((), (), s32[]{:S(2)}) async-start(), calls=%async_computation.18 | async-start | bytes 3112960 | tf_op jit(solution)/shard_map/while/body/eval_jaxpr/all_gather | solution.py:109
  822.5 225.4 %all-gather.54.cloned.1.call-start = ((), (), s32[]{:S(2)}) async-start(), calls=%async_computation.18 | async-start | bytes 3112960 | tf_op jit(solution)/shard_map/while/body/eval_jaxpr/all_gather | solution.py:109
  1142.0 225.4 %all-gather.54.cloned.1.call-start = ((), (), s32[]{:S(2)}) async-start(), calls=%async_computation.18 | async-start | bytes 3112960 | tf_op jit(solution)/shard_map/while/body/eval_jaxpr/all_gather | solution.py:109
  1461.4 225.4 %all-gather.54.cloned.1.call-start = ((), (), s32[]{:S(2)}) async-start(), calls=%async_computation.18 | async-start | bytes 3112960 | tf_op jit(solution)/shard_map/while/body/eval_jaxpr/all_gather | solution.py:109
  1780.9 225.4 %all-gather.54.cloned.1.call-start = ((), (), s32[]{:S(2)}) async-start(), calls=%async_computation.18 | async-start | bytes 3112960 | tf_op jit(solution)/shard_map/while/body/eval_jaxpr/all_gather | solution.py:109
  2100.3 225.4 %all-gather.54.cloned.1.call-start = ((), (), s32[]{:S(2)}) async-start(), calls=%async_computation.18 | async-start | bytes 3112960 | tf_op jit(solution)/shard_map/while/body/eval_jaxpr/all_gather | solution.py:109
  2433.1 220.1 %all-gather.58.cloned.1.call-start = ((), (), s32[]{:S(2)}) async-start(), calls=%async_computation.20 | async-start | bytes 3112960 | tf_op jit(solution)/shard_map/while/body/eval_jaxpr/all_gather | solution.py:109
  2600.7 187.5 %all-gather.60.cloned.1.call-start = ((), (), s32[]{:S(2)}) async-start(), calls=%async_computation.21 | async-start | bytes 3112960 | tf_op jit(solution)/shard_map/while/body/eval_jaxpr/all_gather | solution.py:109
  2735.6 184.1 %all-gather.62.cloned.1.call-start = ((), (), s32[]{:S(2)}) async-start(), calls=%async_computation.22 | async-start | bytes 3112960 | tf_op jit(solution)/shard_map/while/body/eval_jaxpr/all_gather | solution.py:109
  3149.5 218.3 %all-gather.58.cloned.1.call-start = ((), (), s32[]{:S(2)}) async-start(), calls=%async_computation.20 | async-start | bytes 3112960 | tf_op jit(solution)/shard_map/while/body/eval_jaxpr/all_gather | solution.py:109
  3315.2 187.5 %all-gather.60.cloned.1.call-start = ((), (), s32[]{:S(2)}) async-start(), calls=%async_computation.21 | async-start | bytes 3112960 | tf_op jit(solution)/shard_map/while/body/eval_jaxpr/all_gather | solution.py:109
  3865.0 218.4 %all-gather.58.cloned.1.call-start = ((), (), s32[]{:S(2)}) async-start(), calls=%async_computation.20 | async-start | bytes 3112960 | tf_op jit(solution)/shard_map/while/body/eval_jaxpr/all_gather | solution.py:109
  4030.8 187.5 %all-gather.60.cloned.1.call-start = ((), (), s32[]{:S(2)}) async-start(), calls=%async_computation.21 | async-start | bytes 3112960 | tf_op jit(solution)/shard_map/while/body/eval_jaxpr/all_gather | solution.py:109
  4580.5 218.4 %all-gather.58.cloned.1.call-start = ((), (), s32[]{:S(2)}) async-start(), calls=%async_computation.20 | async-start | bytes 3112960 | tf_op jit(solution)/shard_map/while/body/eval_jaxpr/all_gather | solution.py:109
  4746.3 187.5 %all-gather.60.cloned.1.call-start = ((), (), s32[]{:S(2)}) async-start(), calls=%async_computation.21 | async-start | bytes 3112960 | tf_op jit(solution)/shard_map/while/body/eval_jaxpr/all_gather | solution.py:109
  5296.1 218.3 %all-gather.58.cloned.1.call-start = ((), (), s32[]{:S(2)}) async-start(), calls=%async_computation.20 | async-start | bytes 3112960 | tf_op jit(solution)/shard_map/while/body/eval_jaxpr/all_gather | solution.py:109
  5461.8 187.5 %all-gather.60.cloned.1.call-start = ((), (), s32[]{:S(2)}) async-start(), calls=%async_computation.21 | async-start | bytes 3112960 | tf_op jit(solution)/shard_map/while/body/eval_jaxpr/all_gather | solution.py:109
  5596.7 184.1 %all-gather.62.cloned.1.call-start = ((), (), s32[]{:S(2)}) async-start(), calls=%async_computation.22 | async-start | bytes 3112960 | tf_op jit(solution)/shard_map/while/body/eval_jaxpr/all_gather | solution.py:109
  6011.6 218.4 %all-gather.58.cloned.1.call-start = ((), (), s32[]{:S(2)}) async-start(), calls=%async_computation.20 | async-start | bytes 3112960 | tf_op jit(solution)/shard_map/while/body/eval_jaxpr/all_gather | solution.py:109
  6177.3 187.5 %all-gather.60.cloned.1.call-start = ((), (), s32[]{:S(2)}) async-start(), calls=%async_computation.21 | async-start | bytes 3112960 | tf_op jit(solution)/shard_map/while/body/eval_jaxpr/all_gather | solution.py:109
  6727.1 218.3 %all-gather.58.cloned.1.call-start = ((), (), s32[]{:S(2)}) async-start(), calls=%async_computation.20 | async-start | bytes 3112960 | tf_op jit(solution)/shard_map/while/body/eval_jaxpr/all_gather | solution.py:109
  6892.8 187.5 %all-gather.60.cloned.1.call-start = ((), (), s32[]{:S(2)}) async-start(), calls=%async_computation.21 | async-start | bytes 3112960 | tf_op jit(solution)/shard_map/while/body/eval_jaxpr/all_gather | solution.py:109
  7458.1 268.4 %reduce-scatter.21.cloned.1.call-start = ((), (), s32[]{:S(2)}) async-start(), calls=%async_computation.7 | async-start | bytes 8650752 | tf_op jit(solution)/shard_map/reduce_scatter | solution.py:514
  (537 other events, 12209.6 us)
Sparse Core Ops, SparseCore 0:
  11.6 63.6 all-gather.41
  356.4 52.4 all-gather.53
  503.1 54.4 all-gather.51
  822.6 54.4 all-gather.51
  995.4 52.4 all-gather.53
  1142.1 54.4 all-gather.51
  1314.9 52.4 all-gather.53
  1461.5 54.4 all-gather.51
  1781.0 54.4 all-gather.51
  2100.5 54.4 all-gather.51
  2433.2 54.2 all-gather.55
  2600.8 52.4 all-gather.57
  3149.6 52.4 all-gather.55
  3315.4 52.4 all-gather.57
  3865.2 52.4 all-gather.55
  4030.9 52.4 all-gather.57
  4580.7 52.4 all-gather.55
  4746.4 52.4 all-gather.57
  5296.2 52.4 all-gather.55
  5461.9 52.4 all-gather.57
  6011.7 52.4 all-gather.55
  6177.4 52.4 all-gather.57
  6892.9 52.4 all-gather.57
  7542.5 183.9 reduce-scatter.20
  (29 shorter events, 1197.4 us)
where the time goes:
time: 7760 us; the launch traced here: 7730 us
  waiting for transfers between devices  2490 us (32%)
  blocking collectives  2100 us (27%)
  local copies, waits for them, and re-layouts  1200 us (15%)
  matrix products  877 us (11%)
  other arithmetic  867 us (11%)
  starting transfers between devices  121 us (2%)
    all_gather x42, waiting for transfers between devices, spread_rows(): return lax.all_gather(local_rows, 'tensor', axis=0, tiled=True)  2060 us
    while x42, blocking collectives  1990 us
    scatter-add x7, other arithmetic, expand(): picked = jnp.take(table_in, lookup, axis=0)  388 us
    dot_general x36, matrix products, matmul(): return jnp.dot(left, right, preferred_element_type=jnp.float32)  312 us
    while x959, local copies, waits for them, and re-layouts  259 us
    reshape x77, local copies, waits for them, and re-layouts, split_heads(): grid_view.reshape(WIN_ROWS * WIN_COLS, WIN * WIN, channels // HEAD, HEAD)  225 us
  transfers between devices with their start and end apart: 109, of which 90 were waited for; matrix products, arithmetic and copies ran while one was open for 10% of the time, Pallas kernels for 0%

commit v1 on v0

v1 whole, which is shorter than its diff:
```python
import functools

import jax
import jax.numpy as jnp
import numpy as np
from jax import lax
from jax.experimental import pallas as pl
from jax.experimental.pallas import tpu as pltpu
from jax.sharding import PartitionSpec as P

D = 1024
HEAD = 32
FF = 4096
WIN = 10
SHIFT = 5
WIN_ROWS = 4
WIN_COLS = 3
NORM_EPS = 1e-05

GRID_W = WIN * WIN_COLS
UNIT = WIN * GRID_W
LINES = SHIFT * GRID_W
HALF = 160
PAD = 112
KEYS = 128
ROWS = WIN_COLS * PAD
PER = 128 // HEAD
GROUPS = D // 128
STACK = PER * PAD
OWN = 2
BLOCKS = 4
DB = D // OWN
TB = D // BLOCKS
FB = FF // BLOCKS
STEP = 16
SUMS = 16
VMEM_BYTES = 60 * 1024 * 1024

F32 = jnp.float32
BF16 = jnp.bfloat16


def rel_parts(window):
    offsets = np.arange(window)[:, None] - np.arange(window)[None, :] + window - 1
    return (offsets.reshape(-1)[None, :] == np.arange(2 * window - 1)[:, None]).astype(np.float32)


def shift_mask(grid_rows, grid_cols, window, shift_now):
    region = np.zeros((grid_rows, grid_cols), np.int64)
    region_id = 0
    for span_rows in (
        (0, grid_rows - window),
        (grid_rows - window, grid_rows - shift_now),
        (grid_rows - shift_now, grid_rows),
    ):
        for span_cols in (
            (0, grid_cols - window),
            (grid_cols - window, grid_cols - shift_now),
            (grid_cols - shift_now, grid_cols),
        ):
            region[span_rows[0] : span_rows[1], span_cols[0] : span_cols[1]] = region_id
            region_id += 1
    blocks = region.reshape(grid_rows // window, window, grid_cols // window, window).transpose(
        0, 2, 1, 3
    )
    blocks = blocks.reshape(-1, window * window)
    return np.where(blocks[:, :, None] == blocks[:, None, :], 0.0, -100.0).astype(np.float32)


def window_order(shift_now):
    order = np.zeros((ROWS, 2 * HALF), np.float32)
    for win in range(WIN_COLS):
        for row in range(WIN):
            for col in range(WIN):
                source_col = (win * WIN + col + shift_now) % GRID_W
                source = (row // SHIFT) * HALF + (row % SHIFT) * GRID_W + source_col
                order[win * PAD + row * WIN + col, source] = 1.0
    return order


def norm_stats(values):
    row_mean = jnp.mean(values, -1, keepdims=True)
    centred = values - row_mean
    rstd_rows = lax.rsqrt(jnp.mean(centred * centred, -1, keepdims=True) + NORM_EPS)
    return (centred * rstd_rows, rstd_rows)


def norm_back(normed, rstd_rows, grad_normed):
    return rstd_rows * (
        grad_normed
        - jnp.mean(grad_normed, -1, keepdims=True)
        - normed * jnp.mean(grad_normed * normed, -1, keepdims=True)
    )


def dot_nn(left, right):
    return lax.dot_general(left, right, (((1,), (0,)), ((), ())), preferred_element_type=F32)


def dot_nt(left, right):
    return lax.dot_general(left, right, (((1,), (1,)), ((), ())), preferred_element_type=F32)


def dot_tn(left, right):
    return lax.dot_general(left, right, (((0,), (0,)), ((), ())), preferred_element_type=F32)


def row_chunks(body, carry=None):
    def step(index, state):
        return body(pl.ds(pl.multiple_of(index * STEP, STEP), STEP), state)

    return lax.fori_loop(0, ROWS // STEP, step, carry)


def fold8(values):
    return jnp.sum(values.reshape(values.shape[0] // 8, 8, values.shape[1]), 0)


def head_masks():
    lane_head = lax.broadcasted_iota(jnp.int32, (1, 128), 1) // HEAD
    return [(lane_head == head).astype(F32) for head in range(PER)]


def spread_heads(tile, masks):
    return jnp.concatenate([(tile * mask.astype(BF16)) for mask in masks], 0)


def pick_heads(stacked, masks):
    total = stacked[:PAD] * masks[0]
    for head in range(1, PER):
        total = total + stacked[head * PAD : (head + 1) * PAD] * masks[head]
    return total


def group_columns(group):
    return (group // 2) * (3 * TB) + (group % 2) * 128


def lanes(start, size):
    return pl.ds(pl.multiple_of(start, 128), size)


def forward_kernel(
    flags,
    recv_a,
    recv_b,
    firsts,
    perm_in,
    perm_out,
    mask,
    vecs,
    bias_qkv,
    bias_fc1,
    bias_pos,
    w_qkv,
    w_proj,
    w_fc1,
    w_fc2,
    *refs,
):
    (x_all, qkv_all, probs_all, mixed_all, mid_all, rattn_all, rmlp_all, act_all, slope_all) = refs[11:20]
    out_all, hid_all = refs[20:22]
    send = refs[22]
    (
        v_qkv,
        v_proj,
        v_fc1,
        v_fc2,
        v_pos,
        rin,
        xf,
        xb,
        rattn,
        qkv,
        probs,
        mixed,
        mid,
        rmlp,
        act,
        slope,
        total,
        final,
        outb,
        outs,
        sem_w,
        sem_in,
        sem_out,
    ) = refs[23:]
    valid = flags[0]
    slot = flags[1]
    is_first = flags[2]
    is_last = flags[3]

    @pl.when(valid == 1)
    def _():
        def w_copy(kind, block):
            source, target = ((w_qkv, v_qkv), (w_fc1, v_fc1), (w_fc2, v_fc2))[kind]
            return pltpu.make_async_copy(
                source.at[:, block], target.at[:, block], sem_w.at[kind * BLOCKS + block]
            )

        def proj_copy():
            return pltpu.make_async_copy(w_proj, v_proj, sem_w.at[3 * BLOCKS])

        def pos_copy():
            return pltpu.make_async_copy(bias_pos, v_pos, sem_w.at[3 * BLOCKS + 1])

        @pl.when(is_first == 1)
        def _():
            pltpu.make_async_copy(
                firsts.at[slot, 0], rin.at[pl.ds(0, HALF)], sem_in.at[0]
            ).start()
            pltpu.make_async_copy(
                firsts.at[slot, 1], rin.at[pl.ds(HALF, HALF)], sem_in.at[1]
            ).start()

        @pl.when(is_first == 0)
        def _():
            pltpu.make_async_copy(recv_a, rin.at[pl.ds(0, HALF)], sem_in.at[0]).start()
            pltpu.make_async_copy(recv_b, rin.at[pl.ds(HALF, HALF)], sem_in.at[1]).start()

        for block in range(BLOCKS):
            w_copy(0, block).start()
        pos_copy().start()
        proj_copy().start()
        for block in range(BLOCKS):
            w_copy(1, block).start()
        for block in range(BLOCKS):
            w_copy(2, block).start()
        pltpu.make_async_copy(recv_a, rin.at[pl.ds(0, HALF)], sem_in.at[0]).wait()
        pltpu.make_async_copy(recv_b, rin.at[pl.ds(HALF, HALF)], sem_in.at[1]).wait()

        xf[...] = dot_nn(perm_in[...], rin[...])

        def first_norm(rows, state):
            values = xf[rows, :]
            hat, _ = norm_stats(values)
            rattn[rows, :] = (hat * vecs[0:1, :] + vecs[2:3, :]).astype(BF16)
            xb[rows, :] = values.astype(BF16)
            return state

        row_chunks(first_norm)
        saves = [
            pltpu.make_async_copy(rattn, rattn_all.at[slot], sem_out.at[0]),
            pltpu.make_async_copy(xb, x_all.at[slot], sem_out.at[1]),
        ]
        saves[0].start()
        saves[1].start()
        qkv[pl.ds(ROWS, 16), :] = jnp.zeros((16, 3 * D), BF16)

        def qkv_block(block, state):
            w_copy(0, block).wait()
            out = dot_nn(rattn[:, :DB], v_qkv[0, block])
            out = out + dot_nn(rattn[:, DB:], v_qkv[1, block])
            columns = lanes(block * 3 * TB, 3 * TB)
            qkv[pl.ds(0, ROWS), columns] = (out + bias_qkv[:, columns]).astype(BF16)
            return state

        lax.fori_loop(0, BLOCKS, qkv_block, None)
        save_qkv = pltpu.make_async_copy(
            qkv.at[pl.ds(0, ROWS)], qkv_all.at[slot], sem_out.at[2]
        )
        save_qkv.start()
        pos_copy().wait()
        masks = head_masks()

        def attend(win, group):
            base = pl.multiple_of(win * PAD, 16)
            column = group_columns(group)
            query = qkv[pl.ds(base, PAD), lanes(column, 128)]
            key = qkv[pl.ds(base, KEYS), lanes(column + TB, 128)]
            value = qkv[pl.ds(base, KEYS), lanes(column + 2 * TB, 128)]
            scores = dot_nt(spread_heads(query, masks), key)
            scores = scores * HEAD**-0.5 + v_pos[group]
            scores = scores + jnp.concatenate([mask[win]] * PER, 0)
            top = jnp.max(scores, -1, keepdims=True)
            powers = jnp.exp(scores - top)
            low = (powers / jnp.sum(powers, -1, keepdims=True)).astype(BF16)
            probs[win * GROUPS + group] = low
            mixed[pl.ds(base, PAD), lanes(group * 128, 128)] = pick_heads(
                dot_nn(low, value), masks
            ).astype(BF16)

        def attend_pair(index, state):
            win = index // (GROUPS // 2)
            pair = index % (GROUPS // 2)
            attend(win, pair * 2)
            attend(win, pair * 2 + 1)
            return state

        lax.fori_loop(0, WIN_COLS * GROUPS // 2, attend_pair, None)
        saves.append(pltpu.make_async_copy(probs, probs_all.at[slot], sem_out.at[3]))
        saves[-1].start()
        saves.append(pltpu.make_async_copy(mixed, mixed_all.at[slot], sem_out.at[4]))
        saves[-1].start()
        proj_copy().wait()
        for own in range(OWN):
            columns = slice(own * DB, (own + 1) * DB)
            out = xf[:, columns] + vecs[4:5, columns]
            for block in range(BLOCKS):
                out = out + dot_nn(mixed[:, block * TB : (block + 1) * TB], v_proj[own, block])
            mid[:, columns] = out
        saves.append(pltpu.make_async_copy(mid, mid_all.at[slot], sem_out.at[5]))
        saves[-1].start()

        def second_norm(rows, state):
            hat, _ = norm_stats(mid[rows, :])
            rmlp[rows, :] = (hat * vecs[1:2, :] + vecs[3:4, :]).astype(BF16)
            total[rows, :] = mid[rows, :] + vecs[5:6, :]
            return state

        row_chunks(second_norm)
        saves.append(pltpu.make_async_copy(rmlp, rmlp_all.at[slot], sem_out.at[6]))
        saves[-1].start()

        def hidden_block(block, state):
            w_copy(1, block).wait()
            columns = lanes(block * FB, FB)
            pre = dot_nn(rmlp[:, :DB], v_fc1[0, block]) + dot_nn(rmlp[:, DB:], v_fc1[1, block])
            pre = pre + bias_fc1[:, columns]
            chance = 0.5 + 0.5 * lax.erf(pre * np.float32(0.5**0.5))
            slope[:, columns] = (
                chance + pre * (np.float32((2 * np.pi) ** -0.5) * jnp.exp(-0.5 * pre * pre))
            ).astype(BF16)
            act[:, columns] = (pre * chance).astype(BF16)
            w_copy(2, block).wait()
            for own in range(OWN):
                half = slice(own * DB, (own + 1) * DB)
                total[:, half] += dot_nn(act[:, columns], v_fc2[own, block])
            return state

        lax.fori_loop(0, BLOCKS, hidden_block, None)
        saves.append(pltpu.make_async_copy(act, act_all.at[slot], sem_out.at[7]))
        saves[-1].start()
        saves.append(pltpu.make_async_copy(slope, slope_all.at[slot], sem_out.at[8]))
        saves[-1].start()

        def finish(rows, state):
            values = total[rows, :]
            hat, _ = norm_stats(values)
            shown = jnp.where(is_last == 1, hat * vecs[6:7, :] + vecs[7:8, :], values)
            outb[rows, :] = shown.astype(BF16)
            return state

        row_chunks(finish)
        saves.append(pltpu.make_async_copy(total, out_all.at[slot], sem_out.at[9]))
        saves[-1].start()
        outs[...] = dot_nn(perm_out[...], outb[...]).astype(BF16)
        for half in range(2):
            rows = pl.ds(half * HALF, HALF)
            saves.append(
                pltpu.make_async_copy(outs.at[rows], send.at[half], sem_out.at[10 + half])
            )
            saves[-1].start()
            saves.append(
                pltpu.make_async_copy(outs.at[rows], hid_all.at[slot, half], sem_out.at[12 + half])
            )
            saves[-1].start()
        save_qkv.wait()
        for save in saves:
            save.wait()


def backward_kernel(
    flags,
    recv_a,
    recv_b,
    cots,
    perm_in,
    perm_out,
    vecs,
    w_qkv,
    w_proj,
    w_fc1,
    w_fc2,
    probs_all,
    mid_all,
    out_all,
    *refs,
):
    x_all, qkv_all, slope_all, dbm_all, dx_all, sums_all, dpos_all = refs[7:14]
    send = refs[14]
    (
        v_qkv,
        v_proj,
        v_fc1,
        v_fc2,
        rin,
        rcot,
        xb,
        qkv,
        probs,
        mid,
        last,
        slope,
        grad,
        back,
        dbm,
        dba,
        dmix,
        dqkv,
        dpos,
        sums,
        outs,
        sem_w,
        sem_in,
        sem_out,
    ) = refs[15:]
    valid = flags[0]
    slot = flags[1]
    is_last = flags[3]

    @pl.when(valid == 1)
    def _():
        def w_copy(kind, block):
            source, target = ((w_fc2, v_fc2), (w_fc1, v_fc1), (w_qkv, v_qkv))[kind]
            return pltpu.make_async_copy(
                source.at[:, block], target.at[:, block], sem_w.at[kind * BLOCKS + block]
            )

        def proj_copy():
            return pltpu.make_async_copy(w_proj, v_proj, sem_w.at[3 * BLOCKS])

        def load(index):
            source, target = (
                (cots.at[slot, 0], rcot.at[pl.ds(0, HALF)]),
                (cots.at[slot, 1], rcot.at[pl.ds(HALF, HALF)]),
                (recv_a, rin.at[pl.ds(0, HALF)]),
                (recv_b, rin.at[pl.ds(HALF, HALF)]),
                (out_all.at[slot], last),
                (slope_all.at[slot], slope),
                (mid_all.at[slot], mid),
                (qkv_all.at[slot], qkv.at[pl.ds(0, ROWS)]),
                (probs_all.at[slot], probs),
                (x_all.at[slot], xb),
                (dpos_all, dpos),
            )[index]
            return pltpu.make_async_copy(source, target, sem_in.at[index])

        for index in range(5):
            load(index).start()
        w_copy(0, 0).start()
        load(5).start()
        w_copy(1, 0).start()
        for block in range(1, BLOCKS):
            w_copy(0, block).start()
            w_copy(1, block).start()
        load(6).start()
        proj_copy().start()
        load(7).start()
        load(8).start()
        for block in range(BLOCKS):
            w_copy(2, block).start()
        load(9).start()
        load(10).start()
        for index in range(5):
            load(index).wait()
        sums[...] = jnp.zeros_like(sums)
        grad[...] = dot_nn(perm_in[...], rcot[...])

        @pl.when(is_last == 1)
        def _():
            def final_norm(rows, state):
                cot = grad[rows, :]
                hat, rstd = norm_stats(last[rows, :])
                grad[rows, :] = norm_back(hat, rstd, cot * vecs[6:7, :])
                return (state[0] + fold8(cot * hat), state[1] + fold8(cot))

            zero = jnp.zeros((8, D), F32)
            gain, shift = row_chunks(final_norm, (zero, zero))
            sums[6:7, :] = jnp.sum(gain, 0, keepdims=True)
            sums[7:8, :] = jnp.sum(shift, 0, keepdims=True)

        @pl.when(is_last == 0)
        def _():
            grad[...] += dot_nn(perm_in[...], rin[...])

        def enter(rows, state):
            values = grad[rows, :]
            dbm[rows, :] = values.astype(BF16)
            back[rows, :] = jnp.zeros((STEP, D), F32)
            return state + fold8(values)

        out_sum = row_chunks(enter, jnp.zeros((8, D), F32))
        sums[5:6, :] = jnp.sum(out_sum, 0, keepdims=True)
        saves = [pltpu.make_async_copy(dbm, dbm_all.at[slot], sem_out.at[0])]
        saves[0].start()
        load(5).wait()

        def hidden_block(block, state):
            columns = lanes(block * FB, FB)
            w_copy(0, block).wait()
            dact = dot_nt(dbm[:, :DB], v_fc2[0, block]) + dot_nt(dbm[:, DB:], v_fc2[1, block])
            dpre = (dact * slope[:, columns].astype(F32)).astype(BF16)
            slope[:, columns] = dpre
            sums[pl.ds(8 + block, 1), :] = jnp.sum(dpre.astype(F32), 0, keepdims=True)
            w_copy(1, block).wait()
            for own in range(OWN):
                half = slice(own * DB, (own + 1) * DB)
                back[:, half] += dot_nt(slope[:, columns], v_fc1[own, block])
            return state

        lax.fori_loop(0, BLOCKS, hidden_block, None)
        saves.append(pltpu.make_async_copy(slope, slope_all.at[slot], sem_out.at[1]))
        saves[-1].start()
        load(6).wait()

        def mlp_norm(rows, state):
            hat, rstd = norm_stats(mid[rows, :])
            ready = back[rows, :]
            values = grad[rows, :] + norm_back(hat, rstd, ready * vecs[1:2, :])
            grad[rows, :] = values
            dba[rows, :] = values.astype(BF16)
            back[rows, :] = jnp.zeros((STEP, D), F32)
            return (state[0] + fold8(ready * hat), state[1] + fold8(ready), state[2] + fold8(values))

        zero = jnp.zeros((8, D), F32)
        gain, shift, out_sum = row_chunks(mlp_norm, (zero, zero, zero))
        sums[1:2, :] = jnp.sum(gain, 0, keepdims=True)
        sums[3:4, :] = jnp.sum(shift, 0, keepdims=True)
        sums[4:5, :] = jnp.sum(out_sum, 0, keepdims=True)
        load(9).wait()
        saves.append(pltpu.make_async_copy(dba, x_all.at[slot], sem_out.at[2]))
        saves[-1].start()
        proj_copy().wait()
        for block in range(BLOCKS):
            out = dot_nt(dba[:, :DB], v_proj[0, block]) + dot_nt(dba[:, DB:], v_proj[1, block])
            dmix[:, block * TB : (block + 1) * TB] = out.astype(BF16)
        load(7).wait()
        load(8).wait()
        load(10).wait()
        qkv[pl.ds(ROWS, 16), :] = jnp.zeros((16, 3 * D), BF16)
        masks = head_masks()

        def attend_back(group, state):
            column = group_columns(group)
            for win in range(WIN_COLS):
                base = win * PAD
                query = qkv[pl.ds(base, PAD), lanes(column, 128)]
                key = qkv[pl.ds(base, KEYS), lanes(column + TB, 128)]
                value = qkv[pl.ds(base, KEYS), lanes(column + 2 * TB, 128)]
                low = probs[win * GROUPS + group]
                dout = spread_heads(dmix[pl.ds(base, PAD), lanes(group * 128, 128)], masks)
                dprob = dot_nt(dout, value)
                weight = low.astype(F32)
                dscore = weight * (dprob - jnp.sum(dprob * weight, -1, keepdims=True))
                dscore = dscore.astype(BF16)
                dpos[group] += dscore.astype(F32)
                dquery = pick_heads(dot_nn(dscore, key), masks) * HEAD**-0.5
                dkey = dot_tn(dscore, spread_heads(query, masks)) * HEAD**-0.5
                dvalue = dot_tn(low, dout)
                dqkv[pl.ds(base, PAD), lanes(column, 128)] = dquery.astype(BF16)
                dqkv[pl.ds(base, PAD), lanes(column + TB, 128)] = dkey[:PAD].astype(BF16)
                dqkv[pl.ds(base, PAD), lanes(column + 2 * TB, 128)] = dvalue[:PAD].astype(BF16)
            return state

        lax.fori_loop(0, GROUPS, attend_back, None)
        saves.append(pltpu.make_async_copy(dqkv, qkv_all.at[slot], sem_out.at[3]))
        saves[-1].start()
        saves.append(pltpu.make_async_copy(dpos, dpos_all, sem_out.at[4]))
        saves[-1].start()

        def ready_block(block, state):
            columns = lanes(block * 3 * TB, 3 * TB)
            w_copy(2, block).wait()
            for own in range(OWN):
                half = slice(own * DB, (own + 1) * DB)
                back[:, half] += dot_nt(dqkv[:, columns], v_qkv[own, block])
            return state

        lax.fori_loop(0, BLOCKS, ready_block, None)
        for part in range(3):
            columns = slice(part * D, (part + 1) * D)
            sums[12 + part : 13 + part, :] = jnp.sum(dqkv[:, columns].astype(F32), 0, keepdims=True)

        def attn_norm(rows, state):
            hat, rstd = norm_stats(xb[rows, :].astype(F32))
            ready = back[rows, :]
            values = grad[rows, :] + norm_back(hat, rstd, ready * vecs[0:1, :])
            xb[rows, :] = values.astype(BF16)
            return (state[0] + fold8(ready * hat), state[1] + fold8(ready))

        gain, shift = row_chunks(attn_norm, (zero, zero))
        sums[0:1, :] = jnp.sum(gain, 0, keepdims=True)
        sums[2:3, :] = jnp.sum(shift, 0, keepdims=True)
        saves.append(pltpu.make_async_copy(sums, sums_all.at[slot], sem_out.at[5]))
        saves[-1].start()
        outs[...] = dot_nn(perm_out[...], xb[...]).astype(BF16)
        for half in range(2):
            rows = pl.ds(half * HALF, HALF)
            saves.append(
                pltpu.make_async_copy(outs.at[rows], send.at[half], sem_out.at[6 + half])
            )
            saves[-1].start()
            saves.append(
                pltpu.make_async_copy(outs.at[rows], dx_all.at[slot, half], sem_out.at[8 + half])
            )
            saves[-1].start()
        for save in saves:
            save.wait()


def any_specs(count):
    return [pl.BlockSpec(memory_space=pl.ANY)] * count


def vmem_specs(count):
    return [pl.BlockSpec(memory_space=pltpu.VMEM)] * count


def shapes_of(arrays):
    return [jax.ShapeDtypeStruct(array.shape, array.dtype) for array in arrays]


WEIGHT_SCRATCH = [
    pltpu.VMEM((OWN, BLOCKS, DB, 3 * TB), BF16),
    pltpu.VMEM((OWN, BLOCKS, TB, DB), BF16),
    pltpu.VMEM((OWN, BLOCKS, DB, FB), BF16),
    pltpu.VMEM((OWN, BLOCKS, FB, DB), BF16),
]


def layer_forward(flags, recv_a, recv_b, firsts, tables, weights, stacks):
    inputs = (flags, recv_a, recv_b, firsts) + tuple(tables) + tuple(weights) + tuple(stacks)
    first_stack = len(inputs) - len(stacks)
    wide = lambda dtype: pltpu.VMEM((ROWS, D), dtype)
    results = pl.pallas_call(
        forward_kernel,
        out_shape=shapes_of(stacks) + [jax.ShapeDtypeStruct((2, HALF, D), BF16)],
        in_specs=[pl.BlockSpec(memory_space=pltpu.SMEM)]
        + any_specs(3)
        + vmem_specs(6)
        + any_specs(5 + len(stacks)),
        out_specs=any_specs(len(stacks) + 1),
        scratch_shapes=WEIGHT_SCRATCH
        + [
            pltpu.VMEM((GROUPS, STACK, KEYS), F32),
            pltpu.VMEM((2 * HALF, D), BF16),
            wide(F32),
            wide(BF16),
            wide(BF16),
            pltpu.VMEM((ROWS + 16, 3 * D), BF16),
            pltpu.VMEM((WIN_COLS * GROUPS, STACK, KEYS), BF16),
            wide(BF16),
            wide(F32),
            wide(BF16),
            pltpu.VMEM((ROWS, FF), BF16),
            pltpu.VMEM((ROWS, FF), BF16),
            wide(F32),
            wide(F32),
            wide(BF16),
            pltpu.VMEM((2 * HALF, D), BF16),
            pltpu.SemaphoreType.DMA((3 * BLOCKS + 2,)),
            pltpu.SemaphoreType.DMA((2,)),
            pltpu.SemaphoreType.DMA((14,)),
        ],
        input_output_aliases={first_stack + index: index for index in range(len(stacks))},
        compiler_params=pltpu.CompilerParams(vmem_limit_bytes=VMEM_BYTES),
        cost_estimate=pl.CostEstimate(
            flops=24 * ROWS * D * D, bytes_accessed=40 * 1024 * 1024, transcendentals=ROWS * FF
        ),
        name="layer_forward",
    )(*inputs)
    return results[-1], tuple(results[:-1])


def layer_backward(flags, recv_a, recv_b, cots, tables, weights, saved, stacks):
    inputs = (
        (flags, recv_a, recv_b, cots) + tuple(tables) + tuple(weights) + tuple(saved) + tuple(stacks)
    )
    first_stack = len(inputs) - len(stacks)
    wide = lambda dtype: pltpu.VMEM((ROWS, D), dtype)
    results = pl.pallas_call(
        backward_kernel,
        out_shape=shapes_of(stacks) + [jax.ShapeDtypeStruct((2, HALF, D), BF16)],
        in_specs=[pl.BlockSpec(memory_space=pltpu.SMEM)]
        + any_specs(3)
        + vmem_specs(3)
        + any_specs(4 + len(saved) + len(stacks)),
        out_specs=any_specs(len(stacks) + 1),
        scratch_shapes=WEIGHT_SCRATCH
        + [
            pltpu.VMEM((2 * HALF, D), BF16),
            pltpu.VMEM((2 * HALF, D), BF16),
            wide(BF16),
            pltpu.VMEM((ROWS + 16, 3 * D), BF16),
            pltpu.VMEM((WIN_COLS * GROUPS, STACK, KEYS), BF16),
            wide(F32),
            wide(F32),
            pltpu.VMEM((ROWS, FF), BF16),
            wide(F32),
            wide(F32),
            wide(BF16),
            wide(BF16),
            wide(BF16),
            pltpu.VMEM((ROWS, 3 * D), BF16),
            pltpu.VMEM((GROUPS, STACK, KEYS), F32),
            pltpu.VMEM((SUMS, D), F32),
            pltpu.VMEM((2 * HALF, D), BF16),
            pltpu.SemaphoreType.DMA((3 * BLOCKS + 1,)),
            pltpu.SemaphoreType.DMA((11,)),
            pltpu.SemaphoreType.DMA((10,)),
        ],
        input_output_aliases={first_stack + index: index for index in range(len(stacks))},
        compiler_params=pltpu.CompilerParams(vmem_limit_bytes=VMEM_BYTES),
        cost_estimate=pl.CostEstimate(
            flops=24 * ROWS * D * D, bytes_accessed=50 * 1024 * 1024, transcendentals=0
        ),
        name="layer_backward",
    )(*inputs)
    return results[-1], tuple(results[:-1])


def on_device(
    raw_pages,
    w_merge,
    merge_gain,
    merge_bias,
    final_gain,
    final_bias,
    w_qkv,
    w_proj,
    w_fc1,
    w_fc2,
    qv_bias,
    fc1_bias,
    rel_table,
    ln_gain,
    ln_bias,
    out_bias,
    cotangent,
):
    section_now = lax.axis_index("pipe")
    section_count = lax.axis_size("pipe")
    dp_now = lax.axis_index("dp")
    dp_count = lax.axis_size("dp")
    tensor_now = lax.axis_index("tensor")
    tensor_count = lax.axis_size("tensor")
    copies = tensor_count // WIN_ROWS
    unit_now = tensor_now // copies
    all_axes = ("pipe", "dp", "tensor")
    group_axes = ("dp", "tensor")
    is_first = section_now == 0
    is_last = section_now == section_count - 1
    is_odd = section_now % 2 == 1
    owned, _, rows_here, merge_in = raw_pages.shape
    micro_count = cotangent.shape[1]
    own_width = D // dp_count

    def section_pairs(step, moves):
        pairs = []
        for section in range(section_count):
            if 0 <= section + step < section_count:
                for tensor in range(tensor_count):
                    target = (tensor + copies * moves[section % 2]) % tensor_count
                    pairs.append(
                        (section * tensor_count + tensor, (section + step) * tensor_count + target)
                    )
        return pairs

    def odd_pairs(move):
        return [
            (
                section * tensor_count + tensor,
                section * tensor_count + (tensor + copies * move) % tensor_count,
            )
            for section in range(1, section_count, 2)
            for tensor in range(tensor_count)
        ]

    def hop(halves, step):
        to_a = lax.ppermute(halves[1], ("pipe", "tensor"), section_pairs(step, (0, 1)))
        to_b = lax.ppermute(halves[0], ("pipe", "tensor"), section_pairs(step, (-1, 0)))
        return to_a, to_b

    def whole_unit(rows, axis):
        if copies == 1:
            return rows
        rows = lax.all_gather(rows, "tensor", axis=axis, tiled=True)
        return lax.dynamic_slice_in_dim(rows, unit_now * UNIT, UNIT, axis)

    def own_part(rows, axis):
        if copies == 1:
            return rows
        return lax.dynamic_slice_in_dim(
            rows, (tensor_now % copies) * rows_here, rows_here, axis
        )

    def gather_rows(values, axes):
        size = values.shape[0]
        tile = 8 * 128
        rows = jnp.pad(values, (0, -size % tile)).reshape(-1, 128)
        rows = lax.all_gather(rows, axes, axis=0, tiled=True)
        return rows.reshape(-1, size + -size % tile)[:, :size]

    def to_halves(rows):
        rows = rows.reshape(rows.shape[:-2] + (2, LINES, D))
        pads = [(0, 0)] * (rows.ndim - 2) + [(0, HALF - LINES), (0, 0)]
        return jnp.pad(rows, pads)

    def from_halves(halves):
        rows = halves[..., :LINES, :]
        return rows.reshape(rows.shape[:-3] + (UNIT, D))

    share = w_merge.shape[0]
    small = jnp.concatenate((merge_gain, merge_bias, final_gain, final_bias)).astype(BF16)
    merge_weight = lax.all_gather(w_merge.astype(BF16), all_axes, axis=0, tiled=True)
    small_all = lax.all_gather(small, all_axes, axis=0)
    fshare = final_gain.shape[0]
    merge_scale = small_all[:, :share].reshape(-1).astype(F32)
    merge_shift = small_all[:, share : 2 * share].reshape(-1).astype(F32)
    final_scale = small_all[:, 2 * share : 2 * share + fshare].reshape(-1).astype(F32)
    final_shift = small_all[:, 2 * share + fshare :].reshape(-1).astype(F32)

    def gather(weight):
        return lax.all_gather(weight.astype(BF16), group_axes, axis=0)

    split = (dp_count, tensor_count)
    qkv_weight = gather(w_qkv[0].reshape(own_width, -1))
    proj_weight = gather(w_proj[0])
    fc1_weight = gather(w_fc1[0])
    fc2_weight = gather(w_fc2[0])
    if split == (OWN, BLOCKS):
        qkv_weight = qkv_weight.reshape(OWN, BLOCKS, DB, 3 * TB)
        proj_weight = proj_weight.reshape(OWN, BLOCKS, TB, DB)
        fc1_weight = fc1_weight.reshape(OWN, BLOCKS, DB, FB)
        fc2_weight = fc2_weight.reshape(OWN, BLOCKS, FB, DB)
    else:
        qkv_weight = qkv_weight.reshape(split + (own_width, 3, -1)).transpose(0, 2, 3, 1, 4)
        qkv_weight = qkv_weight.reshape(OWN, DB, 3, BLOCKS, TB).transpose(0, 3, 1, 2, 4)
        qkv_weight = qkv_weight.reshape(OWN, BLOCKS, DB, 3 * TB)
        proj_weight = proj_weight.reshape(split + (-1, own_width)).transpose(1, 2, 0, 3)
        proj_weight = proj_weight.reshape(BLOCKS, TB, OWN, DB).transpose(2, 0, 1, 3)
        fc1_weight = fc1_weight.reshape(split + (own_width, -1)).transpose(0, 2, 1, 3)
        fc1_weight = fc1_weight.reshape(OWN, DB, BLOCKS, FB).transpose(0, 2, 1, 3)
        fc2_weight = fc2_weight.reshape(split + (-1, own_width)).transpose(1, 2, 0, 3)
        fc2_weight = fc2_weight.reshape(BLOCKS, FB, OWN, DB).transpose(2, 0, 1, 3)
    weights = (qkv_weight, proj_weight, fc1_weight, fc2_weight)

    heads_here = rel_table.shape[2]
    head_set = jnp.concatenate((qv_bias[0].reshape(-1), rel_table[0].reshape(-1)))
    head_set = gather_rows(head_set, "tensor")
    qv_all = head_set[:, : qv_bias.shape[1] * qv_bias.shape[2]].reshape(tensor_count, 2, -1)
    qv_all = qv_all.transpose(1, 0, 2).reshape(2, BLOCKS, TB)
    bias_qkv = jnp.stack((qv_all[0], jnp.zeros_like(qv_all[0]), qv_all[1]), 1).reshape(1, 3 * D)
    table_all = head_set[:, qv_bias.shape[1] * qv_bias.shape[2] :]
    table_all = table_all.reshape(tensor_count, 2 * WIN - 1, 2 * WIN - 1, heads_here)
    table_all = table_all.transpose(0, 3, 1, 2).reshape(D // HEAD, 2 * WIN - 1, 2 * WIN - 1)
    offsets = jnp.asarray(rel_parts(WIN))
    spread = jnp.einsum("huv,vy->huy", table_all, offsets, precision=lax.Precision.HIGHEST)
    spread = jnp.einsum("huy,ux->hxy", spread, offsets, precision=lax.Precision.HIGHEST)
    spread = spread.reshape(D // HEAD, WIN, WIN, WIN, WIN).transpose(0, 1, 3, 2, 4)
    spread = spread.reshape(D // HEAD, WIN * WIN, WIN * WIN)
    bias_pos = jnp.pad(spread, ((0, 0), (0, PAD - WIN * WIN), (0, 0)))
    bias_pos = jnp.pad(
        bias_pos, ((0, 0), (0, 0), (0, KEYS - WIN * WIN)), constant_values=-1e30
    ).reshape(GROUPS, STACK, KEYS)

    mask_all = np.zeros((WIN_ROWS, WIN_COLS, PAD, KEYS), np.float32)
    mask_all[:, :, : WIN * WIN, : WIN * WIN] = shift_mask(
        WIN * WIN_ROWS, GRID_W, WIN, SHIFT
    ).reshape(WIN_ROWS, WIN_COLS, WIN * WIN, WIN * WIN)
    mask_here = lax.dynamic_index_in_dim(jnp.asarray(mask_all, BF16), unit_now, 0, keepdims=False)
    mask_here = mask_here.astype(F32) * is_odd.astype(F32)
    orders = np.stack((window_order(0), window_order(SHIFT)))
    parity = section_now % 2
    perm_in = lax.dynamic_index_in_dim(jnp.asarray(orders, BF16), parity, 0, keepdims=False)
    perm_out = lax.dynamic_index_in_dim(
        jnp.asarray(orders.transpose(0, 2, 1), BF16), parity, 0, keepdims=False
    )
    vecs = jnp.concatenate(
        (ln_gain[0], ln_bias[0], out_bias[0], final_scale[None], final_shift[None])
    )
    forward_tables = (perm_in, perm_out, mask_here, vecs, bias_qkv, fc1_bias, bias_pos)
    backward_tables = (perm_in, perm_out, vecs)

    raw_rows = raw_pages.reshape(owned * rows_here, merge_in).astype(F32)
    raw_hat, raw_rstd = norm_stats(raw_rows)
    merged_in = (raw_hat * merge_scale + merge_shift).astype(BF16)
    merged = dot_nn(merged_in, merge_weight).astype(BF16).reshape(owned, rows_here, D)
    merged = to_halves(whole_unit(merged, 1))
    first_list = [merged]
    for section in range(1, section_count):
        first_list.append(lax.ppermute(merged, "pipe", [(section, 0)]))
    firsts = jnp.concatenate(first_list, 0)

    cots = to_halves(whole_unit(cotangent[0, :, 0], 1))
    cots_next = lax.ppermute(cots[:, 0], ("pipe", "tensor"), odd_pairs(-1))
    cots = jnp.where(is_odd, jnp.stack((cots[:, 1], cots_next), 1), cots)

    tick_count = micro_count + 2 * (section_count - 1)

    def flags_at(start, tick_now):
        slot_now = tick_now - 2 * start
        is_valid = (slot_now >= 0) & (slot_now < micro_count)
        slot = jnp.clip(slot_now, 0, micro_count - 1)
        return jnp.stack([flag.astype(jnp.int32) for flag in (is_valid, slot, is_first, is_last)])

    def stack_of(shape, dtype):
        return jnp.zeros((micro_count,) + shape, dtype)

    def forward_tick(tick_now, state):
        outgoing, recv_a, recv_b, stacks = state
        next_a, next_b = hop(outgoing, 1)
        outgoing, stacks = layer_forward(
            flags_at(section_now, tick_now), recv_a, recv_b, firsts, forward_tables, weights, stacks
        )
        return outgoing, next_a, next_b, stacks

    empty = jnp.zeros((2, HALF, D), BF16)
    stacks = (
        stack_of((ROWS, D), BF16),
        stack_of((ROWS, 3 * D), BF16),
        stack_of((WIN_COLS * GROUPS, STACK, KEYS), BF16),
        stack_of((ROWS, D), BF16),
        stack_of((ROWS, D), F32),
        stack_of((ROWS, D), BF16),
        stack_of((ROWS, D), BF16),
        stack_of((ROWS, FF), BF16),
        stack_of((ROWS, FF), BF16),
        stack_of((ROWS, D), F32),
        stack_of((2, HALF, D), BF16),
    )
    state = lax.fori_loop(0, tick_count, forward_tick, (empty, empty[0], empty[1], stacks))
    (
        x_all,
        qkv_all,
        probs_all,
        mixed_all,
        mid_all,
        rattn_all,
        rmlp_all,
        act_all,
        slope_all,
        out_all,
        hid_all,
    ) = state[3]
    hid_before = lax.ppermute(hid_all[:, 1], ("pipe", "tensor"), odd_pairs(1))
    shown = jnp.where(is_odd, jnp.stack((hid_before, hid_all[:, 0]), 1), hid_all)
    shown = own_part(from_halves(shown), 1)

    def backward_tick(tick_now, state):
        outgoing, recv_a, recv_b, stacks = state
        next_a, next_b = hop(outgoing, -1)
        outgoing, stacks = layer_backward(
            flags_at(section_count - 1 - section_now, tick_now),
            recv_a,
            recv_b,
            cots,
            backward_tables,
            weights,
            (probs_all, mid_all, out_all),
            stacks,
        )
        return outgoing, next_a, next_b, stacks

    stacks = (
        x_all,
        qkv_all,
        slope_all,
        stack_of((ROWS, D), BF16),
        stack_of((2, HALF, D), BF16),
        stack_of((SUMS, D), F32),
        jnp.zeros((GROUPS, STACK, KEYS), F32),
    )
    state = lax.fori_loop(0, tick_count, backward_tick, (empty, empty[0], empty[1], stacks))
    dba_all, dqkv_all, dpre_all, dbm_all, dx_all, sums_all, dpos = state[3]

    def weight_gradient(left, right):
        left = left.reshape(micro_count * ROWS, -1)
        right = right.reshape(micro_count * ROWS, D)

        def part(target):
            return dot_tn(
                left, lax.dynamic_slice_in_dim(right, target * own_width, own_width, 1)
            )

        total = None
        for step in range(1, dp_count):
            pairs = [(index, (index + step) % dp_count) for index in range(dp_count)]
            moved = lax.ppermute(
                part((dp_now + step) % dp_count).astype(BF16), "dp", pairs
            ).astype(F32)
            total = moved if total is None else total + moved
        mine = part(dp_now)
        total = mine if total is None else mine + total
        return total / copies

    def over_tensor(total):
        return lax.psum_scatter(total.astype(BF16), "tensor", scatter_dimension=0, tiled=True)

    g_fc2 = over_tensor(weight_gradient(act_all, dbm_all)).astype(F32)
    g_fc1 = over_tensor(weight_gradient(dpre_all, rmlp_all)).astype(F32).T
    g_qkv = weight_gradient(dqkv_all, rattn_all)
    if copies > 1:
        g_qkv = g_qkv.reshape(BLOCKS, 3, copies, TB // copies, own_width)
        g_qkv = g_qkv.transpose(0, 2, 1, 3, 4).reshape(3 * D, own_width)
    g_qkv = over_tensor(g_qkv).astype(F32).T.reshape(own_width, 3, D // tensor_count)
    g_proj = over_tensor(weight_gradient(mixed_all, dba_all)).astype(F32)

    sums = jnp.sum(sums_all, 0)
    dpos = dpos.reshape(D // HEAD, PAD, KEYS)[:, : WIN * WIN, : WIN * WIN]
    dpos = dpos.reshape(D // HEAD, WIN, WIN, WIN, WIN).transpose(0, 1, 3, 2, 4)
    dpos = dpos.reshape(D // HEAD, WIN * WIN, WIN * WIN)
    dtable = jnp.einsum("hxy,vy->hxv", dpos, offsets, precision=lax.Precision.HIGHEST)
    dtable = jnp.einsum("hxv,ux->huv", dtable, offsets, precision=lax.Precision.HIGHEST)
    local_sums = jnp.concatenate((sums[:15].reshape(-1), dtable.reshape(-1)))
    local_sums = jnp.sum(gather_rows(local_sums, group_axes), 0) / copies
    sums = local_sums[: 15 * D].reshape(15, D)
    dtable = local_sums[15 * D :].reshape(tensor_count, heads_here, -1)
    g_table = lax.dynamic_index_in_dim(dtable, tensor_now, 0, keepdims=False).T
    dqv = sums[12:15].reshape(BLOCKS, 3, TB)[:, 0::2].transpose(1, 0, 2).reshape(2, D)
    g_qv = lax.dynamic_slice_in_dim(
        dqv, tensor_now * (D // tensor_count), D // tensor_count, 1
    )

    own_grads = dx_all[:owned]
    for section in range(1, section_count):
        moved = lax.ppermute(
            dx_all[section * owned : (section + 1) * owned], "pipe", [(0, section)]
        )
        own_grads = jnp.where(section_now == section, moved, own_grads)
    grad_merged = own_part(from_halves(own_grads), 1).reshape(owned * rows_here, D)
    g_merge = dot_tn(merged_in, grad_merged).astype(BF16)
    grad_unit = dot_nt(grad_merged, merge_weight)
    merge_sums = jnp.stack((jnp.sum(grad_unit * raw_hat, 0), jnp.sum(grad_unit, 0)))
    grad_raw = norm_back(raw_hat, raw_rstd, grad_unit * merge_scale)
    grad_raw = grad_raw.reshape(raw_pages.shape).astype(BF16)
    for axis in all_axes:
        g_merge = lax.psum_scatter(g_merge, axis, scatter_dimension=0, tiled=True)
    final_sums = jnp.sum(sums_all, 0)[6:8] * is_last.astype(F32) / copies
    edge = jnp.concatenate((merge_sums.reshape(-1), final_sums.reshape(-1)))
    edge = jnp.sum(gather_rows(edge, all_axes), 0)
    place = (section_now * dp_count + dp_now) * tensor_count + tensor_now
    edge_parts = []
    start = 0
    for size, width in ((merge_in, share), (merge_in, share), (D, fshare), (D, fshare)):
        edge_parts.append(lax.dynamic_slice_in_dim(edge, start + place * width, width))
        start += size
    return (
        shown[None, :, None],
        grad_raw,
        g_merge.astype(F32),
        *edge_parts,
        g_qkv[None],
        g_proj[None],
        g_fc1[None],
        g_fc2[None],
        g_qv[None],
        sums[8:12].reshape(1, FF),
        g_table[None],
        sums[0:2][None],
        sums[2:4][None],
        sums[4:6][None],
    )


def solution(mesh):
    return jax.shard_map(
        on_device,
        mesh=mesh,
        in_specs=(
            P("pipe", "dp", "tensor", None),
            P(("pipe", "dp", "tensor"), None),
            P(("pipe", "dp", "tensor")),
            P(("pipe", "dp", "tensor")),
            P(("pipe", "dp", "tensor")),
            P(("pipe", "dp", "tensor")),
            P("pipe", "dp", None, "tensor"),
            P("pipe", "tensor", "dp"),
            P("pipe", "dp", "tensor"),
            P("pipe", "tensor", "dp"),
            P("pipe", None, "tensor"),
            P("pipe", None),
            P("pipe", None, "tensor"),
            P("pipe", None, None),
            P("pipe", None, None),
            P("pipe", None, None),
            P("pipe", None, "dp", "tensor", None),
        ),
        out_specs=(
            P("pipe", None, "dp", "tensor", None),
            P("pipe", "dp", "tensor", None),
            P(("pipe", "dp", "tensor"), None),
            P(("pipe", "dp", "tensor")),
            P(("pipe", "dp", "tensor")),
            P(("pipe", "dp", "tensor")),
            P(("pipe", "dp", "tensor")),
            P("pipe", "dp", None, "tensor"),
            P("pipe", "tensor", "dp"),
            P("pipe", "dp", "tensor"),
            P("pipe", "tensor", "dp"),
            P("pipe", None, "tensor"),
            P("pipe", None),
            P("pipe", None, "tensor"),
            P("pipe", None, None),
            P("pipe", None, None),
            P("pipe", None, None),
        ),
        check_vma=False,
    )
```

time: 7760 us -> 1810 us (0.23)
  waiting for transfers between devices: 2490 us -> 514 us
  blocking collectives: 2100 us -> 275 us
  local copies, waits for them, and re-layouts: 1200 us -> 258 us
  other arithmetic: 867 us -> 55.9 us
  matrix products: 877 us -> 102 us
  Pallas kernels: 0 us -> 368 us
    while x42 -> x0, blocking collectives: 1990 us -> none
    all_gather x47 -> x5, waiting for transfers between devices: 2120 us -> 171 us  [the longest x4 171 us: gather(): return lax.all_gather(weight.astype(BF16), group_axes, axis=0)]
    dot_general x157 -> x15, matrix products: 831 us -> 102 us  [the longest x9 82.7 us: dot_tn(): lax.dot_general(left, right, (((0,), (0,)), ((), ())), preferred_element_...]
    scatter-add x7 -> x0, other arithmetic: 388 us -> none  [expand(): picked = jnp.take(table_in, lookup, axis=0)]
    reshape x189 -> x15, local copies, waits for them, and re-layouts: 418 us -> 38.2 us  [the longest x2 11.9 us: on_device(): dpos = dpos.reshape(D // HEAD, WIN * WIN, WIN * WIN)]
    pallas_call x0 -> x20, Pallas kernels: none -> 368 us  [the longest x10 187 us: layer_forward(): pl.pallas_call(forward_kernel, out_shape=shapes_of(stacks) + [jax.ShapeDt...]
    convert_element_type x112 -> x5, local copies, waits for them, and re-layouts: 276 us -> 1.47 us  [the longest x1 1.17 us: gather(): return lax.all_gather(weight.astype(BF16), group_axes, axis=0)]
    all_gather x1 -> x4, blocking collectives: 2.3 us -> 275 us  [the longest x3 188 us: gather_rows(): rows = lax.all_gather(rows, axes, axis=0, tiled=True)]
  transfers between devices with their start and end apart: 109 -> 64, of which waited for: 90 -> 32; matrix products, arithmetic and copies ran while one was open for 10% -> 15% of each run, Pallas kernels for 0% -> 21%
where the time goes in v1:
time: 1810 us; the launch traced here: 1790 us
  waiting for transfers between devices  514 us (28%)
  Pallas kernels  368 us (20%)
  blocking collectives  275 us (15%)
  local copies, waits for them, and re-layouts  258 us (14%)
  starting transfers between devices  198 us (11%)
  matrix products  102 us (6%)
  other arithmetic  55.9 us (3%)
    ppermute x20, waiting for transfers between devices, hop(): lax.ppermute(halves[1], ('pipe', 'tensor'), section_pairs(step, (0, 1)))  201 us
    all_gather x3, blocking collectives, gather_rows(): rows = lax.all_gather(rows, axes, axis=0, tiled=True)  188 us
    pallas_call x10, Pallas kernels, layer_forward(): pl.pallas_call(forward_kernel, out_shape=shapes_of(stacks) + [jax.ShapeDt...  187 us
    pallas_call x10, Pallas kernels, layer_backward(): pl.pallas_call(backward_kernel, out_shape=shapes_of(stacks) + [jax.ShapeD...  181 us
    all_gather x4, waiting for transfers between devices, gather(): return lax.all_gather(weight.astype(BF16), group_axes, axis=0)  171 us
    ppermute x20, starting transfers between devices, hop(): lax.ppermute(halves[1], ('pipe', 'tensor'), section_pairs(step, (0, 1)))  94.3 us
    all_gather x1, blocking collectives, on_device(): small_all = lax.all_gather(small, all_axes, axis=0)  86.9 us
    ppermute x20, starting transfers between devices, hop(): lax.ppermute(halves[0], ('pipe', 'tensor'), section_pairs(step, (-1, 0)))  86 us
  transfers between devices with their start and end apart: 64, of which 32 were waited for; matrix products, arithmetic and copies ran while one was open for 15% of the time, Pallas kernels for 21%

profile of v1, /device:TPU:9, one launch (start us, length us, event | category | flops | bytes accessed | tf_op | source)
XLA Modules:
  0.0 1787.8 jit_solution(18439426867190283919)
XLA Ops:
  35.3 86.9 %all-gather = bf16[32,1,192]{2,1,0:T(2,128)(2,1)S(1)} all-gather(bf16[1,1,192]{2,1,0:T(2,128)(2,1)S(1)} %maximum_bitcast_fusion.2), channel_id=1, replica_groups=mesh['pipe'=4,'dp'=2,'tensor'=4] {'pipe','dp','tensor'}, dimensions={0}, use_global_device_ids=true | all-gather | bytes 12672 | tf_op jit(solution)/shard_map/all_gather | solution.py:808
  195.8 82.3 %all-gather.13.cloned.1.call-done = bf16[8,512,1024]{2,1,0:T(8,128)(2,1)} async-done(((bf16[1,512,1024]{2,1,0:T(8,128)(2,1)}), bf16[8,512,1024]{2,1,0:T(8,128)(2,1)}) %all-gather.13.cloned.1.call-update) | async-done | bytes 8388624 | tf_op jit(solution)/shard_map/all_gather | solution.py:816
  278.2 82.1 %all-gather.15.cloned.1.call-done = bf16[8,1024,512]{2,1,0:T(8,128)(2,1)} async-done(((bf16[1,1024,512]{2,1,0:T(8,128)(2,1)}), bf16[8,1024,512]{2,1,0:T(8,128)(2,1)}) %all-gather.15.cloned.1.call-update) | async-done | bytes 8388624 | tf_op jit(solution)/shard_map/all_gather | solution.py:816
  398.6 428.4 %while.74 = (s32[]{:T(128)}, bf16[2,160,1024]{2,1,0:T(8,128)(2,1)}, bf16[160,1024]{1,0:T(8,128)(2,1)}, bf16[160,1024]{1,0:T(8,128)(2,1)}, bf16[4,336,1024]{2,1,0...) while((s32[]{:T(128)}, bf16[2,160,1024]{2,1,0:T(8,128)(2,1)}, ...), condition=%wide.region_3.4_spmd, body=%wide.region_2.3_spmd.sunk | while | flops 8455716864 | bytes 47186396 | solution.py:924
  409.8 45.2 %layer_forward.7 = (bf16[4,336,1024]{2,1,0:T(8,128)(2,1)S(1)}, bf16[4,336,3072]{2,1,0:T(8,128)(2,1)}, bf16[4,24,448,128]{3,2,1,0:T(8,128)(2,1)}, bf16[4,336,1024...) custom-call(s32[4]{0:T(128)} %pad_add_fusion.4.flags, ...), custom_call_target="tpu_custom_call", output_to_operand_aliasing={{0}: (15, {}), {1}: (16, {}), {2}: (17, {}), {3}: (18, {}),... | custom-call | flops 8455716864 | bytes 41943040 | tf_op jit(solution)/shard_map/while/body/eval_jaxpr/layer_forward/pallas_call | solution.py:627
  465.2 45.2 %layer_forward.7 = (bf16[4,336,1024]{2,1,0:T(8,128)(2,1)S(1)}, bf16[4,336,3072]{2,1,0:T(8,128)(2,1)}, bf16[4,24,448,128]{3,2,1,0:T(8,128)(2,1)}, bf16[4,336,1024...) custom-call(s32[4]{0:T(128)} %pad_add_fusion.4.flags, ...), custom_call_target="tpu_custom_call", output_to_operand_aliasing={{0}: (15, {}), {1}: (16, {}), {2}: (17, {}), {3}: (18, {}),... | custom-call | flops 8455716864 | bytes 41943040 | tf_op jit(solution)/shard_map/while/body/eval_jaxpr/layer_forward/pallas_call | solution.py:627
  520.6 45.3 %layer_forward.7 = (bf16[4,336,1024]{2,1,0:T(8,128)(2,1)S(1)}, bf16[4,336,3072]{2,1,0:T(8,128)(2,1)}, bf16[4,24,448,128]{3,2,1,0:T(8,128)(2,1)}, bf16[4,336,1024...) custom-call(s32[4]{0:T(128)} %pad_add_fusion.4.flags, ...), custom_call_target="tpu_custom_call", output_to_operand_aliasing={{0}: (15, {}), {1}: (16, {}), {2}: (17, {}), {3}: (18, {}),... | custom-call | flops 8455716864 | bytes 41943040 | tf_op jit(solution)/shard_map/while/body/eval_jaxpr/layer_forward/pallas_call | solution.py:627
  576.0 45.3 %layer_forward.7 = (bf16[4,336,1024]{2,1,0:T(8,128)(2,1)S(1)}, bf16[4,336,3072]{2,1,0:T(8,128)(2,1)}, bf16[4,24,448,128]{3,2,1,0:T(8,128)(2,1)}, bf16[4,336,1024...) custom-call(s32[4]{0:T(128)} %pad_add_fusion.4.flags, ...), custom_call_target="tpu_custom_call", output_to_operand_aliasing={{0}: (15, {}), {1}: (16, {}), {2}: (17, {}), {3}: (18, {}),... | custom-call | flops 8455716864 | bytes 41943040 | tf_op jit(solution)/shard_map/while/body/eval_jaxpr/layer_forward/pallas_call | solution.py:627
  673.1 38.5 %collective-permute-start = (bf16[160,1024]{1,0:T(8,128)(2,1)}, bf16[160,1024]{1,0:T(8,128)(2,1)}, u32[]{:S(2)}, u32[]{:S(2)}) collective-permute-start(bf16[160,1024]{1,0:T(8,128)(2,1)} %get-tuple-element.1927), channel_id=1, source_target_pairs={{0,8},{1,9},{2,10},{3,11},{8,17},{9,18},{10,19},{11,16},{16,24},{1... | collective-permute-start | bytes 983048 | tf_op jit(solution)/shard_map/while/body/eval_jaxpr/ppermute | solution.py:772
  757.5 37.5 %collective-permute-start.1 = (bf16[160,1024]{1,0:T(8,128)(2,1)}, bf16[160,1024]{1,0:T(8,128)(2,1)}, u32[]{:S(2)}, u32[]{:S(2)}) collective-permute-start(bf16[160,1024]{1,0:T(8,128)(2,1)} %get-tuple-element.1928), channel_id=1, source_target_pairs={{0,11},{1,8},{2,9},{3,10},{8,16},{9,17},{10,18},{11,19},{16,27},{1... | collective-permute-start | bytes 983048 | tf_op jit(solution)/shard_map/while/body/eval_jaxpr/ppermute | solution.py:773
  834.6 497.3 %while.75 = (s32[]{:T(128)}, bf16[2,160,1024]{2,1,0:T(8,128)(2,1)}, bf16[160,1024]{1,0:T(8,128)(2,1)}, bf16[160,1024]{1,0:T(8,128)(2,1)}, bf16[4,336,1024]{2,1,0...) while((s32[]{:T(128)}, bf16[2,160,1024]{2,1,0:T(8,128)(2,1)}, ...), condition=%wide.region_5.6_spmd, body=%wide.region_4.5_spmd.sunk | while | flops 8455716864 | bytes 57672116 | solution.py:966
  894.0 30.8 %collective-permute-done.2 = bf16[160,1024]{1,0:T(8,128)(2,1)} collective-permute-done((bf16[160,1024]{1,0:T(8,128)(2,1)}, bf16[160,1024]{1,0:T(8,128)(2,1)}, u32[]{:S(2)}, u32[]{:S(2)}) %collective-permute-start.2) | collective-permute-done | bytes 327712 | tf_op jit(solution)/shard_map/while/body/eval_jaxpr/ppermute | solution.py:772
  940.8 43.2 %collective-permute-done.2 = bf16[160,1024]{1,0:T(8,128)(2,1)} collective-permute-done((bf16[160,1024]{1,0:T(8,128)(2,1)}, bf16[160,1024]{1,0:T(8,128)(2,1)}, u32[]{:S(2)}, u32[]{:S(2)}) %collective-permute-start.2) | collective-permute-done | bytes 327712 | tf_op jit(solution)/shard_map/while/body/eval_jaxpr/ppermute | solution.py:772
  1000.1 43.2 %collective-permute-done.2 = bf16[160,1024]{1,0:T(8,128)(2,1)} collective-permute-done((bf16[160,1024]{1,0:T(8,128)(2,1)}, bf16[160,1024]{1,0:T(8,128)(2,1)}, u32[]{:S(2)}, u32[]{:S(2)}) %collective-permute-start.2) | collective-permute-done | bytes 327712 | tf_op jit(solution)/shard_map/while/body/eval_jaxpr/ppermute | solution.py:772
  1059.3 43.2 %collective-permute-done.2 = bf16[160,1024]{1,0:T(8,128)(2,1)} collective-permute-done((bf16[160,1024]{1,0:T(8,128)(2,1)}, bf16[160,1024]{1,0:T(8,128)(2,1)}, u32[]{:S(2)}, u32[]{:S(2)}) %collective-permute-start.2) | collective-permute-done | bytes 327712 | tf_op jit(solution)/shard_map/while/body/eval_jaxpr/ppermute | solution.py:772
  1117.6 43.9 %layer_backward.7 = (bf16[4,336,1024]{2,1,0:T(8,128)(2,1)S(1)}, bf16[4,336,3072]{2,1,0:T(8,128)(2,1)}, bf16[4,336,4096]{2,1,0:T(8,128)(2,1)}, bf16[4,336,1024]{2...) custom-call(s32[4]{0:T(128)} %pad_add_fusion.5.flags, ...), custom_call_target="tpu_custom_call", output_to_operand_aliasing={{0}: (14, {}), {1}: (15, {}), {2}: (16, {}), {3}: (17, {}),... | custom-call | flops 8455716864 | bytes 52428800 | tf_op jit(solution)/shard_map/while/body/eval_jaxpr/layer_backward/pallas_call | solution.py:673
  1176.9 43.9 %layer_backward.7 = (bf16[4,336,1024]{2,1,0:T(8,128)(2,1)S(1)}, bf16[4,336,3072]{2,1,0:T(8,128)(2,1)}, bf16[4,336,4096]{2,1,0:T(8,128)(2,1)}, bf16[4,336,1024]{2...) custom-call(s32[4]{0:T(128)} %pad_add_fusion.5.flags, ...), custom_call_target="tpu_custom_call", output_to_operand_aliasing={{0}: (14, {}), {1}: (15, {}), {2}: (16, {}), {3}: (17, {}),... | custom-call | flops 8455716864 | bytes 52428800 | tf_op jit(solution)/shard_map/while/body/eval_jaxpr/layer_backward/pallas_call | solution.py:673
  1230.7 43.9 %layer_backward.7 = (bf16[4,336,1024]{2,1,0:T(8,128)(2,1)S(1)}, bf16[4,336,3072]{2,1,0:T(8,128)(2,1)}, bf16[4,336,4096]{2,1,0:T(8,128)(2,1)}, bf16[4,336,1024]{2...) custom-call(s32[4]{0:T(128)} %pad_add_fusion.5.flags, ...), custom_call_target="tpu_custom_call", output_to_operand_aliasing={{0}: (14, {}), {1}: (15, {}), {2}: (16, {}), {3}: (17, {}),... | custom-call | flops 8455716864 | bytes 52428800 | tf_op jit(solution)/shard_map/while/body/eval_jaxpr/layer_backward/pallas_call | solution.py:673
  1284.5 43.9 %layer_backward.7 = (bf16[4,336,1024]{2,1,0:T(8,128)(2,1)S(1)}, bf16[4,336,3072]{2,1,0:T(8,128)(2,1)}, bf16[4,336,4096]{2,1,0:T(8,128)(2,1)}, bf16[4,336,1024]{2...) custom-call(s32[4]{0:T(128)} %pad_add_fusion.5.flags, ...), custom_call_target="tpu_custom_call", output_to_operand_aliasing={{0}: (14, {}), {1}: (15, {}), {2}: (16, {}), {3}: (17, {}),... | custom-call | flops 8455716864 | bytes 52428800 | tf_op jit(solution)/shard_map/while/body/eval_jaxpr/layer_backward/pallas_call | solution.py:673
  1353.0 14.0 collective-permute-done.9
  1389.1 45.4 %reduce-scatter.8.cloned.1.call-done = bf16[512,1024]{1,0:T(8,128)(2,1)} async-done(((bf16[2048,1024]{1,0:T(8,128)(2,1)}), bf16[512,1024]{1,0:T(8,128)(2,1)}) %reduce-scatter.8.cloned.1.call-update) | async-done | bytes 1048592 | tf_op jit(solution)/shard_map/reduce_scatter | solution.py:1030
  1480.8 14.2 add_convert_fusion.1
  1561.0 37.8 %all_gather.40 = f32[1728,128]{1,0:T(8,128)S(1)} all-gather(f32[216,128]{1,0:T(8,128)S(1)} %fusion.53), channel_id=1, replica_groups=mesh['pipe'=4,'dp'=2,'tensor'=4] {'dp','tensor'}, dimensions={0}, use_global_device_ids=true | all-gather | bytes 995328 | tf_op jit(solution)/shard_map/all_gather | solution.py:793
  1615.7 139.9 %all_gather.39 = f32[1536,128]{1,0:T(8,128)} all-gather(f32[48,128]{1,0:T(8,128)S(1)} %maximum_bitcast_fusion), channel_id=1, replica_groups=mesh['pipe'=4,'dp'=2,'tensor'=4] {'pipe','dp','tensor'}, dimensions={0}, use_global_device_ids=true | all-gather | bytes 811008 | tf_op jit(solution)/shard_map/all_gather | solution.py:793
  (430 shorter events, 675.8 us)
Async XLA Ops:
  7.2 125.0 %all-gather.7.cloned.1.call-start = ((), (), s32[]{:S(2)}) async-start(), calls=%async_computation.7 | async-start | bytes 4325376 | tf_op jit(solution)/shard_map/all_gather | solution.py:807
  8.9 180.0 %all-gather.11.cloned.1.call-start = ((), (), s32[]{:S(2)}) async-start(), calls=%async_computation.9 | async-start | bytes 2359296 | tf_op jit(solution)/shard_map/all_gather | solution.py:816
  10.7 185.1 %all-gather.9.cloned.1.call-start = ((), (), s32[]{:S(2)}) async-start(), calls=%async_computation.8 | async-start | bytes 7077888 | tf_op jit(solution)/shard_map/all_gather | solution.py:816
  13.8 264.4 %all-gather.13.cloned.1.call-start = ((), (), s32[]{:S(2)}) async-start(), calls=%async_computation.10 | async-start | bytes 9437184 | tf_op jit(solution)/shard_map/all_gather | solution.py:816
  15.0 345.2 %all-gather.15.cloned.1.call-start = ((), (), s32[]{:S(2)}) async-start(), calls=%async_computation.11 | async-start | bytes 9437184 | tf_op jit(solution)/shard_map/all_gather | solution.py:816
  17.8 1416.6 %reduce-scatter.8.cloned.1.call-start = ((), (), s32[]{:S(2)}) async-start(), calls=%async_computation.12 | async-start | bytes 5242880 | tf_op jit(solution)/shard_map/reduce_scatter | solution.py:1030
  22.3 158.9 %collective-permute-start.8 = (bf16[4,160,1024]{2,1,0:T(8,128)(2,1)}, bf16[4,160,1024]{2,1,0:T(8,128)(2,1)}, u32[]{:S(2)}, u32[]{:S(2)}) collective-permute-start(bf16[4,160,1024]{2,1,0:T(8,128)(2,1)} %get-tuple-element.1576), channel_id=1, source_target_pairs={{8,11},{9,8},{10,9},{11,10},{24,27},{25,24},{26,25},{27,26},{12,15... | collective-permute-start | bytes 3932168 | tf_op jit(solution)/shard_map/ppermute | solution.py:888
  400.7 54.4 %collective-permute-start = (bf16[160,1024]{1,0:T(8,128)(2,1)}, bf16[160,1024]{1,0:T(8,128)(2,1)}, u32[]{:S(2)}, u32[]{:S(2)}) collective-permute-start(bf16[160,1024]{1,0:T(8,128)(2,1)} %get-tuple-element.1927), channel_id=1, source_target_pairs={{0,8},{1,9},{2,10},{3,11},{8,17},{9,18},{10,19},{11,16},{16,24},{1... | collective-permute-start | bytes 983048 | tf_op jit(solution)/shard_map/while/body/eval_jaxpr/ppermute | solution.py:772
  404.7 52.1 %collective-permute-start.1 = (bf16[160,1024]{1,0:T(8,128)(2,1)}, bf16[160,1024]{1,0:T(8,128)(2,1)}, u32[]{:S(2)}, u32[]{:S(2)}) collective-permute-start(bf16[160,1024]{1,0:T(8,128)(2,1)} %get-tuple-element.1928), channel_id=1, source_target_pairs={{0,11},{1,8},{2,9},{3,10},{8,16},{9,17},{10,18},{11,19},{16,27},{1... | collective-permute-start | bytes 983048 | tf_op jit(solution)/shard_map/while/body/eval_jaxpr/ppermute | solution.py:773
  515.8 50.0 %collective-permute-start = (bf16[160,1024]{1,0:T(8,128)(2,1)}, bf16[160,1024]{1,0:T(8,128)(2,1)}, u32[]{:S(2)}, u32[]{:S(2)}) collective-permute-start(bf16[160,1024]{1,0:T(8,128)(2,1)} %get-tuple-element.1927), channel_id=1, source_target_pairs={{0,8},{1,9},{2,10},{3,11},{8,17},{9,18},{10,19},{11,16},{16,24},{1... | collective-permute-start | bytes 983048 | tf_op jit(solution)/shard_map/while/body/eval_jaxpr/ppermute | solution.py:772
  571.2 50.0 %collective-permute-start = (bf16[160,1024]{1,0:T(8,128)(2,1)}, bf16[160,1024]{1,0:T(8,128)(2,1)}, u32[]{:S(2)}, u32[]{:S(2)}) collective-permute-start(bf16[160,1024]{1,0:T(8,128)(2,1)} %get-tuple-element.1927), channel_id=1, source_target_pairs={{0,8},{1,9},{2,10},{3,11},{8,17},{9,18},{10,19},{11,16},{16,24},{1... | collective-permute-start | bytes 983048 | tf_op jit(solution)/shard_map/while/body/eval_jaxpr/ppermute | solution.py:772
  673.1 51.0 %collective-permute-start = (bf16[160,1024]{1,0:T(8,128)(2,1)}, bf16[160,1024]{1,0:T(8,128)(2,1)}, u32[]{:S(2)}, u32[]{:S(2)}) collective-permute-start(bf16[160,1024]{1,0:T(8,128)(2,1)} %get-tuple-element.1927), channel_id=1, source_target_pairs={{0,8},{1,9},{2,10},{3,11},{8,17},{9,18},{10,19},{11,16},{16,24},{1... | collective-permute-start | bytes 983048 | tf_op jit(solution)/shard_map/while/body/eval_jaxpr/ppermute | solution.py:772
  937.9 54.3 %collective-permute-start.3 = (bf16[160,1024]{1,0:T(8,128)(2,1)}, bf16[160,1024]{1,0:T(8,128)(2,1)}, u32[]{:S(2)}, u32[]{:S(2)}) collective-permute-start(bf16[160,1024]{1,0:T(8,128)(2,1)} %get-tuple-element.1967), channel_id=1, source_target_pairs={{8,0},{9,1},{10,2},{11,3},{16,11},{17,8},{18,9},{19,10},{24,16},{2... | collective-permute-start | bytes 983048 | tf_op jit(solution)/shard_map/while/body/eval_jaxpr/ppermute | solution.py:773
  997.1 54.3 %collective-permute-start.3 = (bf16[160,1024]{1,0:T(8,128)(2,1)}, bf16[160,1024]{1,0:T(8,128)(2,1)}, u32[]{:S(2)}, u32[]{:S(2)}) collective-permute-start(bf16[160,1024]{1,0:T(8,128)(2,1)} %get-tuple-element.1967), channel_id=1, source_target_pairs={{8,0},{9,1},{10,2},{11,3},{16,11},{17,8},{18,9},{19,10},{24,16},{2... | collective-permute-start | bytes 983048 | tf_op jit(solution)/shard_map/while/body/eval_jaxpr/ppermute | solution.py:773
  1056.4 54.3 %collective-permute-start.3 = (bf16[160,1024]{1,0:T(8,128)(2,1)}, bf16[160,1024]{1,0:T(8,128)(2,1)}, u32[]{:S(2)}, u32[]{:S(2)}) collective-permute-start(bf16[160,1024]{1,0:T(8,128)(2,1)} %get-tuple-element.1967), channel_id=1, source_target_pairs={{8,0},{9,1},{10,2},{11,3},{16,11},{17,8},{18,9},{19,10},{24,16},{2... | collective-permute-start | bytes 983048 | tf_op jit(solution)/shard_map/while/body/eval_jaxpr/ppermute | solution.py:773
  1115.6 54.3 %collective-permute-start.3 = (bf16[160,1024]{1,0:T(8,128)(2,1)}, bf16[160,1024]{1,0:T(8,128)(2,1)}, u32[]{:S(2)}, u32[]{:S(2)}) collective-permute-start(bf16[160,1024]{1,0:T(8,128)(2,1)} %get-tuple-element.1967), channel_id=1, source_target_pairs={{8,0},{9,1},{10,2},{11,3},{16,11},{17,8},{18,9},{19,10},{24,16},{2... | collective-permute-start | bytes 983048 | tf_op jit(solution)/shard_map/while/body/eval_jaxpr/ppermute | solution.py:773
  1377.7 95.9 %reduce-scatter.10.cloned.1.call-start = ((), (), s32[]{:S(2)}) async-start(), calls=%async_computation.13 | async-start | bytes 1572864 | tf_op jit(solution)/shard_map/reduce_scatter | solution.py:1030
  1388.1 59.6 %collective-permute-start.12 = (bf16[3072,512]{1,0:T(8,128)(2,1)}, bf16[3072,512]{1,0:T(8,128)(2,1)}, u32[]{:S(2)}, u32[]{:S(2)}) collective-permute-start(bf16[3072,512]{1,0:T(8,128)(2,1)} %convolution_convert_fusion.2), channel_id=1, source_target_pairs={{0,4},{4,0},{1,5},{5,1},{2,6},{6,2},{3,7},{7,3},{8,12},{12,8},{9,1... | collective-permute-start | bytes 9437192 | tf_op jit(solution)/shard_map/ppermute | solution.py:981
  1434.5 333.5 %reduce-scatter.16.cloned.1.call-start = ((), (), s32[]{:S(2)}) async-start(), calls=%async_computation.16 | async-start | bytes 1310720 | tf_op jit(solution)/shard_map/reduce_scatter | solution.py:990
  1447.6 322.1 %reduce-scatter.14.cloned.1.call-start = ((), (), s32[]{:S(2)}) async-start(), calls=%async_computation.15 | async-start | bytes 3932160 | tf_op jit(solution)/shard_map/reduce_scatter | solution.py:990
  1458.6 314.1 %reduce-scatter.12.cloned.1.call-start = ((), (), s32[]{:S(2)}) async-start(), calls=%async_computation.14 | async-start | bytes 655360 | tf_op jit(solution)/shard_map/reduce_scatter | solution.py:1030
  1473.6 300.7 %reduce-scatter.18.cloned.1.call-start = ((), (), s32[]{:S(2)}) async-start(), calls=%async_computation.17 | async-start | bytes 5242880 | tf_op jit(solution)/shard_map/reduce_scatter | solution.py:990
  1495.0 282.7 %reduce-scatter.20.cloned.1.call-start = ((), (), s32[]{:S(2)}) async-start(), calls=%async_computation.18 | async-start | bytes 5242880 | tf_op jit(solution)/shard_map/reduce_scatter | solution.py:990
  1607.0 155.1 %collective-permute-start.7 = (bf16[4,160,1024]{2,1,0:T(8,128)(2,1)}, bf16[4,160,1024]{2,1,0:T(8,128)(2,1)}, u32[]{:S(2)}, u32[]{:S(2)}) collective-permute-start(bf16[4,160,1024]{2,1,0:T(8,128)(2,1)} %slice_bitcast_fusion.4), channel_id=1, source_target_pairs={{8,9},{9,10},{10,11},{11,8},{24,25},{25,26},{26,27},{27,24},{12,13... | collective-permute-start | bytes 3932168 | tf_op jit(solution)/shard_map/ppermute | solution.py:938
  (75 other events, 1768.5 us)
Sparse Core Ops, SparseCore 0:
  11.6 90.4 all-gather.6
  104.3 27.7 all-gather.10
  133.7 62.0 all-gather.8
  197.8 80.2 all-gather.12
  279.6 80.5 all-gather.14
  1377.8 56.5 reduce-scatter.7
  1436.8 9.2 reduce-scatter.9
  1448.9 25.5 reduce-scatter.15
  1476.9 60.4 reduce-scatter.13
  1539.7 18.2 reduce-scatter.11
  1560.4 94.8 reduce-scatter.17
  1657.4 115.0 reduce-scatter.19

commit v2 on v1

--- a/solution.py
+++ b/solution.py
@@ -32,7 +32,7 @@
 DB = D // OWN
 TB = D // BLOCKS
 FB = FF // BLOCKS
-STEP = 16
+STEP = PAD
 SUMS = 16
 VMEM_BYTES = 60 * 1024 * 1024
 
@@ -160,7 +160,7 @@
 ):
     (x_all, qkv_all, probs_all, mixed_all, mid_all, rattn_all, rmlp_all, act_all, slope_all) = refs[11:20]
     out_all, hid_all = refs[20:22]
-    send = refs[22]
+    sends = refs[22:24]
     (
         v_qkv,
         v_proj,
@@ -185,7 +185,8 @@
         sem_w,
         sem_in,
         sem_out,
-    ) = refs[23:]
+        sem_h,
+    ) = refs[24:]
     valid = flags[0]
     slot = flags[1]
     is_first = flags[2]
@@ -221,12 +222,6 @@
 
         for block in range(BLOCKS):
             w_copy(0, block).start()
-        pos_copy().start()
-        proj_copy().start()
-        for block in range(BLOCKS):
-            w_copy(1, block).start()
-        for block in range(BLOCKS):
-            w_copy(2, block).start()
         pltpu.make_async_copy(recv_a, rin.at[pl.ds(0, HALF)], sem_in.at[0]).wait()
         pltpu.make_async_copy(recv_b, rin.at[pl.ds(HALF, HALF)], sem_in.at[1]).wait()
 
@@ -248,8 +243,12 @@
         saves[1].start()
         qkv[pl.ds(ROWS, 16), :] = jnp.zeros((16, 3 * D), BF16)
 
+        pos_copy().start()
+        proj_copy().start()
+
         def qkv_block(block, state):
             w_copy(0, block).wait()
+            w_copy(1, block).start()
             out = dot_nn(rattn[:, :DB], v_qkv[0, block])
             out = out + dot_nn(rattn[:, DB:], v_qkv[1, block])
             columns = lanes(block * 3 * TB, 3 * TB)
@@ -261,6 +260,8 @@
             qkv.at[pl.ds(0, ROWS)], qkv_all.at[slot], sem_out.at[2]
         )
         save_qkv.start()
+        for block in range(BLOCKS):
+            w_copy(2, block).start()
         pos_copy().wait()
         masks = head_masks()
 
@@ -275,20 +276,18 @@
             scores = scores + jnp.concatenate([mask[win]] * PER, 0)
             top = jnp.max(scores, -1, keepdims=True)
             powers = jnp.exp(scores - top)
-            low = (powers / jnp.sum(powers, -1, keepdims=True)).astype(BF16)
+            low = (powers * (1.0 / jnp.sum(powers, -1, keepdims=True))).astype(BF16)
             probs[win * GROUPS + group] = low
             mixed[pl.ds(base, PAD), lanes(group * 128, 128)] = pick_heads(
                 dot_nn(low, value), masks
             ).astype(BF16)
 
-        def attend_pair(index, state):
-            win = index // (GROUPS // 2)
-            pair = index % (GROUPS // 2)
-            attend(win, pair * 2)
-            attend(win, pair * 2 + 1)
+        def attend_window(win, state):
+            for group in range(GROUPS):
+                attend(win, group)
             return state
 
-        lax.fori_loop(0, WIN_COLS * GROUPS // 2, attend_pair, None)
+        lax.fori_loop(0, WIN_COLS, attend_window, None)
         saves.append(pltpu.make_async_copy(probs, probs_all.at[slot], sem_out.at[3]))
         saves[-1].start()
         saves.append(pltpu.make_async_copy(mixed, mixed_all.at[slot], sem_out.at[4]))
@@ -313,6 +312,15 @@
         saves.append(pltpu.make_async_copy(rmlp, rmlp_all.at[slot], sem_out.at[6]))
         saves[-1].start()
 
+        def hidden_saves(block):
+            columns = lanes(block * FB, FB)
+            return [
+                pltpu.make_async_copy(
+                    source.at[:, columns], target.at[slot, :, columns], sem_h.at[kind * BLOCKS + block]
+                )
+                for kind, (source, target) in enumerate(((act, act_all), (slope, slope_all)))
+            ]
+
         def hidden_block(block, state):
             w_copy(1, block).wait()
             columns = lanes(block * FB, FB)
@@ -323,6 +331,8 @@
                 chance + pre * (np.float32((2 * np.pi) ** -0.5) * jnp.exp(-0.5 * pre * pre))
             ).astype(BF16)
             act[:, columns] = (pre * chance).astype(BF16)
+            for save in hidden_saves(block):
+                save.start()
             w_copy(2, block).wait()
             for own in range(OWN):
                 half = slice(own * DB, (own + 1) * DB)
@@ -330,10 +340,6 @@
             return state
 
         lax.fori_loop(0, BLOCKS, hidden_block, None)
-        saves.append(pltpu.make_async_copy(act, act_all.at[slot], sem_out.at[7]))
-        saves[-1].start()
-        saves.append(pltpu.make_async_copy(slope, slope_all.at[slot], sem_out.at[8]))
-        saves[-1].start()
 
         def finish(rows, state):
             values = total[rows, :]
@@ -343,13 +349,17 @@
             return state
 
         row_chunks(finish)
-        saves.append(pltpu.make_async_copy(total, out_all.at[slot], sem_out.at[9]))
-        saves[-1].start()
+        save_out = pltpu.make_async_copy(total, out_all.at[slot], sem_out.at[9])
+
+        @pl.when(is_last == 1)
+        def _():
+            save_out.start()
+
         outs[...] = dot_nn(perm_out[...], outb[...]).astype(BF16)
         for half in range(2):
             rows = pl.ds(half * HALF, HALF)
             saves.append(
-                pltpu.make_async_copy(outs.at[rows], send.at[half], sem_out.at[10 + half])
+                pltpu.make_async_copy(outs.at[rows], sends[half], sem_out.at[10 + half])
             )
             saves[-1].start()
             saves.append(
@@ -357,8 +367,14 @@
             )
             saves[-1].start()
         save_qkv.wait()
+        for block in range(BLOCKS):
+            saves.extend(hidden_saves(block))
         for save in saves:
             save.wait()
+
+        @pl.when(is_last == 1)
+        def _():
+            save_out.wait()
 
 
 def backward_kernel(
@@ -379,7 +395,7 @@
     *refs,
 ):
     x_all, qkv_all, slope_all, dbm_all, dx_all, sums_all, dpos_all = refs[7:14]
-    send = refs[14]
+    sends = refs[14:16]
     (
         v_qkv,
         v_proj,
@@ -405,7 +421,8 @@
         sem_w,
         sem_in,
         sem_out,
-    ) = refs[15:]
+        sem_h,
+    ) = refs[16:]
     valid = flags[0]
     slot = flags[1]
     is_last = flags[3]
@@ -437,29 +454,25 @@
             )[index]
             return pltpu.make_async_copy(source, target, sem_in.at[index])
 
-        for index in range(5):
+        for index in range(4):
             load(index).start()
+
+        @pl.when(is_last == 1)
+        def _():
+            load(4).start()
+
         w_copy(0, 0).start()
         load(5).start()
         w_copy(1, 0).start()
-        for block in range(1, BLOCKS):
-            w_copy(0, block).start()
-            w_copy(1, block).start()
-        load(6).start()
-        proj_copy().start()
-        load(7).start()
-        load(8).start()
-        for block in range(BLOCKS):
-            w_copy(2, block).start()
-        load(9).start()
-        load(10).start()
-        for index in range(5):
+        for index in range(4):
             load(index).wait()
         sums[...] = jnp.zeros_like(sums)
         grad[...] = dot_nn(perm_in[...], rcot[...])
 
         @pl.when(is_last == 1)
         def _():
+            load(4).wait()
+
             def final_norm(rows, state):
                 cot = grad[rows, :]
                 hat, rstd = norm_stats(last[rows, :])
@@ -487,12 +500,32 @@
         saves[0].start()
         load(5).wait()
 
+        def hidden_save(block):
+            columns = lanes(block * FB, FB)
+            return pltpu.make_async_copy(
+                slope.at[:, columns], slope_all.at[slot, :, columns], sem_h.at[block]
+            )
+
         def hidden_block(block, state):
             columns = lanes(block * FB, FB)
             w_copy(0, block).wait()
+
+            @pl.when(block < BLOCKS - 1)
+            def _():
+                w_copy(0, block + 1).start()
+                w_copy(1, block + 1).start()
+
+            @pl.when(block == BLOCKS - 1)
+            def _():
+                load(6).start()
+                proj_copy().start()
+                load(7).start()
+                load(8).start()
+
             dact = dot_nt(dbm[:, :DB], v_fc2[0, block]) + dot_nt(dbm[:, DB:], v_fc2[1, block])
             dpre = (dact * slope[:, columns].astype(F32)).astype(BF16)
             slope[:, columns] = dpre
+            hidden_save(block).start()
             sums[pl.ds(8 + block, 1), :] = jnp.sum(dpre.astype(F32), 0, keepdims=True)
             w_copy(1, block).wait()
             for own in range(OWN):
@@ -501,8 +534,14 @@
             return state
 
         lax.fori_loop(0, BLOCKS, hidden_block, None)
-        saves.append(pltpu.make_async_copy(slope, slope_all.at[slot], sem_out.at[1]))
-        saves[-1].start()
+        for block in range(BLOCKS):
+            w_copy(2, block).start()
+        load(9).start()
+
+        @pl.when(slot > 0)
+        def _():
+            load(10).start()
+
         load(6).wait()
 
         def mlp_norm(rows, state):
@@ -528,7 +567,15 @@
             dmix[:, block * TB : (block + 1) * TB] = out.astype(BF16)
         load(7).wait()
         load(8).wait()
-        load(10).wait()
+
+        @pl.when(slot > 0)
+        def _():
+            load(10).wait()
+
+        @pl.when(slot == 0)
+        def _():
+            dpos[...] = jnp.zeros_like(dpos)
+
         qkv[pl.ds(ROWS, 16), :] = jnp.zeros((16, 3 * D), BF16)
         masks = head_masks()
 
@@ -554,7 +601,10 @@
                 dqkv[pl.ds(base, PAD), lanes(column + 2 * TB, 128)] = dvalue[:PAD].astype(BF16)
             return state
 
-        lax.fori_loop(0, GROUPS, attend_back, None)
+        def attend_back_pair(pair, state):
+            return attend_back(2 * pair + 1, attend_back(2 * pair, state))
+
+        lax.fori_loop(0, GROUPS // 2, attend_back_pair, None)
         saves.append(pltpu.make_async_copy(dqkv, qkv_all.at[slot], sem_out.at[3]))
         saves[-1].start()
         saves.append(pltpu.make_async_copy(dpos, dpos_all, sem_out.at[4]))
@@ -589,13 +639,15 @@
         for half in range(2):
             rows = pl.ds(half * HALF, HALF)
             saves.append(
-                pltpu.make_async_copy(outs.at[rows], send.at[half], sem_out.at[6 + half])
+                pltpu.make_async_copy(outs.at[rows], sends[half], sem_out.at[6 + half])
             )
             saves[-1].start()
             saves.append(
                 pltpu.make_async_copy(outs.at[rows], dx_all.at[slot, half], sem_out.at[8 + half])
             )
             saves[-1].start()
+        for block in range(BLOCKS):
+            saves.append(hidden_save(block))
         for save in saves:
             save.wait()
 
@@ -626,12 +678,12 @@
     wide = lambda dtype: pltpu.VMEM((ROWS, D), dtype)
     results = pl.pallas_call(
         forward_kernel,
-        out_shape=shapes_of(stacks) + [jax.ShapeDtypeStruct((2, HALF, D), BF16)],
+        out_shape=shapes_of(stacks) + [jax.ShapeDtypeStruct((HALF, D), BF16)] * 2,
         in_specs=[pl.BlockSpec(memory_space=pltpu.SMEM)]
         + any_specs(3)
         + vmem_specs(6)
         + any_specs(5 + len(stacks)),
-        out_specs=any_specs(len(stacks) + 1),
+        out_specs=any_specs(len(stacks) + 2),
         scratch_shapes=WEIGHT_SCRATCH
         + [
             pltpu.VMEM((GROUPS, STACK, KEYS), F32),
@@ -653,6 +705,7 @@
             pltpu.SemaphoreType.DMA((3 * BLOCKS + 2,)),
             pltpu.SemaphoreType.DMA((2,)),
             pltpu.SemaphoreType.DMA((14,)),
+            pltpu.SemaphoreType.DMA((2 * BLOCKS,)),
         ],
         input_output_aliases={first_stack + index: index for index in range(len(stacks))},
         compiler_params=pltpu.CompilerParams(vmem_limit_bytes=VMEM_BYTES),
@@ -661,7 +714,7 @@
         ),
         name="layer_forward",
     )(*inputs)
-    return results[-1], tuple(results[:-1])
+    return results[-2:], tuple(results[:-2])
 
 
 def layer_backward(flags, recv_a, recv_b, cots, tables, weights, saved, stacks):
@@ -672,12 +725,12 @@
     wide = lambda dtype: pltpu.VMEM((ROWS, D), dtype)
     results = pl.pallas_call(
         backward_kernel,
-        out_shape=shapes_of(stacks) + [jax.ShapeDtypeStruct((2, HALF, D), BF16)],
+        out_shape=shapes_of(stacks) + [jax.ShapeDtypeStruct((HALF, D), BF16)] * 2,
         in_specs=[pl.BlockSpec(memory_space=pltpu.SMEM)]
         + any_specs(3)
         + vmem_specs(3)
         + any_specs(4 + len(saved) + len(stacks)),
-        out_specs=any_specs(len(stacks) + 1),
+        out_specs=any_specs(len(stacks) + 2),
         scratch_shapes=WEIGHT_SCRATCH
         + [
             pltpu.VMEM((2 * HALF, D), BF16),
@@ -700,6 +753,7 @@
             pltpu.SemaphoreType.DMA((3 * BLOCKS + 1,)),
             pltpu.SemaphoreType.DMA((11,)),
             pltpu.SemaphoreType.DMA((10,)),
+            pltpu.SemaphoreType.DMA((BLOCKS,)),
         ],
         input_output_aliases={first_stack + index: index for index in range(len(stacks))},
         compiler_params=pltpu.CompilerParams(vmem_limit_bytes=VMEM_BYTES),
@@ -708,7 +762,7 @@
         ),
         name="layer_backward",
     )(*inputs)
-    return results[-1], tuple(results[:-1])
+    return results[-2:], tuple(results[:-2])
 
 
 def on_device(
@@ -747,15 +801,14 @@
     micro_count = cotangent.shape[1]
     own_width = D // dp_count
 
-    def section_pairs(step, moves):
+    def section_pairs(sections, step, moves):
         pairs = []
-        for section in range(section_count):
-            if 0 <= section + step < section_count:
-                for tensor in range(tensor_count):
-                    target = (tensor + copies * moves[section % 2]) % tensor_count
-                    pairs.append(
-                        (section * tensor_count + tensor, (section + step) * tensor_count + target)
-                    )
+        for section in sections:
+            for tensor in range(tensor_count):
+                target = (tensor + copies * moves[section % 2]) % tensor_count
+                pairs.append(
+                    (section * tensor_count + tensor, (section + step) * tensor_count + target)
+                )
         return pairs
 
     def odd_pairs(move):
@@ -768,10 +821,31 @@
             for tensor in range(tensor_count)
         ]
 
-    def hop(halves, step):
-        to_a = lax.ppermute(halves[1], ("pipe", "tensor"), section_pairs(step, (0, 1)))
-        to_b = lax.ppermute(halves[0], ("pipe", "tensor"), section_pairs(step, (-1, 0)))
+    def hop(halves, sections, step):
+        axes = ("pipe", "tensor")
+        to_a = lax.ppermute(halves[1], axes, section_pairs(sections, step, (0, 1)))
+        to_b = lax.ppermute(halves[0], axes, section_pairs(sections, step, (-1, 0)))
         return to_a, to_b
+
+    def shares_summed(values, axis):
+        count = lax.axis_size(axis)
+        index = lax.axis_index(axis)
+        blocks = values.reshape((count, values.shape[0] // count) + values.shape[1:])
+        total = lax.dynamic_index_in_dim(blocks, index, 0, keepdims=False).astype(F32)
+        for step in range(1, count):
+            block = lax.dynamic_index_in_dim(blocks, (index + step) % count, 0, keepdims=False)
+            pairs = [(source, (source + step) % count) for source in range(count)]
+            total = total + lax.ppermute(block, axis, pairs).astype(F32)
+        return total
+
+    def summed(values, axis):
+        count = lax.axis_size(axis)
+        step = 1
+        while step < count:
+            pairs = [(source, source ^ step) for source in range(count)]
+            values = values + lax.ppermute(values, axis, pairs)
+            step *= 2
+        return values
 
     def whole_unit(rows, axis):
         if copies == 1:
@@ -803,14 +877,27 @@
         return rows.reshape(rows.shape[:-3] + (UNIT, D))
 
     share = w_merge.shape[0]
-    small = jnp.concatenate((merge_gain, merge_bias, final_gain, final_bias)).astype(BF16)
-    merge_weight = lax.all_gather(w_merge.astype(BF16), all_axes, axis=0, tiled=True)
-    small_all = lax.all_gather(small, all_axes, axis=0)
     fshare = final_gain.shape[0]
+    small = jnp.concatenate((merge_gain, merge_bias, final_gain, final_bias))
+    small = jnp.pad(small, (0, 8 * D - small.shape[0])).reshape(8, D)
+    packed = jnp.concatenate((w_merge, small)).astype(BF16)
+    packed = lax.all_gather(packed, group_axes, axis=0)
+    parts = [packed]
+    for step in range(1, section_count):
+        pairs = [(source, (source + step) % section_count) for source in range(section_count)]
+        parts.append(lax.ppermute(packed, "pipe", pairs))
+    parts = parts[::-1]
+    packed = lax.dynamic_slice_in_dim(
+        jnp.concatenate(parts + parts[:-1]),
+        (section_count - 1 - section_now) * packed.shape[0],
+        section_count * packed.shape[0],
+    )
+    merge_weight = packed[:, :share].reshape(merge_in, D)
+    small_all = packed[:, share]
     merge_scale = small_all[:, :share].reshape(-1).astype(F32)
     merge_shift = small_all[:, share : 2 * share].reshape(-1).astype(F32)
     final_scale = small_all[:, 2 * share : 2 * share + fshare].reshape(-1).astype(F32)
-    final_shift = small_all[:, 2 * share + fshare :].reshape(-1).astype(F32)
+    final_shift = small_all[:, 2 * share + fshare : 2 * (share + fshare)].reshape(-1).astype(F32)
 
     def gather(weight):
         return lax.all_gather(weight.astype(BF16), group_axes, axis=0)
@@ -896,32 +983,47 @@
         slot = jnp.clip(slot_now, 0, micro_count - 1)
         return jnp.stack([flag.astype(jnp.int32) for flag in (is_valid, slot, is_first, is_last)])
 
-    def stack_of(shape, dtype):
-        return jnp.zeros((micro_count,) + shape, dtype)
-
-    def forward_tick(tick_now, state):
-        outgoing, recv_a, recv_b, stacks = state
-        next_a, next_b = hop(outgoing, 1)
+    def busy(starts, tick_now):
+        return [
+            section
+            for section, start in enumerate(starts)
+            if 0 <= tick_now - 2 * start < micro_count
+        ]
+
+    def stacks_of(*kinds):
+        return pl.pallas_call(
+            lambda *refs: None,
+            out_shape=[jax.ShapeDtypeStruct(shape, dtype) for shape, dtype in kinds],
+            out_specs=any_specs(len(kinds)),
+        )()
+
+    def of_micro(shape, dtype):
+        return ((micro_count,) + shape, dtype)
+
+    *stacks, empty_a, empty_b = stacks_of(
+        of_micro((ROWS, D), BF16),
+        of_micro((ROWS, 3 * D), BF16),
+        of_micro((WIN_COLS * GROUPS, STACK, KEYS), BF16),
+        of_micro((ROWS, D), BF16),
+        of_micro((ROWS, D), F32),
+        of_micro((ROWS, D), BF16),
+        of_micro((ROWS, D), BF16),
+        of_micro((ROWS, FF), BF16),
+        of_micro((ROWS, FF), BF16),
+        of_micro((ROWS, D), F32),
+        of_micro((2, HALF, D), BF16),
+        ((HALF, D), BF16),
+        ((HALF, D), BF16),
+    )
+    starts = list(range(section_count))
+    recv = (empty_a, empty_b)
+    for tick_now in range(tick_count):
+        senders = [section for section in busy(starts, tick_now - 1) if section < section_count - 1]
+        coming = hop(outgoing, senders, 1) if senders else (empty_a, empty_b)
         outgoing, stacks = layer_forward(
-            flags_at(section_now, tick_now), recv_a, recv_b, firsts, forward_tables, weights, stacks
+            flags_at(section_now, tick_now), *recv, firsts, forward_tables, weights, stacks
         )
-        return outgoing, next_a, next_b, stacks
-
-    empty = jnp.zeros((2, HALF, D), BF16)
-    stacks = (
-        stack_of((ROWS, D), BF16),
-        stack_of((ROWS, 3 * D), BF16),
-        stack_of((WIN_COLS * GROUPS, STACK, KEYS), BF16),
-        stack_of((ROWS, D), BF16),
-        stack_of((ROWS, D), F32),
-        stack_of((ROWS, D), BF16),
-        stack_of((ROWS, D), BF16),
-        stack_of((ROWS, FF), BF16),
-        stack_of((ROWS, FF), BF16),
-        stack_of((ROWS, D), F32),
-        stack_of((2, HALF, D), BF16),
-    )
-    state = lax.fori_loop(0, tick_count, forward_tick, (empty, empty[0], empty[1], stacks))
+        recv = coming
     (
         x_all,
         qkv_all,
@@ -934,37 +1036,41 @@
         slope_all,
         out_all,
         hid_all,
-    ) = state[3]
+    ) = stacks
     hid_before = lax.ppermute(hid_all[:, 1], ("pipe", "tensor"), odd_pairs(1))
-    shown = jnp.where(is_odd, jnp.stack((hid_before, hid_all[:, 0]), 1), hid_all)
-    shown = own_part(from_halves(shown), 1)
-
-    def backward_tick(tick_now, state):
-        outgoing, recv_a, recv_b, stacks = state
-        next_a, next_b = hop(outgoing, -1)
+
+    stacks = (
+        x_all,
+        qkv_all,
+        slope_all,
+        *stacks_of(
+            of_micro((ROWS, D), BF16),
+            of_micro((2, HALF, D), BF16),
+            of_micro((SUMS, D), F32),
+            ((GROUPS, STACK, KEYS), F32),
+        ),
+    )
+    starts = starts[::-1]
+    recv = (empty_a, empty_b)
+    for tick_now in range(tick_count):
+        senders = [section for section in busy(starts, tick_now - 1) if section > 0]
+        coming = hop(outgoing, senders, -1) if senders else (empty_a, empty_b)
+        flags = flags_at(section_count - 1 - section_now, tick_now)
+        if tick_now == tick_count // 2:
+            flags, hid_before = lax.optimization_barrier((flags, hid_before))
         outgoing, stacks = layer_backward(
-            flags_at(section_count - 1 - section_now, tick_now),
-            recv_a,
-            recv_b,
+            flags,
+            *recv,
             cots,
             backward_tables,
             weights,
             (probs_all, mid_all, out_all),
             stacks,
         )
-        return outgoing, next_a, next_b, stacks
-
-    stacks = (
-        x_all,
-        qkv_all,
-        slope_all,
-        stack_of((ROWS, D), BF16),
-        stack_of((2, HALF, D), BF16),
-        stack_of((SUMS, D), F32),
-        jnp.zeros((GROUPS, STACK, KEYS), F32),
-    )
-    state = lax.fori_loop(0, tick_count, backward_tick, (empty, empty[0], empty[1], stacks))
-    dba_all, dqkv_all, dpre_all, dbm_all, dx_all, sums_all, dpos = state[3]
+        recv = coming
+    dba_all, dqkv_all, dpre_all, dbm_all, dx_all, sums_all, dpos = stacks
+    shown = jnp.where(is_odd, jnp.stack((hid_before, hid_all[:, 0]), 1), hid_all)
+    shown = own_part(from_halves(shown), 1)
 
     def weight_gradient(left, right):
         left = left.reshape(micro_count * ROWS, -1)
@@ -989,6 +1095,7 @@
     def over_tensor(total):
         return lax.psum_scatter(total.astype(BF16), "tensor", scatter_dimension=0, tiled=True)
 
+    g_proj = over_tensor(weight_gradient(mixed_all, dba_all)).astype(F32)
     g_fc2 = over_tensor(weight_gradient(act_all, dbm_all)).astype(F32)
     g_fc1 = over_tensor(weight_gradient(dpre_all, rmlp_all)).astype(F32).T
     g_qkv = weight_gradient(dqkv_all, rattn_all)
@@ -996,23 +1103,6 @@
         g_qkv = g_qkv.reshape(BLOCKS, 3, copies, TB // copies, own_width)
         g_qkv = g_qkv.transpose(0, 2, 1, 3, 4).reshape(3 * D, own_width)
     g_qkv = over_tensor(g_qkv).astype(F32).T.reshape(own_width, 3, D // tensor_count)
-    g_proj = over_tensor(weight_gradient(mixed_all, dba_all)).astype(F32)
-
-    sums = jnp.sum(sums_all, 0)
-    dpos = dpos.reshape(D // HEAD, PAD, KEYS)[:, : WIN * WIN, : WIN * WIN]
-    dpos = dpos.reshape(D // HEAD, WIN, WIN, WIN, WIN).transpose(0, 1, 3, 2, 4)
-    dpos = dpos.reshape(D // HEAD, WIN * WIN, WIN * WIN)
-    dtable = jnp.einsum("hxy,vy->hxv", dpos, offsets, precision=lax.Precision.HIGHEST)
-    dtable = jnp.einsum("hxv,ux->huv", dtable, offsets, precision=lax.Precision.HIGHEST)
-    local_sums = jnp.concatenate((sums[:15].reshape(-1), dtable.reshape(-1)))
-    local_sums = jnp.sum(gather_rows(local_sums, group_axes), 0) / copies
-    sums = local_sums[: 15 * D].reshape(15, D)
-    dtable = local_sums[15 * D :].reshape(tensor_count, heads_here, -1)
-    g_table = lax.dynamic_index_in_dim(dtable, tensor_now, 0, keepdims=False).T
-    dqv = sums[12:15].reshape(BLOCKS, 3, TB)[:, 0::2].transpose(1, 0, 2).reshape(2, D)
-    g_qv = lax.dynamic_slice_in_dim(
-        dqv, tensor_now * (D // tensor_count), D // tensor_count, 1
-    )
 
     own_grads = dx_all[:owned]
     for section in range(1, section_count):
@@ -1021,16 +1111,39 @@
         )
         own_grads = jnp.where(section_now == section, moved, own_grads)
     grad_merged = own_part(from_halves(own_grads), 1).reshape(owned * rows_here, D)
-    g_merge = dot_tn(merged_in, grad_merged).astype(BF16)
+    g_merge = dot_tn(merged_in, grad_merged)
+    g_merge = g_merge.reshape(section_count, dp_count, tensor_count, share, D)
+    g_merge = shares_summed(g_merge.transpose(1, 0, 2, 3, 4).astype(BF16), "dp")[0]
+    g_merge = shares_summed(g_merge.astype(BF16), "pipe")[0]
+    g_merge = shares_summed(g_merge.astype(BF16), "tensor")[0]
     grad_unit = dot_nt(grad_merged, merge_weight)
     merge_sums = jnp.stack((jnp.sum(grad_unit * raw_hat, 0), jnp.sum(grad_unit, 0)))
     grad_raw = norm_back(raw_hat, raw_rstd, grad_unit * merge_scale)
     grad_raw = grad_raw.reshape(raw_pages.shape).astype(BF16)
-    for axis in all_axes:
-        g_merge = lax.psum_scatter(g_merge, axis, scatter_dimension=0, tiled=True)
-    final_sums = jnp.sum(sums_all, 0)[6:8] * is_last.astype(F32) / copies
-    edge = jnp.concatenate((merge_sums.reshape(-1), final_sums.reshape(-1)))
-    edge = jnp.sum(gather_rows(edge, all_axes), 0)
+
+    sums = jnp.sum(sums_all, 0) / copies
+    dpos = dpos.reshape(D // HEAD, PAD, KEYS)[:, : WIN * WIN, : WIN * WIN]
+    dpos = dpos.reshape(D // HEAD, WIN, WIN, WIN, WIN).transpose(0, 1, 3, 2, 4)
+    dpos = dpos.reshape(D // HEAD, WIN * WIN, WIN * WIN) / copies
+    dtable = jnp.einsum("hxy,vy->hxv", dpos, offsets, precision=lax.Precision.HIGHEST)
+    dtable = jnp.einsum("hxv,ux->huv", dtable, offsets, precision=lax.Precision.HIGHEST)
+    final_sums = sums[6:8] * is_last.astype(F32)
+    every = jnp.concatenate((merge_sums.reshape(-1), final_sums.reshape(-1)))
+    vector = jnp.concatenate((every, sums.reshape(-1), dtable.reshape(-1)))
+    size = vector.shape[0]
+    vector = jnp.pad(vector, (0, -size % D)).reshape(-1, 128)
+    for axis in group_axes:
+        vector = summed(vector, axis)
+    edge_rows = every.shape[0] // 128
+    edge = summed(vector[:edge_rows], "pipe").reshape(-1)
+    local_sums = vector[edge_rows:].reshape(-1)
+    sums = local_sums[: SUMS * D].reshape(SUMS, D)
+    dtable = local_sums[SUMS * D : SUMS * D + dtable.size].reshape(tensor_count, heads_here, -1)
+    g_table = lax.dynamic_index_in_dim(dtable, tensor_now, 0, keepdims=False).T
+    dqv = sums[12:15].reshape(BLOCKS, 3, TB)[:, 0::2].transpose(1, 0, 2).reshape(2, D)
+    g_qv = lax.dynamic_slice_in_dim(
+        dqv, tensor_now * (D // tensor_count), D // tensor_count, 1
+    )
     place = (section_now * dp_count + dp_now) * tensor_count + tensor_now
     edge_parts = []
     start = 0
@@ -1040,7 +1153,7 @@
     return (
         shown[None, :, None],
         grad_raw,
-        g_merge.astype(F32),
+        g_merge,
         *edge_parts,
         g_qkv[None],
         g_proj[None],

time: 1810 us -> 1270 us (0.70)
  waiting for transfers between devices: 514 us -> 247 us
  blocking collectives: 275 us -> 10.3 us
  starting transfers between devices: 198 us -> 432 us
  local copies, waits for them, and re-layouts: 258 us -> 133 us
  Pallas kernels: 368 us -> 274 us
    ppermute x40 -> x47, starting transfers between devices: 180 us -> 410 us  [the longest x16 289 us: hop(): to_a = lax.ppermute(halves[1], axes, section_pairs(sections, step, (0, 1)))]
    all_gather x3 -> x1, blocking collectives: 188 us -> 10.3 us  [gather_rows(): rows = lax.all_gather(rows, axes, axis=0, tiled=True)]
    ppermute x40 -> x47, waiting for transfers between devices: 256 us -> 132 us  [the longest x7 37.7 us: shares_summed(): total = total + lax.ppermute(block, axis, pairs).astype(F32)]
    all_gather x1 -> x0, blocking collectives: 86.9 us -> none  [on_device(): small_all = lax.all_gather(small, all_axes, axis=0)]
    all_gather x4, waiting for transfers between devices: 171 us -> 89.6 us  [gather(): return lax.all_gather(weight.astype(BF16), group_axes, axis=0)]
    pallas_call x10, Pallas kernels: 187 us -> 111 us  [layer_forward(): pl.pallas_call(forward_kernel, out_shape=shapes_of(stacks) + [jax.ShapeDt...]
    while x40 -> x0, local copies, waits for them, and re-layouts: 68.7 us -> none
    reduce_scatter x3 -> x0, waiting for transfers between devices: 45.4 us -> none  [on_device(): g_merge = lax.psum_scatter(g_merge, axis, scatter_dimension=0, tiled=True)]
  transfers between devices with their start and end apart: 64 -> 68, of which waited for: 32 -> 21; matrix products, arithmetic and copies ran while one was open for 15% -> 20% of each run, Pallas kernels for 21% -> 16%
where the time goes in v2:
time: 1270 us; the launch traced here: 1260 us
  starting transfers between devices  432 us (34%)
  Pallas kernels  274 us (22%)
  waiting for transfers between devices  247 us (19%)
  local copies, waits for them, and re-layouts  133 us (10%)
  matrix products  90 us (7%)
  other arithmetic  60.9 us (5%)
  between operations  16.2 us (1%)
    ppermute x16, starting transfers between devices, hop(): to_a = lax.ppermute(halves[1], axes, section_pairs(sections, step, (0, 1)))  289 us
    pallas_call x10, Pallas kernels, layer_backward(): pl.pallas_call(backward_kernel, out_shape=shapes_of(stacks) + [jax.ShapeD...  162 us
    pallas_call x10, Pallas kernels, layer_forward(): pl.pallas_call(forward_kernel, out_shape=shapes_of(stacks) + [jax.ShapeDt...  111 us
    all_gather x4, waiting for transfers between devices, gather(): return lax.all_gather(weight.astype(BF16), group_axes, axis=0)  89.6 us
    dot_general x9, matrix products, dot_tn(): lax.dot_general(left, right, (((0,), (0,)), ((), ())), preferred_element_...  74.9 us
    unnamed x152, local copies, waits for them, and re-layouts  45.1 us
    ppermute x3, starting transfers between devices, on_device(): parts.append(lax.ppermute(packed, 'pipe', pairs))  42.3 us
    ppermute x16, starting transfers between devices, hop(): to_b = lax.ppermute(halves[0], axes, section_pairs(sections, step, (-1, 0)))  41.3 us
  transfers between devices with their start and end apart: 68, of which 21 were waited for; matrix products, arithmetic and copies ran while one was open for 20% of the time, Pallas kernels for 16%

profile of v2, /device:TPU:9, one launch (start us, length us, event | category | flops | bytes accessed | tf_op | source)
XLA Modules:
  0.0 1262.5 jit_solution(7342203600873617677)
XLA Ops:
  59.9 41.8 %collective-permute-start = (bf16[8,72,1024]{2,0,1:T(8,128)(2,1)}, bf16[8,72,1024]{2,0,1:T(8,128)(2,1)}, u32[]{:S(2)}, u32[]{:S(2)}) collective-permute-start(bf16[8,72,1024]{2,0,1:T(8,128)(2,1)} %copy.266), channel_id=1, source_target_pairs={{0,24},{8,0},{16,8},{24,16},{1,25},{9,1},{17,9},{25,17},{2,26},{10... | collective-permute-start | bytes 3538952 | tf_op jit(solution)/shard_map/ppermute | solution.py:888
  113.0 11.7 collective-permute-done
  129.8 21.0 %collective-permute-done.2 = bf16[8,72,1024]{2,0,1:T(8,128)(2,1)} collective-permute-done((bf16[8,72,1024]{2,0,1:T(8,128)(2,1)}, bf16[8,72,1024]{2,0,1:T(8,128)(2,1)}, u32[]{:S(2)}, u32[]{:S(2)}) %collective-permute-start.2) | collective-permute-done | bytes 1179680 | tf_op jit(solution)/shard_map/ppermute | solution.py:888
  228.3 82.1 %all-gather.14.cloned.1.call-done = bf16[8,1024,512]{2,1,0:T(8,128)(2,1)} async-done(((bf16[1,1024,512]{2,1,0:T(8,128)(2,1)}), bf16[8,1024,512]{2,1,0:T(8,128)(2,1)}) %all-gather.14.cloned.1.call-update) | async-done | bytes 8388624 | tf_op jit(solution)/shard_map/all_gather | solution.py:903
  310.4 24.6 %layer_forward.10 = (bf16[4,336,1024]{2,1,0:T(8,128)(2,1)}, bf16[4,336,3072]{2,1,0:T(8,128)(2,1)}, bf16[4,24,448,128]{3,2,1,0:T(8,128)(2,1)}, bf16[4,336,1024]{2...) custom-call(s32[4]{0:T(128)} %get-tuple-element.578.flags, ...), custom_call_target="tpu_custom_call", output_to_operand_aliasing={{0}: (15, {}), {1}: (16, {}), {2}: (17, {}), {3}: (18, {}),... | custom-call | flops 8455716864 | bytes 41943040 | tf_op jit(solution)/shard_map/layer_forward/pallas_call | solution.py:679
  337.6 25.1 %layer_forward.11 = (bf16[4,336,1024]{2,1,0:T(8,128)(2,1)}, bf16[4,336,3072]{2,1,0:T(8,128)(2,1)}, bf16[4,24,448,128]{3,2,1,0:T(8,128)(2,1)}, bf16[4,336,1024]{2...) custom-call(s32[4]{0:T(128)} %get-tuple-element.577.flags, ...), custom_call_target="tpu_custom_call", output_to_operand_aliasing={{0}: (15, {}), {1}: (16, {}), {2}: (17, {}), {3}: (18, {}),... | custom-call | flops 8455716864 | bytes 41943040 | tf_op jit(solution)/shard_map/layer_forward/pallas_call | solution.py:679
  366.2 24.6 %layer_forward.12 = (bf16[4,336,1024]{2,1,0:T(8,128)(2,1)}, bf16[4,336,3072]{2,1,0:T(8,128)(2,1)}, bf16[4,24,448,128]{3,2,1,0:T(8,128)(2,1)}, bf16[4,336,1024]{2...) custom-call(s32[4]{0:T(128)} %add_add_fusion.7.flags, ...), custom_call_target="tpu_custom_call", output_to_operand_aliasing={{0}: (15, {}), {1}: (16, {}), {2}: (17, {}), {3}: (18, {}),... | custom-call | flops 8455716864 | bytes 41943040 | tf_op jit(solution)/shard_map/layer_forward/pallas_call | solution.py:679
  394.3 24.8 %layer_forward.13 = (bf16[4,336,1024]{2,1,0:T(8,128)(2,1)}, bf16[4,336,3072]{2,1,0:T(8,128)(2,1)}, bf16[4,24,448,128]{3,2,1,0:T(8,128)(2,1)}, bf16[4,336,1024]{2...) custom-call(s32[4]{0:T(128)} %add_add_fusion.4.flags, ...), custom_call_target="tpu_custom_call", output_to_operand_aliasing={{0}: (15, {}), {1}: (16, {}), {2}: (17, {}), {3}: (18, {}),... | custom-call | flops 8455716864 | bytes 41943040 | tf_op jit(solution)/shard_map/layer_forward/pallas_call | solution.py:679
  424.1 20.8 %collective-permute-start.16 = (bf16[160,1024]{1,0:T(8,128)(2,1)}, bf16[160,1024]{1,0:T(8,128)(2,1)S(1)}, u32[]{:S(2)}, u32[]{:S(2)}) collective-permute-start(bf16[160,1024]{1,0:T(8,128)(2,1)} %get-tuple-element.326), channel_id=1, source_target_pairs={{8,17},{9,18},{10,19},{11,16},{16,24},{17,25},{18,26},{19,27},{12,... | collective-permute-start | bytes 983048 | tf_op jit(solution)/shard_map/ppermute | solution.py:826
  453.8 30.1 %collective-permute-start.14 = (bf16[160,1024]{1,0:T(8,128)(2,1)}, bf16[160,1024]{1,0:T(8,128)(2,1)S(1)}, u32[]{:S(2)}, u32[]{:S(2)}) collective-permute-start(bf16[160,1024]{1,0:T(8,128)(2,1)} %get-tuple-element.324), channel_id=1, source_target_pairs={{8,17},{9,18},{10,19},{11,16},{16,24},{17,25},{18,26},{19,27},{12,... | collective-permute-start | bytes 983048 | tf_op jit(solution)/shard_map/ppermute | solution.py:826
  531.8 185.4 %collective-permute-start.30 = (bf16[160,1024]{1,0:T(8,128)(2,1)}, bf16[160,1024]{1,0:T(8,128)(2,1)S(1)}, u32[]{:S(2)}, u32[]{:S(2)}) collective-permute-start(bf16[160,1024]{1,0:T(8,128)(2,1)} %get-tuple-element.416), channel_id=1, source_target_pairs={{16,8},{17,9},{18,10},{19,11},{24,17},{25,18},{26,19},{27,16},{20,... | collective-permute-start | bytes 983048 | tf_op jit(solution)/shard_map/ppermute | solution.py:826
  725.7 38.6 %collective-permute-start.28 = (bf16[160,1024]{1,0:T(8,128)(2,1)}, bf16[160,1024]{1,0:T(8,128)(2,1)S(1)}, u32[]{:S(2)}, u32[]{:S(2)}) collective-permute-start(bf16[160,1024]{1,0:T(8,128)(2,1)} %get-tuple-element.414), channel_id=1, source_target_pairs={{16,8},{17,9},{18,10},{19,11},{24,17},{25,18},{26,19},{27,16},{20,... | collective-permute-start | bytes 983048 | tf_op jit(solution)/shard_map/ppermute | solution.py:826
  789.3 25.3 %collective-permute-done.34.recv_a = bf16[160,1024]{1,0:T(8,128)(2,1)S(1)} collective-permute-done((bf16[160,1024]{1,0:T(8,128)(2,1)}, bf16[160,1024]{1,0:T(8,128)(2,1)S(1)}, u32[]{:S(2)}, u32[]{:S(2)}) %collective-permute-start.34) | collective-permute-done | bytes 327712 | tf_op jit(solution)/shard_map/ppermute | solution.py:826
  822.7 31.5 %layer_backward.16 = (bf16[4,336,1024]{2,1,0:T(8,128)(2,1)}, bf16[4,336,3072]{2,1,0:T(8,128)(2,1)}, bf16[4,336,4096]{2,1,0:T(8,128)(2,1)}, bf16[4,336,1024]{2,1,...) custom-call(s32[4]{0:T(128)} %add_add_fusion.18.flags, ...), custom_call_target="tpu_custom_call", output_to_operand_aliasing={{0}: (14, {}), {1}: (15, {}), {2}: (16, {}), {3}: (17, {}),... | custom-call | flops 8455716864 | bytes 52428800 | tf_op jit(solution)/shard_map/layer_backward/pallas_call | solution.py:726
  860.0 32.6 %layer_backward.17 = (bf16[4,336,1024]{2,1,0:T(8,128)(2,1)}, bf16[4,336,3072]{2,1,0:T(8,128)(2,1)}, bf16[4,336,4096]{2,1,0:T(8,128)(2,1)}, bf16[4,336,1024]{2,1,...) custom-call(s32[4]{0:T(128)} %add_add_fusion.12.flags, ...), custom_call_target="tpu_custom_call", output_to_operand_aliasing={{0}: (14, {}), {1}: (15, {}), {2}: (16, {}), {3}: (17, {}),... | custom-call | flops 8455716864 | bytes 52428800 | tf_op jit(solution)/shard_map/layer_backward/pallas_call | solution.py:726
  897.3 32.9 %layer_backward.18 = (bf16[4,336,1024]{2,1,0:T(8,128)(2,1)}, bf16[4,336,3072]{2,1,0:T(8,128)(2,1)}, bf16[4,336,4096]{2,1,0:T(8,128)(2,1)}, bf16[4,336,1024]{2,1,...) custom-call(s32[4]{0:T(128)} %add_add_fusion.19.flags, ...), custom_call_target="tpu_custom_call", output_to_operand_aliasing={{0}: (14, {}), {1}: (15, {}), {2}: (16, {}), {3}: (17, {}),... | custom-call | flops 8455716864 | bytes 52428800 | tf_op jit(solution)/shard_map/layer_backward/pallas_call | solution.py:726
  933.3 33.0 %layer_backward.19 = (bf16[4,336,1024]{2,1,0:T(8,128)(2,1)}, bf16[4,336,3072]{2,1,0:T(8,128)(2,1)}, bf16[4,336,4096]{2,1,0:T(8,128)(2,1)}, bf16[4,336,1024]{2,1,...) custom-call(s32[4]{0:T(128)} %add_add_fusion.11.flags, ...), custom_call_target="tpu_custom_call", output_to_operand_aliasing={{0}: (14, {}), {1}: (15, {}), {2}: (16, {}), {3}: (17, {}),... | custom-call | flops 8455716864 | bytes 52428800 | tf_op jit(solution)/shard_map/layer_backward/pallas_call | solution.py:726
  966.4 10.5 convolution_convert_fusion.2
  989.4 10.9 add_convert_fusion.2
  1026.7 11.5 convolution_convert_fusion
  1045.7 11.9 add_convert_fusion
  1145.5 10.5 collective-permute-done.52
  1191.2 11.9 collective-permute-done.45
  1218.0 14.9 %collective-permute-done.48 = bf16[1,64,1024]{2,1,0:T(8,128)(2,1)S(1)} collective-permute-done((bf16[1,64,1024]{2,1,0:T(8,128)(2,1)S(1)}, bf16[1,64,1024]{2,1,0:T(8,128)(2,1)S(1)}, u32[]{:S(2)}, u32[]{:S(2)}) %collective-permute-start.48) | collective-permute-done | bytes 131104 | tf_op jit(solution)/shard_map/ppermute | solution.py:838
  (437 shorter events, 478.6 us)
Async XLA Ops:
  7.2 49.7 %all-gather.6.cloned.1.call-start = ((), (), s32[]{:S(2)}) async-start(), calls=%async_computation.4 | async-start | bytes 1327104 | tf_op jit(solution)/shard_map/all_gather | solution.py:884
  11.6 209.2 %all-gather.10.cloned.1.call-start = ((), (), s32[]{:S(2)}) async-start(), calls=%async_computation.6 | async-start | bytes 2359296 | tf_op jit(solution)/shard_map/all_gather | solution.py:903
  13.6 207.2 %all-gather.8.cloned.1.call-start = ((), (), s32[]{:S(2)}) async-start(), calls=%async_computation.5 | async-start | bytes 7077888 | tf_op jit(solution)/shard_map/all_gather | solution.py:903
  16.6 211.8 %all-gather.12.cloned.1.call-start = ((), (), s32[]{:S(2)}) async-start(), calls=%async_computation.7 | async-start | bytes 9437184 | tf_op jit(solution)/shard_map/all_gather | solution.py:903
  17.8 292.6 %all-gather.14.cloned.1.call-start = ((), (), s32[]{:S(2)}) async-start(), calls=%async_computation.8 | async-start | bytes 9437184 | tf_op jit(solution)/shard_map/all_gather | solution.py:903
  20.6 1195.7 %reduce-scatter.7.cloned.1.call-start = ((), (), s32[]{:S(2)}) async-start(), calls=%async_computation.10 | async-start | bytes 1310720 | tf_op jit(solution)/shard_map/reduce_scatter | solution.py:1096
  25.1 187.4 %collective-permute-start.23 = (bf16[4,160,1024]{2,1,0:T(8,128)(2,1)}, bf16[4,160,1024]{2,1,0:T(8,128)(2,1)}, u32[]{:S(2)}, u32[]{:S(2)}) collective-permute-start(bf16[4,160,1024]{2,1,0:T(8,128)(2,1)} %get-tuple-element.556), channel_id=1, source_target_pairs={{8,11},{9,8},{10,9},{11,10},{24,27},{25,24},{26,25},{27,26},{12,15... | collective-permute-start | bytes 3932168 | tf_op jit(solution)/shard_map/ppermute | solution.py:975
  59.9 64.8 %collective-permute-start = (bf16[8,72,1024]{2,0,1:T(8,128)(2,1)}, bf16[8,72,1024]{2,0,1:T(8,128)(2,1)}, u32[]{:S(2)}, u32[]{:S(2)}) collective-permute-start(bf16[8,72,1024]{2,0,1:T(8,128)(2,1)} %copy.266), channel_id=1, source_target_pairs={{0,24},{8,0},{16,8},{24,16},{1,25},{9,1},{17,9},{25,17},{2,26},{10... | collective-permute-start | bytes 3538952 | tf_op jit(solution)/shard_map/ppermute | solution.py:888
  103.3 47.5 %collective-permute-start.2 = (bf16[8,72,1024]{2,0,1:T(8,128)(2,1)}, bf16[8,72,1024]{2,0,1:T(8,128)(2,1)}, u32[]{:S(2)}, u32[]{:S(2)}) collective-permute-start(bf16[8,72,1024]{2,0,1:T(8,128)(2,1)} %copy.266), channel_id=1, source_target_pairs={{0,8},{8,16},{16,24},{24,0},{1,9},{9,17},{17,25},{25,1},{2,10},{10... | collective-permute-start | bytes 3538952 | tf_op jit(solution)/shard_map/ppermute | solution.py:888
  171.5 46.0 %collective-permute-start.3 = (bf16[1,2,160,1024]{3,2,1,0:T(8,128)(2,1)S(1)}, bf16[1,2,160,1024]{3,2,1,0:T(8,128)(2,1)}, u32[]{:S(2)}, u32[]{:S(2)}) collective-permute-start(bf16[1,2,160,1024]{3,2,1,0:T(8,128)(2,1)S(1)} %pad.30), channel_id=1, source_target_pairs={{8,0},{9,1},{10,2},{11,3},{12,4},{13,5},{14,6},{15,7}} | collective-permute-start | bytes 1966088 | tf_op jit(solution)/shard_map/ppermute | solution.py:971
  424.1 66.2 %collective-permute-start.16 = (bf16[160,1024]{1,0:T(8,128)(2,1)}, bf16[160,1024]{1,0:T(8,128)(2,1)S(1)}, u32[]{:S(2)}, u32[]{:S(2)}) collective-permute-start(bf16[160,1024]{1,0:T(8,128)(2,1)} %get-tuple-element.326), channel_id=1, source_target_pairs={{8,17},{9,18},{10,19},{11,16},{16,24},{17,25},{18,26},{19,27},{12,... | collective-permute-start | bytes 983048 | tf_op jit(solution)/shard_map/ppermute | solution.py:826
  444.9 45.5 %collective-permute-start.17 = (bf16[160,1024]{1,0:T(8,128)(2,1)}, bf16[160,1024]{1,0:T(8,128)(2,1)S(1)}, u32[]{:S(2)}, u32[]{:S(2)}) collective-permute-start(bf16[160,1024]{1,0:T(8,128)(2,1)} %get-tuple-element.327), channel_id=1, source_target_pairs={{8,16},{9,17},{10,18},{11,19},{16,27},{17,24},{18,25},{19,26},{12,... | collective-permute-start | bytes 983048 | tf_op jit(solution)/shard_map/ppermute | solution.py:827
  518.3 205.9 %collective-permute-start.24 = (bf16[160,1024]{1,0:T(8,128)(2,1)}, bf16[160,1024]{1,0:T(8,128)(2,1)}, u32[]{:S(2)}, u32[]{:S(2)}) collective-permute-start(bf16[160,1024]{1,0:T(8,128)(2,1)} %get-tuple-element.396), channel_id=1, source_target_pairs={{24,17},{25,18},{26,19},{27,16},{28,21},{29,22},{30,23},{31,20}} | collective-permute-start | bytes 983048 | tf_op jit(solution)/shard_map/ppermute | solution.py:826
  519.7 204.5 %collective-permute-start.25 = (bf16[160,1024]{1,0:T(8,128)(2,1)}, bf16[160,1024]{1,0:T(8,128)(2,1)}, u32[]{:S(2)}, u32[]{:S(2)}) collective-permute-start(bf16[160,1024]{1,0:T(8,128)(2,1)} %get-tuple-element.397), channel_id=1, source_target_pairs={{24,16},{25,17},{26,18},{27,19},{28,20},{29,21},{30,22},{31,23}} | collective-permute-start | bytes 983048 | tf_op jit(solution)/shard_map/ppermute | solution.py:827
  521.2 263.2 %collective-permute-start.22 = (bf16[4,160,1024]{2,1,0:T(8,128)(2,1)S(1)}, bf16[4,160,1024]{2,1,0:T(8,128)(2,1)S(1)}, u32[]{:S(2)}, u32[]{:S(2)}) collective-permute-start(bf16[4,160,1024]{2,1,0:T(8,128)(2,1)S(1)} %slice_bitcast_fusion), channel_id=1, source_target_pairs={{8,9},{9,10},{10,11},{11,8},{24,25},{25,26},{26,27},{27,24},{12,13... | collective-permute-start | bytes 3932168 | tf_op jit(solution)/shard_map/ppermute | solution.py:1040
  531.8 239.5 %collective-permute-start.30 = (bf16[160,1024]{1,0:T(8,128)(2,1)}, bf16[160,1024]{1,0:T(8,128)(2,1)S(1)}, u32[]{:S(2)}, u32[]{:S(2)}) collective-permute-start(bf16[160,1024]{1,0:T(8,128)(2,1)} %get-tuple-element.416), channel_id=1, source_target_pairs={{16,8},{17,9},{18,10},{19,11},{24,17},{25,18},{26,19},{27,16},{20,... | collective-permute-start | bytes 983048 | tf_op jit(solution)/shard_map/ppermute | solution.py:826
  717.1 54.2 %collective-permute-start.31 = (bf16[160,1024]{1,0:T(8,128)(2,1)}, bf16[160,1024]{1,0:T(8,128)(2,1)S(1)}, u32[]{:S(2)}, u32[]{:S(2)}) collective-permute-start(bf16[160,1024]{1,0:T(8,128)(2,1)} %get-tuple-element.417), channel_id=1, source_target_pairs={{16,11},{17,8},{18,9},{19,10},{24,16},{25,17},{26,18},{27,19},{20,... | collective-permute-start | bytes 983048 | tf_op jit(solution)/shard_map/ppermute | solution.py:827
  725.7 58.7 %collective-permute-start.28 = (bf16[160,1024]{1,0:T(8,128)(2,1)}, bf16[160,1024]{1,0:T(8,128)(2,1)S(1)}, u32[]{:S(2)}, u32[]{:S(2)}) collective-permute-start(bf16[160,1024]{1,0:T(8,128)(2,1)} %get-tuple-element.414), channel_id=1, source_target_pairs={{16,8},{17,9},{18,10},{19,11},{24,17},{25,18},{26,19},{27,16},{20,... | collective-permute-start | bytes 983048 | tf_op jit(solution)/shard_map/ppermute | solution.py:826
  786.7 70.2 %collective-permute-start.32 = (bf16[160,1024]{1,0:T(8,128)(2,1)}, bf16[160,1024]{1,0:T(8,128)(2,1)S(1)}, u32[]{:S(2)}, u32[]{:S(2)}) collective-permute-start(bf16[160,1024]{1,0:T(8,128)(2,1)} %get-tuple-element.432), channel_id=1, source_target_pairs={{8,1},{9,2},{10,3},{11,0},{16,8},{17,9},{18,10},{19,11},{12,5},{13... | collective-permute-start | bytes 983048 | tf_op jit(solution)/shard_map/ppermute | solution.py:826
  788.0 71.3 %collective-permute-start.33 = (bf16[160,1024]{1,0:T(8,128)(2,1)}, bf16[160,1024]{1,0:T(8,128)(2,1)S(1)}, u32[]{:S(2)}, u32[]{:S(2)}) collective-permute-start(bf16[160,1024]{1,0:T(8,128)(2,1)} %get-tuple-element.433), channel_id=1, source_target_pairs={{8,0},{9,1},{10,2},{11,3},{16,11},{17,8},{18,9},{19,10},{12,4},{13... | collective-permute-start | bytes 983048 | tf_op jit(solution)/shard_map/ppermute | solution.py:827
  989.3 249.3 %reduce-scatter.5.cloned.1.call-start = ((), (), s32[]{:S(2)}) async-start(), calls=%async_computation.9 | async-start | bytes 3932160 | tf_op jit(solution)/shard_map/reduce_scatter | solution.py:1096
  1000.3 241.2 %reduce-scatter.9.cloned.1.call-start = ((), (), s32[]{:S(2)}) async-start(), calls=%async_computation.11 | async-start | bytes 5242880 | tf_op jit(solution)/shard_map/reduce_scatter | solution.py:1096
  1026.5 226.2 %reduce-scatter.11.cloned.1.call-start = ((), (), s32[]{:S(2)}) async-start(), calls=%async_computation.12 | async-start | bytes 5242880 | tf_op jit(solution)/shard_map/reduce_scatter | solution.py:1096
  1123.2 49.3 %collective-permute-start.43 = (bf16[1,4,4,64,1024]{4,3,2,1,0:T(8,128)(2,1)S(1)}, bf16[1,4,4,64,1024]{4,3,2,1,0:T(8,128)(2,1)}, u32[]{:S(2)}, u32[]{:S(2)}) collective-permute-start(bf16[1,4,4,64,1024]{4,3,2,1,0:T(8,128)(2,1)S(1)} %dynamic-slice_bitcast_fusion), channel_id=1, source_target_pairs={{0,4},{4,0},{1,5},{5,1},{2,6},{6,2},{3,7},{7,3},{8,12},{12,8},{9,1... | collective-permute-start | bytes 6291464 | tf_op jit(solution)/shard_map/ppermute | solution.py:838
  (111 other events, 1664.7 us)
Sparse Core Ops, SparseCore 0:
  11.8 24.1 all-gather.5
  38.2 28.8 all-gather.9
  68.7 77.8 all-gather.7
  148.0 80.2 all-gather.11
  229.8 80.5 all-gather.13
  989.4 23.8 reduce-scatter.6
  1015.7 60.4 reduce-scatter.4
  1078.6 83.2 reduce-scatter.8
  1164.2 88.4 reduce-scatter.10

commit v3 on v2

--- a/solution.py
+++ b/solution.py
@@ -136,6 +136,14 @@
     return (group // 2) * (3 * TB) + (group % 2) * 128
 
 
+def weight_views(w_tall, w_wide, v_qkv, v_fc1, v_fc2, block):
+    return (
+        (w_wide.at[:, block, :, pl.ds(0, 3 * TB)], v_qkv.at[:, block]),
+        (w_wide.at[:, block, :, pl.ds(3 * TB, FB)], v_fc1.at[:, block]),
+        (w_tall.at[:, block, pl.ds(0, FB)], v_fc2.at[:, block]),
+    )
+
+
 def lanes(start, size):
     return pl.ds(pl.multiple_of(start, 128), size)
 
@@ -152,10 +160,8 @@
     bias_qkv,
     bias_fc1,
     bias_pos,
-    w_qkv,
-    w_proj,
-    w_fc1,
-    w_fc2,
+    w_tall,
+    w_wide,
     *refs,
 ):
     (x_all, qkv_all, probs_all, mixed_all, mid_all, rattn_all, rmlp_all, act_all, slope_all) = refs[11:20]
@@ -195,13 +201,13 @@
     @pl.when(valid == 1)
     def _():
         def w_copy(kind, block):
-            source, target = ((w_qkv, v_qkv), (w_fc1, v_fc1), (w_fc2, v_fc2))[kind]
+            source, target = weight_views(w_tall, w_wide, v_qkv, v_fc1, v_fc2, block)[kind]
+            return pltpu.make_async_copy(source, target, sem_w.at[kind * BLOCKS + block])
+
+        def proj_copy():
             return pltpu.make_async_copy(
-                source.at[:, block], target.at[:, block], sem_w.at[kind * BLOCKS + block]
+                w_tall.at[:, :, pl.ds(FB, TB)], v_proj, sem_w.at[3 * BLOCKS]
             )
-
-        def proj_copy():
-            return pltpu.make_async_copy(w_proj, v_proj, sem_w.at[3 * BLOCKS])
 
         def pos_copy():
             return pltpu.make_async_copy(bias_pos, v_pos, sem_w.at[3 * BLOCKS + 1])
@@ -385,10 +391,8 @@
     perm_in,
     perm_out,
     vecs,
-    w_qkv,
-    w_proj,
-    w_fc1,
-    w_fc2,
+    w_tall,
+    w_wide,
     probs_all,
     mid_all,
     out_all,
@@ -430,13 +434,13 @@
     @pl.when(valid == 1)
     def _():
         def w_copy(kind, block):
-            source, target = ((w_fc2, v_fc2), (w_fc1, v_fc1), (w_qkv, v_qkv))[kind]
+            source, target = weight_views(w_tall, w_wide, v_qkv, v_fc1, v_fc2, block)[2 - kind]
+            return pltpu.make_async_copy(source, target, sem_w.at[kind * BLOCKS + block])
+
+        def proj_copy():
             return pltpu.make_async_copy(
-                source.at[:, block], target.at[:, block], sem_w.at[kind * BLOCKS + block]
+                w_tall.at[:, :, pl.ds(FB, TB)], v_proj, sem_w.at[3 * BLOCKS]
             )
-
-        def proj_copy():
-            return pltpu.make_async_copy(w_proj, v_proj, sem_w.at[3 * BLOCKS])
 
         def load(index):
             source, target = (
@@ -682,7 +686,7 @@
         in_specs=[pl.BlockSpec(memory_space=pltpu.SMEM)]
         + any_specs(3)
         + vmem_specs(6)
-        + any_specs(5 + len(stacks)),
+        + any_specs(3 + len(stacks)),
         out_specs=any_specs(len(stacks) + 2),
         scratch_shapes=WEIGHT_SCRATCH
         + [
@@ -729,7 +733,7 @@
         in_specs=[pl.BlockSpec(memory_space=pltpu.SMEM)]
         + any_specs(3)
         + vmem_specs(3)
-        + any_specs(4 + len(saved) + len(stacks)),
+        + any_specs(2 + len(saved) + len(stacks)),
         out_specs=any_specs(len(stacks) + 2),
         scratch_shapes=WEIGHT_SCRATCH
         + [
@@ -881,7 +885,33 @@
     small = jnp.concatenate((merge_gain, merge_bias, final_gain, final_bias))
     small = jnp.pad(small, (0, 8 * D - small.shape[0])).reshape(8, D)
     packed = jnp.concatenate((w_merge, small)).astype(BF16)
-    packed = lax.all_gather(packed, group_axes, axis=0)
+    tall_rows = (w_fc2.shape[1], w_proj.shape[1], packed.size // own_width)
+    tall = jnp.concatenate(
+        (w_fc2[0].astype(BF16), w_proj[0].astype(BF16), packed.reshape(-1, own_width))
+    )
+    wide = jnp.concatenate(
+        (w_qkv[0].astype(BF16).reshape(own_width, -1), w_fc1[0].astype(BF16)), 1
+    )
+    tall = lax.all_gather(tall, group_axes, axis=0)
+    wide = lax.all_gather(wide, group_axes, axis=0)
+    packed = tall[:, tall_rows[0] + tall_rows[1] :].reshape((-1,) + packed.shape)
+    tall = tall.reshape((dp_count, tensor_count) + tall.shape[1:])
+    wide = wide.reshape((dp_count, tensor_count) + wide.shape[1:])
+    if (dp_count, tensor_count) != (OWN, BLOCKS):
+        fc2_full = tall[:, :, : tall_rows[0]].transpose(1, 2, 0, 3)
+        fc2_full = fc2_full.reshape(BLOCKS, FB, OWN, DB).transpose(2, 0, 1, 3)
+        proj_full = tall[:, :, tall_rows[0] : tall_rows[0] + tall_rows[1]].transpose(1, 2, 0, 3)
+        proj_full = proj_full.reshape(BLOCKS, TB, OWN, DB).transpose(2, 0, 1, 3)
+        tall = jnp.concatenate((fc2_full, proj_full), 2)
+        qkv_width = 3 * D // tensor_count
+        qkv_full = wide[..., :qkv_width].reshape(dp_count, tensor_count, own_width, 3, -1)
+        qkv_full = qkv_full.transpose(0, 2, 3, 1, 4).reshape(OWN, DB, 3, BLOCKS, TB)
+        qkv_full = qkv_full.transpose(0, 3, 1, 2, 4).reshape(OWN, BLOCKS, DB, 3 * TB)
+        fc1_full = wide[..., qkv_width:].transpose(0, 2, 1, 3)
+        fc1_full = fc1_full.reshape(OWN, DB, BLOCKS, FB).transpose(0, 2, 1, 3)
+        wide = jnp.concatenate((qkv_full, fc1_full), 3)
+    weights = (tall, wide)
+
     parts = [packed]
     for step in range(1, section_count):
         pairs = [(source, (source + step) % section_count) for source in range(section_count)]
@@ -898,31 +928,6 @@
     merge_shift = small_all[:, share : 2 * share].reshape(-1).astype(F32)
     final_scale = small_all[:, 2 * share : 2 * share + fshare].reshape(-1).astype(F32)
     final_shift = small_all[:, 2 * share + fshare : 2 * (share + fshare)].reshape(-1).astype(F32)
-
-    def gather(weight):
-        return lax.all_gather(weight.astype(BF16), group_axes, axis=0)
-
-    split = (dp_count, tensor_count)
-    qkv_weight = gather(w_qkv[0].reshape(own_width, -1))
-    proj_weight = gather(w_proj[0])
-    fc1_weight = gather(w_fc1[0])
-    fc2_weight = gather(w_fc2[0])
-    if split == (OWN, BLOCKS):
-        qkv_weight = qkv_weight.reshape(OWN, BLOCKS, DB, 3 * TB)
-        proj_weight = proj_weight.reshape(OWN, BLOCKS, TB, DB)
-        fc1_weight = fc1_weight.reshape(OWN, BLOCKS, DB, FB)
-        fc2_weight = fc2_weight.reshape(OWN, BLOCKS, FB, DB)
-    else:
-        qkv_weight = qkv_weight.reshape(split + (own_width, 3, -1)).transpose(0, 2, 3, 1, 4)
-        qkv_weight = qkv_weight.reshape(OWN, DB, 3, BLOCKS, TB).transpose(0, 3, 1, 2, 4)
-        qkv_weight = qkv_weight.reshape(OWN, BLOCKS, DB, 3 * TB)
-        proj_weight = proj_weight.reshape(split + (-1, own_width)).transpose(1, 2, 0, 3)
-        proj_weight = proj_weight.reshape(BLOCKS, TB, OWN, DB).transpose(2, 0, 1, 3)
-        fc1_weight = fc1_weight.reshape(split + (own_width, -1)).transpose(0, 2, 1, 3)
-        fc1_weight = fc1_weight.reshape(OWN, DB, BLOCKS, FB).transpose(0, 2, 1, 3)
-        fc2_weight = fc2_weight.reshape(split + (-1, own_width)).transpose(1, 2, 0, 3)
-        fc2_weight = fc2_weight.reshape(BLOCKS, FB, OWN, DB).transpose(2, 0, 1, 3)
-    weights = (qkv_weight, proj_weight, fc1_weight, fc2_weight)
 
     heads_here = rel_table.shape[2]
     head_set = jnp.concatenate((qv_bias[0].reshape(-1), rel_table[0].reshape(-1)))
@@ -983,13 +988,6 @@
         slot = jnp.clip(slot_now, 0, micro_count - 1)
         return jnp.stack([flag.astype(jnp.int32) for flag in (is_valid, slot, is_first, is_last)])
 
-    def busy(starts, tick_now):
-        return [
-            section
-            for section, start in enumerate(starts)
-            if 0 <= tick_now - 2 * start < micro_count
-        ]
-
     def stacks_of(*kinds):
         return pl.pallas_call(
             lambda *refs: None,
@@ -1015,11 +1013,11 @@
         ((HALF, D), BF16),
         ((HALF, D), BF16),
     )
-    starts = list(range(section_count))
     recv = (empty_a, empty_b)
     for tick_now in range(tick_count):
-        senders = [section for section in busy(starts, tick_now - 1) if section < section_count - 1]
-        coming = hop(outgoing, senders, 1) if senders else (empty_a, empty_b)
+        coming = recv
+        if tick_now > 0:
+            coming = hop(outgoing, range(section_count - 1), 1)
         outgoing, stacks = layer_forward(
             flags_at(section_now, tick_now), *recv, firsts, forward_tables, weights, stacks
         )
@@ -1050,11 +1048,11 @@
             ((GROUPS, STACK, KEYS), F32),
         ),
     )
-    starts = starts[::-1]
     recv = (empty_a, empty_b)
     for tick_now in range(tick_count):
-        senders = [section for section in busy(starts, tick_now - 1) if section > 0]
-        coming = hop(outgoing, senders, -1) if senders else (empty_a, empty_b)
+        coming = recv
+        if tick_now > 0:
+            coming = hop(outgoing, range(1, section_count), -1)
         flags = flags_at(section_count - 1 - section_now, tick_now)
         if tick_now == tick_count // 2:
             flags, hid_before = lax.optimization_barrier((flags, hid_before))
@@ -1095,7 +1093,11 @@
     def over_tensor(total):
         return lax.psum_scatter(total.astype(BF16), "tensor", scatter_dimension=0, tiled=True)
 
-    g_proj = over_tensor(weight_gradient(mixed_all, dba_all)).astype(F32)
+    g_proj = weight_gradient(mixed_all, dba_all).astype(BF16)
+    g_proj, act_all, dbm_all, dpre_all, rmlp_all, dqkv_all, rattn_all = lax.optimization_barrier(
+        (g_proj, act_all, dbm_all, dpre_all, rmlp_all, dqkv_all, rattn_all)
+    )
+    g_proj = over_tensor(g_proj).astype(F32)
     g_fc2 = over_tensor(weight_gradient(act_all, dbm_all)).astype(F32)
     g_fc1 = over_tensor(weight_gradient(dpre_all, rmlp_all)).astype(F32).T
     g_qkv = weight_gradient(dqkv_all, rattn_all)

time: 1270 us -> 1140 us (0.90)
  starting transfers between devices: 432 us -> 182 us
  waiting for transfers between devices: 247 us -> 358 us
    ppermute x16, starting transfers between devices: 289 us -> 55.2 us  [hop(): to_a = lax.ppermute(halves[1], axes, section_pairs(sections, step, (0, 1)))]
    ppermute x16, waiting for transfers between devices: 25.3 us -> 108 us  [hop(): to_a = lax.ppermute(halves[1], axes, section_pairs(sections, step, (0, 1)))]
    ppermute x16, waiting for transfers between devices: 13.5 us -> 35.6 us  [hop(): to_b = lax.ppermute(halves[0], axes, section_pairs(sections, step, (-1, 0)))]
    ppermute x16, starting transfers between devices: 41.3 us -> 61.2 us  [hop(): to_b = lax.ppermute(halves[0], axes, section_pairs(sections, step, (-1, 0)))]
    reduce_scatter x4, waiting for transfers between devices: 7.77 us -> 23.7 us  [over_tensor(): lax.psum_scatter(total.astype(BF16), 'tensor', scatter_dimension=0, tiled...]
    all_gather x5 -> x2, waiting for transfers between devices: 89.6 us -> 75.5 us  [the longest x1 70.6 us: on_device(): tall = lax.all_gather(tall, group_axes, axis=0)]
    ppermute x5, starting transfers between devices: 21.8 us -> 8.93 us  [summed(): values = values + lax.ppermute(values, axis, pairs)]
    unnamed x152 -> x163, local copies, waits for them, and re-layouts: 45.1 us -> 42.8 us
  transfers between devices with their start and end apart: 68 -> 65, of which waited for: 21 -> 27; matrix products, arithmetic and copies ran while one was open for 20% -> 21% of each run, Pallas kernels for 16% -> 18%
where the time goes in v3:
time: 1140 us; the launch traced here: 1120 us
  waiting for transfers between devices  358 us (31%)
  Pallas kernels  272 us (24%)
  starting transfers between devices  182 us (16%)
  local copies, waits for them, and re-layouts  130 us (11%)
  matrix products  92.1 us (8%)
  other arithmetic  58.1 us (5%)
  between operations  16.6 us (1%)
  blocking collectives  15 us (1%)
    pallas_call x10, Pallas kernels, layer_backward(): pl.pallas_call(backward_kernel, out_shape=shapes_of(stacks) + [jax.ShapeD...  164 us
    ppermute x16, waiting for transfers between devices, hop(): to_a = lax.ppermute(halves[1], axes, section_pairs(sections, step, (0, 1)))  108 us
    pallas_call x10, Pallas kernels, layer_forward(): pl.pallas_call(forward_kernel, out_shape=shapes_of(stacks) + [jax.ShapeDt...  107 us
    dot_general x9, matrix products, dot_tn(): lax.dot_general(left, right, (((0,), (0,)), ((), ())), preferred_element_...  76.9 us
    all_gather x1, waiting for transfers between devices, on_device(): tall = lax.all_gather(tall, group_axes, axis=0)  70.6 us
    ppermute x16, starting transfers between devices, hop(): to_b = lax.ppermute(halves[0], axes, section_pairs(sections, step, (-1, 0)))  61.2 us
    ppermute x16, starting transfers between devices, hop(): to_a = lax.ppermute(halves[1], axes, section_pairs(sections, step, (0, 1)))  55.2 us
    unnamed x163, local copies, waits for them, and re-layouts  42.8 us
  transfers between devices with their start and end apart: 65, of which 27 were waited for; matrix products, arithmetic and copies ran while one was open for 21% of the time, Pallas kernels for 18%

profile of v3, /device:TPU:9, one launch (start us, length us, event | category | flops | bytes accessed | tf_op | source)
XLA Modules:
  0.0 1123.6 jit_solution(8464712221532218505)
XLA Ops:
  22.1 15.0 %all_gather.17 = f32[128,128]{1,0:T(8,128)S(1)} all-gather(f32[32,128]{1,0:T(8,128)S(1)} %fusion.63), channel_id=1, replica_groups=mesh['pipe'=4,'dp'=2,'tensor'=4] {'tensor'}, dimensions={0}, use_global_device_ids=true | all-gather | bytes 81920 | tf_op jit(solution)/shard_map/all_gather | solution.py:871
  50.2 70.6 %all-gather.5.cloned.1.call-done = bf16[11392,512]{1,0:T(8,128)(2,1)} async-done(((bf16[1424,512]{1,0:T(8,128)(2,1)}), bf16[11392,512]{1,0:T(8,128)(2,1)}) %all-gather.5.cloned.1.call-update) | async-done | bytes 11665424 | tf_op jit(solution)/shard_map/all_gather | solution.py:895
  126.1 30.3 %collective-permute-start = (bf16[8,72,1024]{2,1,0:T(8,128)(2,1)}, bf16[8,72,1024]{2,1,0:T(8,128)(2,1)}, u32[]{:S(2)}, u32[]{:S(2)}) collective-permute-start(bf16[8,72,1024]{2,1,0:T(8,128)(2,1)} %reshape.311), channel_id=1, source_target_pairs={{0,24},{8,0},{16,8},{24,16},{1,25},{9,1},{17,9},{25,17},{2,26},{10... | collective-permute-start | bytes 3538952 | tf_op jit(solution)/shard_map/ppermute | solution.py:918
  167.7 14.3 %collective-permute-done = bf16[8,72,1024]{2,1,0:T(8,128)(2,1)} collective-permute-done((bf16[8,72,1024]{2,1,0:T(8,128)(2,1)}, bf16[8,72,1024]{2,1,0:T(8,128)(2,1)}, u32[]{:S(2)}, u32[]{:S(2)}) %collective-permute-start) | collective-permute-done | bytes 1179680 | tf_op jit(solution)/shard_map/ppermute | solution.py:918
  183.4 26.3 %collective-permute-done.1 = bf16[8,72,1024]{2,1,0:T(8,128)(2,1)} collective-permute-done((bf16[8,72,1024]{2,1,0:T(8,128)(2,1)}, bf16[8,72,1024]{2,1,0:T(8,128)(2,1)}, u32[]{:S(2)}, u32[]{:S(2)}) %collective-permute-start.1) | collective-permute-done | bytes 1179680 | tf_op jit(solution)/shard_map/ppermute | solution.py:918
  283.0 24.1 %layer_forward.10 = (bf16[4,336,1024]{2,1,0:T(8,128)(2,1)}, bf16[4,336,3072]{2,1,0:T(8,128)(2,1)}, bf16[4,24,448,128]{3,2,1,0:T(8,128)(2,1)}, bf16[4,336,1024]{2...) custom-call(s32[4]{0:T(128)} %get-tuple-element.575.flags, ...), custom_call_target="tpu_custom_call", output_to_operand_aliasing={{0}: (13, {}), {1}: (14, {}), {2}: (15, {}), {3}: (16, {}),... | custom-call | flops 8455716864 | bytes 41943040 | tf_op jit(solution)/shard_map/layer_forward/pallas_call | solution.py:683
  309.8 24.6 %layer_forward.11 = (bf16[4,336,1024]{2,1,0:T(8,128)(2,1)}, bf16[4,336,3072]{2,1,0:T(8,128)(2,1)}, bf16[4,24,448,128]{3,2,1,0:T(8,128)(2,1)}, bf16[4,336,1024]{2...) custom-call(s32[4]{0:T(128)} %get-tuple-element.574.flags, ...), custom_call_target="tpu_custom_call", output_to_operand_aliasing={{0}: (13, {}), {1}: (14, {}), {2}: (15, {}), {3}: (16, {}),... | custom-call | flops 8455716864 | bytes 41943040 | tf_op jit(solution)/shard_map/layer_forward/pallas_call | solution.py:683
  337.9 24.2 %layer_forward.12 = (bf16[4,336,1024]{2,1,0:T(8,128)(2,1)}, bf16[4,336,3072]{2,1,0:T(8,128)(2,1)}, bf16[4,24,448,128]{3,2,1,0:T(8,128)(2,1)}, bf16[4,336,1024]{2...) custom-call(s32[4]{0:T(128)} %add_add_fusion.7.flags, ...), custom_call_target="tpu_custom_call", output_to_operand_aliasing={{0}: (13, {}), {1}: (14, {}), {2}: (15, {}), {3}: (16, {}),... | custom-call | flops 8455716864 | bytes 41943040 | tf_op jit(solution)/shard_map/layer_forward/pallas_call | solution.py:683
  365.5 24.3 %layer_forward.13 = (bf16[4,336,1024]{2,1,0:T(8,128)(2,1)}, bf16[4,336,3072]{2,1,0:T(8,128)(2,1)}, bf16[4,24,448,128]{3,2,1,0:T(8,128)(2,1)}, bf16[4,336,1024]{2...) custom-call(s32[4]{0:T(128)} %add_add_fusion.4.flags, ...), custom_call_target="tpu_custom_call", output_to_operand_aliasing={{0}: (13, {}), {1}: (14, {}), {2}: (15, {}), {3}: (16, {}),... | custom-call | flops 8455716864 | bytes 41943040 | tf_op jit(solution)/shard_map/layer_forward/pallas_call | solution.py:683
  394.8 15.0 %collective-permute-start.16 = (bf16[160,1024]{1,0:T(8,128)(2,1)}, bf16[160,1024]{1,0:T(8,128)(2,1)S(1)}, u32[]{:S(2)}, u32[]{:S(2)}) collective-permute-start(bf16[160,1024]{1,0:T(8,128)(2,1)} %get-tuple-element.333), channel_id=1, source_target_pairs={{0,8},{1,9},{2,10},{3,11},{8,17},{9,18},{10,19},{11,16},{16,24},{1... | collective-permute-start | bytes 983048 | tf_op jit(solution)/shard_map/ppermute | solution.py:830
  416.9 22.0 %collective-permute-start.14 = (bf16[160,1024]{1,0:T(8,128)(2,1)}, bf16[160,1024]{1,0:T(8,128)(2,1)S(1)}, u32[]{:S(2)}, u32[]{:S(2)}) collective-permute-start(bf16[160,1024]{1,0:T(8,128)(2,1)} %get-tuple-element.331), channel_id=1, source_target_pairs={{0,8},{1,9},{2,10},{3,11},{8,17},{9,18},{10,19},{11,16},{16,24},{1... | collective-permute-start | bytes 983048 | tf_op jit(solution)/shard_map/ppermute | solution.py:830
  447.1 11.7 %collective-permute-start.21 = (bf16[160,1024]{1,0:T(8,128)(2,1)}, bf16[160,1024]{1,0:T(8,128)(2,1)S(1)}, u32[]{:S(2)}, u32[]{:S(2)}) collective-permute-start(bf16[160,1024]{1,0:T(8,128)(2,1)} %get-tuple-element.360), channel_id=1, source_target_pairs={{0,11},{1,8},{2,9},{3,10},{8,16},{9,17},{10,18},{11,19},{16,27},{1... | collective-permute-start | bytes 983048 | tf_op jit(solution)/shard_map/ppermute | solution.py:831
  462.9 25.1 %collective-permute-start.19 = (bf16[160,1024]{1,0:T(8,128)(2,1)}, bf16[160,1024]{1,0:T(8,128)(2,1)S(1)}, u32[]{:S(2)}, u32[]{:S(2)}) collective-permute-start(bf16[160,1024]{1,0:T(8,128)(2,1)} %get-tuple-element.358), channel_id=1, source_target_pairs={{0,11},{1,8},{2,9},{3,10},{8,16},{9,17},{10,18},{11,19},{16,27},{1... | collective-permute-start | bytes 983048 | tf_op jit(solution)/shard_map/ppermute | solution.py:831
  522.2 15.4 %collective-permute-done.27.recv_b = bf16[160,1024]{1,0:T(8,128)(2,1)} collective-permute-done((bf16[160,1024]{1,0:T(8,128)(2,1)}, bf16[160,1024]{1,0:T(8,128)(2,1)}, u32[]{:S(2)}, u32[]{:S(2)}) %collective-permute-start.27) | collective-permute-done | bytes 327712 | tf_op jit(solution)/shard_map/ppermute | solution.py:831
  584.5 88.3 %collective-permute-done.34.recv_a = bf16[160,1024]{1,0:T(8,128)(2,1)S(1)} collective-permute-done((bf16[160,1024]{1,0:T(8,128)(2,1)}, bf16[160,1024]{1,0:T(8,128)(2,1)S(1)}, u32[]{:S(2)}, u32[]{:S(2)}) %collective-permute-start.34) | collective-permute-done | bytes 327712 | tf_op jit(solution)/shard_map/ppermute | solution.py:830
  681.6 33.4 %layer_backward.16 = (bf16[4,336,1024]{2,1,0:T(8,128)(2,1)}, bf16[4,336,3072]{2,1,0:T(8,128)(2,1)}, bf16[4,336,4096]{2,1,0:T(8,128)(2,1)}, bf16[4,336,1024]{2,1,...) custom-call(s32[4]{0:T(128)} %add_add_fusion.18.flags, ...), custom_call_target="tpu_custom_call", output_to_operand_aliasing={{0}: (12, {}), {1}: (13, {}), {2}: (14, {}), {3}: (15, {}),... | custom-call | flops 8455716864 | bytes 52428800 | tf_op jit(solution)/shard_map/layer_backward/pallas_call | solution.py:730
  719.0 32.7 %layer_backward.17 = (bf16[4,336,1024]{2,1,0:T(8,128)(2,1)}, bf16[4,336,3072]{2,1,0:T(8,128)(2,1)}, bf16[4,336,4096]{2,1,0:T(8,128)(2,1)}, bf16[4,336,1024]{2,1,...) custom-call(s32[4]{0:T(128)} %add_add_fusion.12.flags, ...), custom_call_target="tpu_custom_call", output_to_operand_aliasing={{0}: (12, {}), {1}: (13, {}), {2}: (14, {}), {3}: (15, {}),... | custom-call | flops 8455716864 | bytes 52428800 | tf_op jit(solution)/shard_map/layer_backward/pallas_call | solution.py:730
  757.0 33.1 %layer_backward.18 = (bf16[4,336,1024]{2,1,0:T(8,128)(2,1)}, bf16[4,336,3072]{2,1,0:T(8,128)(2,1)}, bf16[4,336,4096]{2,1,0:T(8,128)(2,1)}, bf16[4,336,1024]{2,1,...) custom-call(s32[4]{0:T(128)} %add_add_fusion.19.flags, ...), custom_call_target="tpu_custom_call", output_to_operand_aliasing={{0}: (12, {}), {1}: (13, {}), {2}: (14, {}), {3}: (15, {}),... | custom-call | flops 8455716864 | bytes 52428800 | tf_op jit(solution)/shard_map/layer_backward/pallas_call | solution.py:730
  794.4 33.1 %layer_backward.19 = (bf16[4,336,1024]{2,1,0:T(8,128)(2,1)}, bf16[4,336,3072]{2,1,0:T(8,128)(2,1)}, bf16[4,336,4096]{2,1,0:T(8,128)(2,1)}, bf16[4,336,1024]{2,1,...) custom-call(s32[4]{0:T(128)} %add_add_fusion.11.flags, ...), custom_call_target="tpu_custom_call", output_to_operand_aliasing={{0}: (12, {}), {1}: (13, {}), {2}: (14, {}), {3}: (15, {}),... | custom-call | flops 8455716864 | bytes 52428800 | tf_op jit(solution)/shard_map/layer_backward/pallas_call | solution.py:730
  894.2 11.5 %convolution_convert_fusion = bf16[4096,512]{1,0:T(8,128)(2,1)} fusion(bf16[1344,4096]{1,0:T(8,128)(2,1)} %bitcast.298, bf16[1344,1024]{1,0:T(8,128)(2,1)} %bitcast.302, s32[]{:T(128)S(6)} %select_n.186), kind=kOutput, calls=%fused_computation.3 | convolution fusion | flops 5639241728 | bytes 16580612 | tf_op jit(solution)/shard_map/dot_general | solution.py:105
  913.2 11.9 %add_convert_fusion = bf16[4096,512]{1,0:T(8,128)(2,1)} fusion(bf16[4096,512]{1,0:T(8,128)(2,1)} %collective-permute-done.58, bf16[1344,4096]{1,0:T(8,128)(2,1)} %bitcast.299, bf16[1344,1024]{1,0:T(8,128)(2,1)} %bitcast.303, s32[]{:T(128)S(6)} %select_n.185), kind=kOutput, calls=%fused_computation | convolution fusion | flops 5643436032 | bytes 20774916 | tf_op jit(solution)/shard_map/dot_general | solution.py:105
  1037.7 11.9 %collective-permute-done.45 = bf16[1,4,64,1024]{3,2,1,0:T(8,128)(2,1)} collective-permute-done((bf16[1,4,64,1024]{3,2,1,0:T(8,128)(2,1)S(1)}, bf16[1,4,64,1024]{3,2,1,0:T(8,128)(2,1)}, u32[]{:S(2)}, u32[]{:S(2)}) %collective-permute-start.45) | collective-permute-done | bytes 524320 | tf_op jit(solution)/shard_map/ppermute | solution.py:842
  1063.4 16.4 %collective-permute-done.48 = bf16[1,64,1024]{2,1,0:T(8,128)(2,1)S(1)} collective-permute-done((bf16[1,64,1024]{2,1,0:T(8,128)(2,1)S(1)}, bf16[1,64,1024]{2,1,0:T(8,128)(2,1)S(1)}, u32[]{:S(2)}, u32[]{:S(2)}) %collective-permute-start.48) | collective-permute-done | bytes 131104 | tf_op jit(solution)/shard_map/ppermute | solution.py:842
  1089.7 23.7 %reduce-scatter.11.cloned.1.call-done = bf16[1024,512]{1,0:T(8,128)(2,1)} async-done(((bf16[4096,512]{1,0:T(8,128)(2,1)}), bf16[1024,512]{1,0:T(8,128)(2,1)}) %reduce-scatter.11.cloned.1.call-update) | async-done | bytes 1048592 | tf_op jit(solution)/shard_map/reduce_scatter | solution.py:1094
  (442 shorter events, 468.1 us)
Async XLA Ops:
  7.2 113.5 %all-gather.5.cloned.1.call-start = ((), (), s32[]{:S(2)}) async-start(), calls=%async_computation.8 | async-start | bytes 13123584 | tf_op jit(solution)/shard_map/all_gather | solution.py:895
  11.8 271.3 %all-gather.7.cloned.1.call-start = ((), (), s32[]{:S(2)}) async-start(), calls=%async_computation.9 | async-start | bytes 16515072 | tf_op jit(solution)/shard_map/all_gather | solution.py:896
  15.5 1042.9 %reduce-scatter.7.cloned.1.call-start = ((), (), s32[]{:S(2)}) async-start(), calls=%async_computation.5 | async-start | bytes 1310720 | tf_op jit(solution)/shard_map/reduce_scatter | solution.py:1094
  20.0 249.7 %collective-permute-start.23 = (bf16[4,160,1024]{2,1,0:T(8,128)(2,1)}, bf16[4,160,1024]{2,1,0:T(8,128)(2,1)}, u32[]{:S(2)}, u32[]{:S(2)}) collective-permute-start(bf16[4,160,1024]{2,1,0:T(8,128)(2,1)} %get-tuple-element.553), channel_id=1, source_target_pairs={{8,11},{9,8},{10,9},{11,10},{24,27},{25,24},{26,25},{27,26},{12,15... | collective-permute-start | bytes 3932168 | tf_op jit(solution)/shard_map/ppermute | solution.py:980
  126.1 55.9 %collective-permute-start = (bf16[8,72,1024]{2,1,0:T(8,128)(2,1)}, bf16[8,72,1024]{2,1,0:T(8,128)(2,1)}, u32[]{:S(2)}, u32[]{:S(2)}) collective-permute-start(bf16[8,72,1024]{2,1,0:T(8,128)(2,1)} %reshape.311), channel_id=1, source_target_pairs={{0,24},{8,0},{16,8},{24,16},{1,25},{9,1},{17,9},{25,17},{2,26},{10... | collective-permute-start | bytes 3538952 | tf_op jit(solution)/shard_map/ppermute | solution.py:918
  157.1 52.6 %collective-permute-start.1 = (bf16[8,72,1024]{2,1,0:T(8,128)(2,1)}, bf16[8,72,1024]{2,1,0:T(8,128)(2,1)}, u32[]{:S(2)}, u32[]{:S(2)}) collective-permute-start(bf16[8,72,1024]{2,1,0:T(8,128)(2,1)} %reshape.311), channel_id=1, source_target_pairs={{0,16},{8,24},{16,0},{24,8},{1,17},{9,25},{17,1},{25,9},{2,18},{10... | collective-permute-start | bytes 3538952 | tf_op jit(solution)/shard_map/ppermute | solution.py:918
  158.0 53.1 %collective-permute-start.2 = (bf16[8,72,1024]{2,1,0:T(8,128)(2,1)}, bf16[8,72,1024]{2,1,0:T(8,128)(2,1)}, u32[]{:S(2)}, u32[]{:S(2)}) collective-permute-start(bf16[8,72,1024]{2,1,0:T(8,128)(2,1)} %reshape.311), channel_id=1, source_target_pairs={{0,8},{8,16},{16,24},{24,0},{1,9},{9,17},{17,25},{25,1},{2,10},{10... | collective-permute-start | bytes 3538952 | tf_op jit(solution)/shard_map/ppermute | solution.py:918
  228.6 46.2 %collective-permute-start.3 = (bf16[1,2,160,1024]{3,2,1,0:T(8,128)(2,1)S(1)}, bf16[1,2,160,1024]{3,2,1,0:T(8,128)(2,1)}, u32[]{:S(2)}, u32[]{:S(2)}) collective-permute-start(bf16[1,2,160,1024]{3,2,1,0:T(8,128)(2,1)S(1)} %pad.30), channel_id=1, source_target_pairs={{8,0},{9,1},{10,2},{11,3},{12,4},{13,5},{14,6},{15,7}} | collective-permute-start | bytes 1966088 | tf_op jit(solution)/shard_map/ppermute | solution.py:976
  230.1 44.7 %collective-permute-start.4 = (bf16[1,2,160,1024]{3,2,1,0:T(8,128)(2,1)S(1)}, bf16[1,2,160,1024]{3,2,1,0:T(8,128)(2,1)}, u32[]{:S(2)}, u32[]{:S(2)}) collective-permute-start(bf16[1,2,160,1024]{3,2,1,0:T(8,128)(2,1)S(1)} %pad.30), channel_id=1, source_target_pairs={{16,0},{17,1},{18,2},{19,3},{20,4},{21,5},{22,6},{23,7}} | collective-permute-start | bytes 1966088 | tf_op jit(solution)/shard_map/ppermute | solution.py:976
  231.4 43.4 %collective-permute-start.5 = (bf16[1,2,160,1024]{3,2,1,0:T(8,128)(2,1)S(1)}, bf16[1,2,160,1024]{3,2,1,0:T(8,128)(2,1)}, u32[]{:S(2)}, u32[]{:S(2)}) collective-permute-start(bf16[1,2,160,1024]{3,2,1,0:T(8,128)(2,1)S(1)} %pad.30), channel_id=1, source_target_pairs={{24,0},{25,1},{26,2},{27,3},{28,4},{29,5},{30,6},{31,7}} | collective-permute-start | bytes 1966088 | tf_op jit(solution)/shard_map/ppermute | solution.py:976
  394.8 48.5 %collective-permute-start.16 = (bf16[160,1024]{1,0:T(8,128)(2,1)}, bf16[160,1024]{1,0:T(8,128)(2,1)S(1)}, u32[]{:S(2)}, u32[]{:S(2)}) collective-permute-start(bf16[160,1024]{1,0:T(8,128)(2,1)} %get-tuple-element.333), channel_id=1, source_target_pairs={{0,8},{1,9},{2,10},{3,11},{8,17},{9,18},{10,19},{11,16},{16,24},{1... | collective-permute-start | bytes 983048 | tf_op jit(solution)/shard_map/ppermute | solution.py:830
  416.9 41.9 %collective-permute-start.14 = (bf16[160,1024]{1,0:T(8,128)(2,1)}, bf16[160,1024]{1,0:T(8,128)(2,1)S(1)}, u32[]{:S(2)}, u32[]{:S(2)}) collective-permute-start(bf16[160,1024]{1,0:T(8,128)(2,1)} %get-tuple-element.331), channel_id=1, source_target_pairs={{0,8},{1,9},{2,10},{3,11},{8,17},{9,18},{10,19},{11,16},{16,24},{1... | collective-permute-start | bytes 983048 | tf_op jit(solution)/shard_map/ppermute | solution.py:830
  445.7 42.3 %collective-permute-start.20 = (bf16[160,1024]{1,0:T(8,128)(2,1)}, bf16[160,1024]{1,0:T(8,128)(2,1)S(1)}, u32[]{:S(2)}, u32[]{:S(2)}) collective-permute-start(bf16[160,1024]{1,0:T(8,128)(2,1)} %get-tuple-element.359), channel_id=1, source_target_pairs={{0,8},{1,9},{2,10},{3,11},{8,17},{9,18},{10,19},{11,16},{16,24},{1... | collective-permute-start | bytes 983048 | tf_op jit(solution)/shard_map/ppermute | solution.py:830
  447.1 41.0 %collective-permute-start.21 = (bf16[160,1024]{1,0:T(8,128)(2,1)}, bf16[160,1024]{1,0:T(8,128)(2,1)S(1)}, u32[]{:S(2)}, u32[]{:S(2)}) collective-permute-start(bf16[160,1024]{1,0:T(8,128)(2,1)} %get-tuple-element.360), channel_id=1, source_target_pairs={{0,11},{1,8},{2,9},{3,10},{8,16},{9,17},{10,18},{11,19},{16,27},{1... | collective-permute-start | bytes 983048 | tf_op jit(solution)/shard_map/ppermute | solution.py:831
  508.9 41.1 %collective-permute-start.24 = (bf16[160,1024]{1,0:T(8,128)(2,1)}, bf16[160,1024]{1,0:T(8,128)(2,1)}, u32[]{:S(2)}, u32[]{:S(2)}) collective-permute-start(bf16[160,1024]{1,0:T(8,128)(2,1)} %get-tuple-element.403), channel_id=1, source_target_pairs={{8,1},{9,2},{10,3},{11,0},{16,8},{17,9},{18,10},{19,11},{24,17},{2... | collective-permute-start | bytes 983048 | tf_op jit(solution)/shard_map/ppermute | solution.py:830
  511.6 65.7 %collective-permute-start.22 = (bf16[4,160,1024]{2,1,0:T(8,128)(2,1)S(1)}, bf16[4,160,1024]{2,1,0:T(8,128)(2,1)S(1)}, u32[]{:S(2)}, u32[]{:S(2)}) collective-permute-start(bf16[4,160,1024]{2,1,0:T(8,128)(2,1)S(1)} %slice_bitcast_fusion), channel_id=1, source_target_pairs={{8,9},{9,10},{10,11},{11,8},{24,25},{25,26},{26,27},{27,24},{12,13... | collective-permute-start | bytes 3932168 | tf_op jit(solution)/shard_map/ppermute | solution.py:1038
  574.7 98.0 %collective-permute-start.34 = (bf16[160,1024]{1,0:T(8,128)(2,1)}, bf16[160,1024]{1,0:T(8,128)(2,1)S(1)}, u32[]{:S(2)}, u32[]{:S(2)}) collective-permute-start(bf16[160,1024]{1,0:T(8,128)(2,1)} %get-tuple-element.441), channel_id=1, source_target_pairs={{8,1},{9,2},{10,3},{11,0},{16,8},{17,9},{18,10},{19,11},{24,17},{2... | collective-permute-start | bytes 983048 | tf_op jit(solution)/shard_map/ppermute | solution.py:830
  576.0 104.8 %collective-permute-start.35 = (bf16[160,1024]{1,0:T(8,128)(2,1)}, bf16[160,1024]{1,0:T(8,128)(2,1)S(1)}, u32[]{:S(2)}, u32[]{:S(2)}) collective-permute-start(bf16[160,1024]{1,0:T(8,128)(2,1)} %get-tuple-element.442), channel_id=1, source_target_pairs={{8,0},{9,1},{10,2},{11,3},{16,11},{17,8},{18,9},{19,10},{24,16},{2... | collective-permute-start | bytes 983048 | tf_op jit(solution)/shard_map/ppermute | solution.py:831
  581.9 135.7 %collective-permute-start.32 = (bf16[160,1024]{1,0:T(8,128)(2,1)}, bf16[160,1024]{1,0:T(8,128)(2,1)S(1)}, u32[]{:S(2)}, u32[]{:S(2)}) collective-permute-start(bf16[160,1024]{1,0:T(8,128)(2,1)} %get-tuple-element.439), channel_id=1, source_target_pairs={{8,1},{9,2},{10,3},{11,0},{16,8},{17,9},{18,10},{19,11},{24,17},{2... | collective-permute-start | bytes 983048 | tf_op jit(solution)/shard_map/ppermute | solution.py:830
  583.2 135.1 %collective-permute-start.33 = (bf16[160,1024]{1,0:T(8,128)(2,1)}, bf16[160,1024]{1,0:T(8,128)(2,1)S(1)}, u32[]{:S(2)}, u32[]{:S(2)}) collective-permute-start(bf16[160,1024]{1,0:T(8,128)(2,1)} %get-tuple-element.440), channel_id=1, source_target_pairs={{8,0},{9,1},{10,2},{11,3},{16,11},{17,8},{18,9},{19,10},{24,16},{2... | collective-permute-start | bytes 983048 | tf_op jit(solution)/shard_map/ppermute | solution.py:831
  851.4 232.0 %reduce-scatter.5.cloned.1.call-start = ((), (), s32[]{:S(2)}) async-start(), calls=%async_computation.4 | async-start | bytes 3932160 | tf_op jit(solution)/shard_map/reduce_scatter | solution.py:1094
  867.7 218.6 %reduce-scatter.9.cloned.1.call-start = ((), (), s32[]{:S(2)}) async-start(), calls=%async_computation.6 | async-start | bytes 5242880 | tf_op jit(solution)/shard_map/reduce_scatter | solution.py:1094
  893.9 219.6 %reduce-scatter.11.cloned.1.call-start = ((), (), s32[]{:S(2)}) async-start(), calls=%async_computation.7 | async-start | bytes 5242880 | tf_op jit(solution)/shard_map/reduce_scatter | solution.py:1094
  932.7 42.3 %collective-permute-start.40 = (bf16[1,2,160,1024]{3,2,1,0:T(8,128)(2,1)}, bf16[1,2,160,1024]{3,2,1,0:T(8,128)(2,1)}, u32[]{:S(2)}, u32[]{:S(2)}) collective-permute-start(bf16[1,2,160,1024]{3,2,1,0:T(8,128)(2,1)} %get-tuple-element.551), channel_id=1, source_target_pairs={{0,24},{1,25},{2,26},{3,27},{4,28},{5,29},{6,30},{7,31}} | collective-permute-start | bytes 1966088 | tf_op jit(solution)/shard_map/ppermute | solution.py:1111
  (113 other events, 1718.4 us)
Sparse Core Ops, SparseCore 0:
  11.9 108.8 all-gather.4
  122.9 160.0 all-gather.6
  851.5 22.9 reduce-scatter.6
  876.8 60.4 reduce-scatter.4
  939.6 79.8 reduce-scatter.8
  1021.6 91.7 reduce-scatter.10

commit v4 on v3

--- a/solution.py
+++ b/solution.py
@@ -27,6 +27,7 @@
 PER = 128 // HEAD
 GROUPS = D // 128
 STACK = PER * PAD
+QKV_AT, PROJ_AT, FC1_AT, FC2_AT, BLOCK_ROWS = 0, 768, 1024, 2048, 3072
 OWN = 2
 BLOCKS = 4
 DB = D // OWN
@@ -136,12 +137,47 @@
     return (group // 2) * (3 * TB) + (group % 2) * 128
 
 
-def weight_views(w_tall, w_wide, v_qkv, v_fc1, v_fc2, block):
-    return (
-        (w_wide.at[:, block, :, pl.ds(0, 3 * TB)], v_qkv.at[:, block]),
-        (w_wide.at[:, block, :, pl.ds(3 * TB, FB)], v_fc1.at[:, block]),
-        (w_tall.at[:, block, pl.ds(0, FB)], v_fc2.at[:, block]),
-    )
+class Copies:
+    def __init__(self, copies):
+        self.copies = copies
+
+    def start(self):
+        for copy in self.copies:
+            copy.start()
+
+    def wait(self):
+        for copy in self.copies:
+            copy.wait()
+
+
+def weight_copies(w_all, targets, sems, block):
+    v_qkv, v_proj, v_fc1, v_fc2 = targets
+    half = DB // 2
+    moves = {
+        "qkv": (
+            (v_qkv, (0, DB), (0, DB), 0, 0),
+            (v_qkv, (0, half), (DB, half), QKV_AT + DB, 0),
+            (v_qkv, (half, half), (DB, half), QKV_AT + DB, half),
+        ),
+        "proj": ((v_proj, (0, TB), (0, DB), PROJ_AT, 0),),
+        "fc1": ((v_fc1, (0, DB), (0, DB), FC1_AT, 0), (v_fc1, (0, DB), (DB, DB), FC1_AT + DB, 0)),
+        "fc2": ((v_fc2, (0, FB), (0, DB), FC2_AT, 0),),
+    }
+    starts = {"qkv": 0, "proj": 3, "fc1": 4, "fc2": 6}
+
+    def copies(kind):
+        result = []
+        for index, (target, rows, columns, row, column) in enumerate(moves[kind]):
+            result.append(
+                pltpu.make_async_copy(
+                    w_all.at[:, block, pl.ds(row, rows[1]), pl.ds(column, columns[1])],
+                    target.at[:, block, pl.ds(*rows), pl.ds(*columns)],
+                    sems.at[(starts[kind] + index) * BLOCKS + block],
+                )
+            )
+        return Copies(result)
+
+    return copies
 
 
 def lanes(start, size):
@@ -160,8 +196,7 @@
     bias_qkv,
     bias_fc1,
     bias_pos,
-    w_tall,
-    w_wide,
+    w_all,
     *refs,
 ):
     (x_all, qkv_all, probs_all, mixed_all, mid_all, rattn_all, rmlp_all, act_all, slope_all) = refs[11:20]
@@ -200,17 +235,18 @@
 
     @pl.when(valid == 1)
     def _():
+        targets = (v_qkv, v_proj, v_fc1, v_fc2)
+
         def w_copy(kind, block):
-            source, target = weight_views(w_tall, w_wide, v_qkv, v_fc1, v_fc2, block)[kind]
-            return pltpu.make_async_copy(source, target, sem_w.at[kind * BLOCKS + block])
+            return weight_copies(w_all, targets, sem_w, block)(("qkv", "fc1", "fc2")[kind])
 
         def proj_copy():
-            return pltpu.make_async_copy(
-                w_tall.at[:, :, pl.ds(FB, TB)], v_proj, sem_w.at[3 * BLOCKS]
+            return Copies(
+                [weight_copies(w_all, targets, sem_w, block)("proj").copies[0] for block in range(BLOCKS)]
             )
 
         def pos_copy():
-            return pltpu.make_async_copy(bias_pos, v_pos, sem_w.at[3 * BLOCKS + 1])
+            return pltpu.make_async_copy(bias_pos, v_pos, sem_w.at[7 * BLOCKS])
 
         @pl.when(is_first == 1)
         def _():
@@ -255,8 +291,7 @@
         def qkv_block(block, state):
             w_copy(0, block).wait()
             w_copy(1, block).start()
-            out = dot_nn(rattn[:, :DB], v_qkv[0, block])
-            out = out + dot_nn(rattn[:, DB:], v_qkv[1, block])
+            out = dot_nn(rattn[...], v_qkv[:, block].reshape(D, 3 * TB))
             columns = lanes(block * 3 * TB, 3 * TB)
             qkv[pl.ds(0, ROWS), columns] = (out + bias_qkv[:, columns]).astype(BF16)
             return state
@@ -301,10 +336,8 @@
         proj_copy().wait()
         for own in range(OWN):
             columns = slice(own * DB, (own + 1) * DB)
-            out = xf[:, columns] + vecs[4:5, columns]
-            for block in range(BLOCKS):
-                out = out + dot_nn(mixed[:, block * TB : (block + 1) * TB], v_proj[own, block])
-            mid[:, columns] = out
+            out = dot_nn(mixed[...], v_proj[own].reshape(D, DB))
+            mid[:, columns] = xf[:, columns] + vecs[4:5, columns] + out
         saves.append(pltpu.make_async_copy(mid, mid_all.at[slot], sem_out.at[5]))
         saves[-1].start()
 
@@ -330,7 +363,7 @@
         def hidden_block(block, state):
             w_copy(1, block).wait()
             columns = lanes(block * FB, FB)
-            pre = dot_nn(rmlp[:, :DB], v_fc1[0, block]) + dot_nn(rmlp[:, DB:], v_fc1[1, block])
+            pre = dot_nn(rmlp[...], v_fc1[:, block].reshape(D, FB))
             pre = pre + bias_fc1[:, columns]
             chance = 0.5 + 0.5 * lax.erf(pre * np.float32(0.5**0.5))
             slope[:, columns] = (
@@ -339,22 +372,28 @@
             act[:, columns] = (pre * chance).astype(BF16)
             for save in hidden_saves(block):
                 save.start()
+            return state
+
+        lax.fori_loop(0, BLOCKS, hidden_block, None)
+        for block in range(BLOCKS):
             w_copy(2, block).wait()
-            for own in range(OWN):
-                half = slice(own * DB, (own + 1) * DB)
-                total[:, half] += dot_nn(act[:, columns], v_fc2[own, block])
+        for own in range(OWN):
+            half = slice(own * DB, (own + 1) * DB)
+            total[:, half] += dot_nn(act[...], v_fc2[own].reshape(FF, DB))
+
+        def finish(rows, state):
+            hat, _ = norm_stats(total[rows, :])
+            outb[rows, :] = (hat * vecs[6:7, :] + vecs[7:8, :]).astype(BF16)
             return state
 
-        lax.fori_loop(0, BLOCKS, hidden_block, None)
-
-        def finish(rows, state):
-            values = total[rows, :]
-            hat, _ = norm_stats(values)
-            shown = jnp.where(is_last == 1, hat * vecs[6:7, :] + vecs[7:8, :], values)
-            outb[rows, :] = shown.astype(BF16)
-            return state
-
-        row_chunks(finish)
+        @pl.when(is_last == 1)
+        def _():
+            row_chunks(finish)
+
+        @pl.when(is_last == 0)
+        def _():
+            outb[...] = total[...].astype(BF16)
+
         save_out = pltpu.make_async_copy(total, out_all.at[slot], sem_out.at[9])
 
         @pl.when(is_last == 1)
@@ -388,11 +427,11 @@
     recv_a,
     recv_b,
     cots,
+    cots_next,
     perm_in,
     perm_out,
     vecs,
-    w_tall,
-    w_wide,
+    w_all,
     probs_all,
     mid_all,
     out_all,
@@ -433,13 +472,14 @@
 
     @pl.when(valid == 1)
     def _():
+        targets = (v_qkv, v_proj, v_fc1, v_fc2)
+
         def w_copy(kind, block):
-            source, target = weight_views(w_tall, w_wide, v_qkv, v_fc1, v_fc2, block)[2 - kind]
-            return pltpu.make_async_copy(source, target, sem_w.at[kind * BLOCKS + block])
+            return weight_copies(w_all, targets, sem_w, block)(("fc2", "fc1", "qkv")[kind])
 
         def proj_copy():
-            return pltpu.make_async_copy(
-                w_tall.at[:, :, pl.ds(FB, TB)], v_proj, sem_w.at[3 * BLOCKS]
+            return Copies(
+                [weight_copies(w_all, targets, sem_w, block)("proj").copies[0] for block in range(BLOCKS)]
             )
 
         def load(index):
@@ -458,8 +498,20 @@
             )[index]
             return pltpu.make_async_copy(source, target, sem_in.at[index])
 
-        for index in range(4):
-            load(index).start()
+        @pl.when(flags[4] == 0)
+        def _():
+            load(0).start()
+            load(1).start()
+
+        @pl.when(flags[4] == 1)
+        def _():
+            for half, source in enumerate((cots.at[slot, 1], cots_next.at[slot])):
+                pltpu.make_async_copy(
+                    source, rcot.at[pl.ds(half * HALF, HALF)], sem_in.at[half]
+                ).start()
+
+        load(2).start()
+        load(3).start()
 
         @pl.when(is_last == 1)
         def _():
@@ -677,7 +729,7 @@
 
 
 def layer_forward(flags, recv_a, recv_b, firsts, tables, weights, stacks):
-    inputs = (flags, recv_a, recv_b, firsts) + tuple(tables) + tuple(weights) + tuple(stacks)
+    inputs = (flags, recv_a, recv_b, firsts) + tuple(tables) + (weights,) + tuple(stacks)
     first_stack = len(inputs) - len(stacks)
     wide = lambda dtype: pltpu.VMEM((ROWS, D), dtype)
     results = pl.pallas_call(
@@ -686,7 +738,7 @@
         in_specs=[pl.BlockSpec(memory_space=pltpu.SMEM)]
         + any_specs(3)
         + vmem_specs(6)
-        + any_specs(3 + len(stacks)),
+        + any_specs(2 + len(stacks)),
         out_specs=any_specs(len(stacks) + 2),
         scratch_shapes=WEIGHT_SCRATCH
         + [
@@ -706,7 +758,7 @@
             wide(F32),
             wide(BF16),
             pltpu.VMEM((2 * HALF, D), BF16),
-            pltpu.SemaphoreType.DMA((3 * BLOCKS + 2,)),
+            pltpu.SemaphoreType.DMA((7 * BLOCKS + 1,)),
             pltpu.SemaphoreType.DMA((2,)),
             pltpu.SemaphoreType.DMA((14,)),
             pltpu.SemaphoreType.DMA((2 * BLOCKS,)),
@@ -721,9 +773,13 @@
     return results[-2:], tuple(results[:-2])
 
 
-def layer_backward(flags, recv_a, recv_b, cots, tables, weights, saved, stacks):
+def layer_backward(flags, recv_a, recv_b, cots, cots_next, tables, weights, saved, stacks):
     inputs = (
-        (flags, recv_a, recv_b, cots) + tuple(tables) + tuple(weights) + tuple(saved) + tuple(stacks)
+        (flags, recv_a, recv_b, cots, cots_next)
+        + tuple(tables)
+        + (weights,)
+        + tuple(saved)
+        + tuple(stacks)
     )
     first_stack = len(inputs) - len(stacks)
     wide = lambda dtype: pltpu.VMEM((ROWS, D), dtype)
@@ -731,9 +787,9 @@
         backward_kernel,
         out_shape=shapes_of(stacks) + [jax.ShapeDtypeStruct((HALF, D), BF16)] * 2,
         in_specs=[pl.BlockSpec(memory_space=pltpu.SMEM)]
-        + any_specs(3)
+        + any_specs(4)
         + vmem_specs(3)
-        + any_specs(2 + len(saved) + len(stacks)),
+        + any_specs(1 + len(saved) + len(stacks)),
         out_specs=any_specs(len(stacks) + 2),
         scratch_shapes=WEIGHT_SCRATCH
         + [
@@ -754,7 +810,7 @@
             pltpu.VMEM((GROUPS, STACK, KEYS), F32),
             pltpu.VMEM((SUMS, D), F32),
             pltpu.VMEM((2 * HALF, D), BF16),
-            pltpu.SemaphoreType.DMA((3 * BLOCKS + 1,)),
+            pltpu.SemaphoreType.DMA((7 * BLOCKS,)),
             pltpu.SemaphoreType.DMA((11,)),
             pltpu.SemaphoreType.DMA((10,)),
             pltpu.SemaphoreType.DMA((BLOCKS,)),
@@ -880,54 +936,98 @@
         rows = halves[..., :LINES, :]
         return rows.reshape(rows.shape[:-3] + (UNIT, D))
 
+    def stacks_of(*kinds, after=()):
+        return pl.pallas_call(
+            lambda *refs: None,
+            out_shape=[jax.ShapeDtypeStruct(shape, dtype) for shape, dtype in kinds],
+            in_specs=any_specs(len(after)),
+            out_specs=any_specs(len(kinds)),
+        )(*after)
+
+    lined = (dp_count, tensor_count) == (OWN, BLOCKS)
+
+    def block_rows(qkv, proj, fc1, fc2):
+        half = DB // 2
+        tail = (qkv[..., :half, DB:], qkv[..., half:, DB:])
+        rows = (qkv[..., :DB], jnp.concatenate(tail, -1), proj, fc1[..., :DB], fc1[..., DB:], fc2)
+        return jnp.concatenate(rows, -2)
+
+    shards = [
+        weight.astype(BF16)
+        for weight in (w_qkv[0].reshape(own_width, -1), w_proj[0], w_fc1[0], w_fc2[0])
+    ]
+    if lined:
+        weights = lax.all_gather(block_rows(*shards), group_axes, axis=0)
+        weights = weights.reshape(OWN, BLOCKS, BLOCK_ROWS, DB)
+    else:
+        split = (dp_count, tensor_count)
+        qkv_full, proj_full, fc1_full, fc2_full = [
+            lax.all_gather(shard, group_axes, axis=0).reshape(split + shard.shape)
+            for shard in shards
+        ]
+        qkv_full = qkv_full.reshape(split + (own_width, 3, -1)).transpose(0, 2, 3, 1, 4)
+        qkv_full = qkv_full.reshape(OWN, DB, 3, BLOCKS, TB).transpose(0, 3, 1, 2, 4)
+        qkv_full = qkv_full.reshape(OWN, BLOCKS, DB, 3 * TB)
+        fc1_full = fc1_full.transpose(0, 2, 1, 3).reshape(OWN, DB, BLOCKS, FB)
+        fc1_full = fc1_full.transpose(0, 2, 1, 3)
+        proj_full, fc2_full = [
+            full.transpose(1, 2, 0, 3).reshape(BLOCKS, -1, OWN, DB).transpose(2, 0, 1, 3)
+            for full in (proj_full, fc2_full)
+        ]
+        weights = block_rows(qkv_full, proj_full, fc1_full, fc2_full)
+
     share = w_merge.shape[0]
     fshare = final_gain.shape[0]
     small = jnp.concatenate((merge_gain, merge_bias, final_gain, final_bias))
     small = jnp.pad(small, (0, 8 * D - small.shape[0])).reshape(8, D)
     packed = jnp.concatenate((w_merge, small)).astype(BF16)
-    tall_rows = (w_fc2.shape[1], w_proj.shape[1], packed.size // own_width)
-    tall = jnp.concatenate(
-        (w_fc2[0].astype(BF16), w_proj[0].astype(BF16), packed.reshape(-1, own_width))
-    )
-    wide = jnp.concatenate(
-        (w_qkv[0].astype(BF16).reshape(own_width, -1), w_fc1[0].astype(BF16)), 1
-    )
-    tall = lax.all_gather(tall, group_axes, axis=0)
-    wide = lax.all_gather(wide, group_axes, axis=0)
-    packed = tall[:, tall_rows[0] + tall_rows[1] :].reshape((-1,) + packed.shape)
-    tall = tall.reshape((dp_count, tensor_count) + tall.shape[1:])
-    wide = wide.reshape((dp_count, tensor_count) + wide.shape[1:])
-    if (dp_count, tensor_count) != (OWN, BLOCKS):
-        fc2_full = tall[:, :, : tall_rows[0]].transpose(1, 2, 0, 3)
-        fc2_full = fc2_full.reshape(BLOCKS, FB, OWN, DB).transpose(2, 0, 1, 3)
-        proj_full = tall[:, :, tall_rows[0] : tall_rows[0] + tall_rows[1]].transpose(1, 2, 0, 3)
-        proj_full = proj_full.reshape(BLOCKS, TB, OWN, DB).transpose(2, 0, 1, 3)
-        tall = jnp.concatenate((fc2_full, proj_full), 2)
-        qkv_width = 3 * D // tensor_count
-        qkv_full = wide[..., :qkv_width].reshape(dp_count, tensor_count, own_width, 3, -1)
-        qkv_full = qkv_full.transpose(0, 2, 3, 1, 4).reshape(OWN, DB, 3, BLOCKS, TB)
-        qkv_full = qkv_full.transpose(0, 3, 1, 2, 4).reshape(OWN, BLOCKS, DB, 3 * TB)
-        fc1_full = wide[..., qkv_width:].transpose(0, 2, 1, 3)
-        fc1_full = fc1_full.reshape(OWN, DB, BLOCKS, FB).transpose(0, 2, 1, 3)
-        wide = jnp.concatenate((qkv_full, fc1_full), 3)
-    weights = (tall, wide)
-
-    parts = [packed]
-    for step in range(1, section_count):
-        pairs = [(source, (source + step) % section_count) for source in range(section_count)]
-        parts.append(lax.ppermute(packed, "pipe", pairs))
-    parts = parts[::-1]
-    packed = lax.dynamic_slice_in_dim(
-        jnp.concatenate(parts + parts[:-1]),
-        (section_count - 1 - section_now) * packed.shape[0],
-        section_count * packed.shape[0],
-    )
+
+    def passed_round(block, axis):
+        count = lax.axis_size(axis)
+        index = lax.axis_index(axis)
+        parts = [block]
+        for step in range(1, count):
+            pairs = [(source, (source + step) % count) for source in range(count)]
+            parts.append(lax.ppermute(block, axis, pairs))
+        parts = parts[::-1]
+        return lax.dynamic_slice_in_dim(jnp.stack(parts + parts[:-1]), count - 1 - index, count)
+
+    packed_shape = packed.shape
+    packed = passed_round(passed_round(packed, "tensor"), "dp")
+    packed = packed.reshape((-1,) + packed_shape)
+
+    packed = passed_round(packed, "pipe").reshape((-1,) + packed_shape)
     merge_weight = packed[:, :share].reshape(merge_in, D)
     small_all = packed[:, share]
     merge_scale = small_all[:, :share].reshape(-1).astype(F32)
     merge_shift = small_all[:, share : 2 * share].reshape(-1).astype(F32)
     final_scale = small_all[:, 2 * share : 2 * share + fshare].reshape(-1).astype(F32)
     final_shift = small_all[:, 2 * share + fshare : 2 * (share + fshare)].reshape(-1).astype(F32)
+
+    mask_all = np.zeros((WIN_ROWS, WIN_COLS, PAD, KEYS), np.float32)
+    mask_all[:, :, : WIN * WIN, : WIN * WIN] = shift_mask(
+        WIN * WIN_ROWS, GRID_W, WIN, SHIFT
+    ).reshape(WIN_ROWS, WIN_COLS, WIN * WIN, WIN * WIN)
+    mask_here = lax.dynamic_index_in_dim(jnp.asarray(mask_all, BF16), unit_now, 0, keepdims=False)
+    mask_here = mask_here.astype(F32) * is_odd.astype(F32)
+    orders = np.stack((window_order(0), window_order(SHIFT)))
+    parity = section_now % 2
+    perm_in = lax.dynamic_index_in_dim(jnp.asarray(orders, BF16), parity, 0, keepdims=False)
+    perm_out = lax.dynamic_index_in_dim(
+        jnp.asarray(orders.transpose(0, 2, 1), BF16), parity, 0, keepdims=False
+    )
+    raw_rows = raw_pages.reshape(owned * rows_here, merge_in).astype(F32)
+    raw_hat, raw_rstd = norm_stats(raw_rows)
+    merged_in = (raw_hat * merge_scale + merge_shift).astype(BF16)
+    merged = dot_nn(merged_in, merge_weight).astype(BF16).reshape(owned, rows_here, D)
+    merged = to_halves(whole_unit(merged, 1))
+    merged, qv_bias, rel_table = lax.optimization_barrier((merged, qv_bias, rel_table))
+    cots = to_halves(whole_unit(cotangent[0, :, 0], 1))
+    weights, cots_first = lax.optimization_barrier((weights, cots[:, 0]))
+    first_list = [merged]
+    for section in range(1, section_count):
+        first_list.append(lax.ppermute(merged, "pipe", [(section, 0)]))
+    firsts = jnp.concatenate(first_list, 0)
 
     heads_here = rel_table.shape[2]
     head_set = jnp.concatenate((qv_bias[0].reshape(-1), rel_table[0].reshape(-1)))
@@ -946,39 +1046,16 @@
     bias_pos = jnp.pad(spread, ((0, 0), (0, PAD - WIN * WIN), (0, 0)))
     bias_pos = jnp.pad(
         bias_pos, ((0, 0), (0, 0), (0, KEYS - WIN * WIN)), constant_values=-1e30
-    ).reshape(GROUPS, STACK, KEYS)
-
-    mask_all = np.zeros((WIN_ROWS, WIN_COLS, PAD, KEYS), np.float32)
-    mask_all[:, :, : WIN * WIN, : WIN * WIN] = shift_mask(
-        WIN * WIN_ROWS, GRID_W, WIN, SHIFT
-    ).reshape(WIN_ROWS, WIN_COLS, WIN * WIN, WIN * WIN)
-    mask_here = lax.dynamic_index_in_dim(jnp.asarray(mask_all, BF16), unit_now, 0, keepdims=False)
-    mask_here = mask_here.astype(F32) * is_odd.astype(F32)
-    orders = np.stack((window_order(0), window_order(SHIFT)))
-    parity = section_now % 2
-    perm_in = lax.dynamic_index_in_dim(jnp.asarray(orders, BF16), parity, 0, keepdims=False)
-    perm_out = lax.dynamic_index_in_dim(
-        jnp.asarray(orders.transpose(0, 2, 1), BF16), parity, 0, keepdims=False
     )
+    bias_pos = bias_pos.reshape(GROUPS, STACK, KEYS)
+
     vecs = jnp.concatenate(
         (ln_gain[0], ln_bias[0], out_bias[0], final_scale[None], final_shift[None])
     )
     forward_tables = (perm_in, perm_out, mask_here, vecs, bias_qkv, fc1_bias, bias_pos)
     backward_tables = (perm_in, perm_out, vecs)
 
-    raw_rows = raw_pages.reshape(owned * rows_here, merge_in).astype(F32)
-    raw_hat, raw_rstd = norm_stats(raw_rows)
-    merged_in = (raw_hat * merge_scale + merge_shift).astype(BF16)
-    merged = dot_nn(merged_in, merge_weight).astype(BF16).reshape(owned, rows_here, D)
-    merged = to_halves(whole_unit(merged, 1))
-    first_list = [merged]
-    for section in range(1, section_count):
-        first_list.append(lax.ppermute(merged, "pipe", [(section, 0)]))
-    firsts = jnp.concatenate(first_list, 0)
-
-    cots = to_halves(whole_unit(cotangent[0, :, 0], 1))
-    cots_next = lax.ppermute(cots[:, 0], ("pipe", "tensor"), odd_pairs(-1))
-    cots = jnp.where(is_odd, jnp.stack((cots[:, 1], cots_next), 1), cots)
+    cots_next = lax.ppermute(cots_first, ("pipe", "tensor"), odd_pairs(-1))
 
     tick_count = micro_count + 2 * (section_count - 1)
 
@@ -986,14 +1063,7 @@
         slot_now = tick_now - 2 * start
         is_valid = (slot_now >= 0) & (slot_now < micro_count)
         slot = jnp.clip(slot_now, 0, micro_count - 1)
-        return jnp.stack([flag.astype(jnp.int32) for flag in (is_valid, slot, is_first, is_last)])
-
-    def stacks_of(*kinds):
-        return pl.pallas_call(
-            lambda *refs: None,
-            out_shape=[jax.ShapeDtypeStruct(shape, dtype) for shape, dtype in kinds],
-            out_specs=any_specs(len(kinds)),
-        )()
+        return jnp.stack([flag.astype(jnp.int32) for flag in (is_valid, slot, is_first, is_last, is_odd)])
 
     def of_micro(shape, dtype):
         return ((micro_count,) + shape, dtype)
@@ -1012,14 +1082,18 @@
         of_micro((2, HALF, D), BF16),
         ((HALF, D), BF16),
         ((HALF, D), BF16),
+        after=() if lined else (weights,),
     )
     recv = (empty_a, empty_b)
     for tick_now in range(tick_count):
         coming = recv
         if tick_now > 0:
             coming = hop(outgoing, range(section_count - 1), 1)
+        flags = flags_at(section_now, tick_now)
+        if tick_now == 2:
+            flags, cots_next = lax.optimization_barrier((flags, cots_next))
         outgoing, stacks = layer_forward(
-            flags_at(section_now, tick_now), *recv, firsts, forward_tables, weights, stacks
+            flags, *recv, firsts, forward_tables, weights, stacks
         )
         recv = coming
     (
@@ -1035,8 +1109,6 @@
         out_all,
         hid_all,
     ) = stacks
-    hid_before = lax.ppermute(hid_all[:, 1], ("pipe", "tensor"), odd_pairs(1))
-
     stacks = (
         x_all,
         qkv_all,
@@ -1054,18 +1126,22 @@
         if tick_now > 0:
             coming = hop(outgoing, range(1, section_count), -1)
         flags = flags_at(section_count - 1 - section_now, tick_now)
-        if tick_now == tick_count // 2:
+        if tick_now == tick_count - 3:
             flags, hid_before = lax.optimization_barrier((flags, hid_before))
         outgoing, stacks = layer_backward(
             flags,
             *recv,
             cots,
+            cots_next,
             backward_tables,
             weights,
             (probs_all, mid_all, out_all),
             stacks,
         )
         recv = coming
+        if tick_now == micro_count - 1:
+            outgoing, hid_all = lax.optimization_barrier((outgoing, hid_all))
+            hid_before = lax.ppermute(hid_all[:, 1], ("pipe", "tensor"), odd_pairs(1))
     dba_all, dqkv_all, dpre_all, dbm_all, dx_all, sums_all, dpos = stacks
     shown = jnp.where(is_odd, jnp.stack((hid_before, hid_all[:, 0]), 1), hid_all)
     shown = own_part(from_halves(shown), 1)
@@ -1090,21 +1166,28 @@
         total = mine if total is None else mine + total
         return total / copies
 
-    def over_tensor(total):
-        return lax.psum_scatter(total.astype(BF16), "tensor", scatter_dimension=0, tiled=True)
-
-    g_proj = weight_gradient(mixed_all, dba_all).astype(BF16)
-    g_proj, act_all, dbm_all, dpre_all, rmlp_all, dqkv_all, rattn_all = lax.optimization_barrier(
-        (g_proj, act_all, dbm_all, dpre_all, rmlp_all, dqkv_all, rattn_all)
-    )
-    g_proj = over_tensor(g_proj).astype(F32)
-    g_fc2 = over_tensor(weight_gradient(act_all, dbm_all)).astype(F32)
-    g_fc1 = over_tensor(weight_gradient(dpre_all, rmlp_all)).astype(F32).T
+    def over_tensor(*totals):
+        totals = [
+            total.astype(BF16).reshape(tensor_count, -1, total.shape[1]) for total in totals
+        ]
+        rows = [total.shape[1] for total in totals]
+        total = jnp.concatenate(totals, 1)
+        total = lax.psum_scatter(total, "tensor", scatter_dimension=0).astype(F32)
+        return jnp.split(total, np.cumsum(rows)[:-1])
+
+    g_proj = weight_gradient(mixed_all, dba_all)
     g_qkv = weight_gradient(dqkv_all, rattn_all)
     if copies > 1:
         g_qkv = g_qkv.reshape(BLOCKS, 3, copies, TB // copies, own_width)
         g_qkv = g_qkv.transpose(0, 2, 1, 3, 4).reshape(3 * D, own_width)
-    g_qkv = over_tensor(g_qkv).astype(F32).T.reshape(own_width, 3, D // tensor_count)
+    g_proj, g_qkv, act_all, dbm_all, dpre_all, rmlp_all, dx_all = lax.optimization_barrier(
+        (g_proj, g_qkv, act_all, dbm_all, dpre_all, rmlp_all, dx_all)
+    )
+    g_proj, g_qkv = over_tensor(g_proj, g_qkv)
+    g_fc2 = weight_gradient(act_all, dbm_all)
+    g_fc2, g_fc1 = over_tensor(g_fc2, weight_gradient(dpre_all, rmlp_all))
+    g_fc1 = g_fc1.T
+    g_qkv = g_qkv.T.reshape(own_width, 3, D // tensor_count)
 
     own_grads = dx_all[:owned]
     for section in range(1, section_count):

time: 1140 us -> 1080 us (0.947)
  waiting for transfers between devices: 358 us -> 303 us
  local copies, waits for them, and re-layouts: 130 us -> 166 us
  starting transfers between devices: 182 us -> 150 us
  other arithmetic: 58.1 us -> 37.8 us
  Pallas kernels: 272 us -> 289 us
    ppermute x7, waiting for transfers between devices: 38.5 us -> 12 us  [shares_summed(): total = total + lax.ppermute(block, axis, pairs).astype(F32)]
    reduce_scatter x4 -> x2, waiting for transfers between devices: 23.7 us -> 0.01 us  [over_tensor(): total = lax.psum_scatter(total, 'tensor', scatter_dimension=0).astype(F32)]
    ppermute x16, waiting for transfers between devices: 108 us -> 84.7 us  [hop(): to_a = lax.ppermute(halves[1], axes, section_pairs(sections, step, (0, 1)))]
    all_gather x2 -> x1, waiting for transfers between devices: 75.5 us -> 52.8 us  [on_device(): weights = lax.all_gather(block_rows(*shards), group_axes, axis=0)]
    ppermute x5, waiting for transfers between devices: 14.2 us -> 36.5 us  [summed(): values = values + lax.ppermute(values, axis, pairs)]
    ppermute x4 -> x8, starting transfers between devices: 32.4 us -> 12.2 us  [the longest x7 10.5 us: passed_round(): parts.append(lax.ppermute(block, axis, pairs))]
    ppermute x3, waiting for transfers between devices: 0.01 us -> 19.8 us  [on_device(): lax.ppermute(dx_all[section * owned:(section + 1) * owned], 'pipe', [(0,...]
    ppermute x4, waiting for transfers between devices: 21.1 us -> 4.3 us  [weight_gradient(): lax.ppermute(part((dp_now + step) % dp_count).astype(BF16), 'dp', pairs)]
  transfers between devices with their start and end apart: 65 -> 66, of which waited for: 27 -> 23; matrix products, arithmetic and copies ran while one was open for 21% -> 22% of each run, Pallas kernels for 18% -> 23%
where the time goes in v4:
time: 1080 us; the launch traced here: 1070 us
  waiting for transfers between devices  303 us (28%)
  Pallas kernels  289 us (27%)
  local copies, waits for them, and re-layouts  166 us (15%)
  starting transfers between devices  150 us (14%)
  matrix products  88.5 us (8%)
  other arithmetic  37.8 us (3%)
  between operations  16.2 us (2%)
  blocking collectives  15.2 us (1%)
    pallas_call x10, Pallas kernels, layer_backward(): pl.pallas_call(backward_kernel, out_shape=shapes_of(stacks) + [jax.ShapeD...  166 us
    pallas_call x10, Pallas kernels, layer_forward(): pl.pallas_call(forward_kernel, out_shape=shapes_of(stacks) + [jax.ShapeDt...  123 us
    ppermute x16, waiting for transfers between devices, hop(): to_a = lax.ppermute(halves[1], axes, section_pairs(sections, step, (0, 1)))  84.7 us
    dot_general x9, matrix products, dot_tn(): lax.dot_general(left, right, (((0,), (0,)), ((), ())), preferred_element_...  73.2 us
    ppermute x16, starting transfers between devices, hop(): to_b = lax.ppermute(halves[0], axes, section_pairs(sections, step, (-1, 0)))  53.8 us
    all_gather x1, waiting for transfers between devices, on_device(): weights = lax.all_gather(block_rows(*shards), group_axes, axis=0)  52.8 us
    ppermute x16, starting transfers between devices, hop(): to_a = lax.ppermute(halves[1], axes, section_pairs(sections, step, (0, 1)))  51.5 us
    unnamed x194, local copies, waits for them, and re-layouts  50.6 us
  transfers between devices with their start and end apart: 66, of which 23 were waited for; matrix products, arithmetic and copies ran while one was open for 22% of the time, Pallas kernels for 23%

profile of v4, /device:TPU:9, one launch (start us, length us, event | category | flops | bytes accessed | tf_op | source)
XLA Modules:
  0.0 1066.2 jit_solution(14641805882548155802)
XLA Ops:
  27.2 13.2 %collective-permute-done.3 = bf16[72,1024]{1,0:T(8,128)(2,1)S(1)} collective-permute-done((bf16[72,1024]{1,0:T(8,128)(2,1)S(1)}, bf16[72,1024]{1,0:T(8,128)(2,1)S(1)}, u32[]{:S(2)}, u32[]{:S(2)}) %collective-permute-start.3) | collective-permute-done | bytes 147488 | tf_op jit(solution)/shard_map/ppermute | solution.py:991
  76.6 26.3 %collective-permute-done.6 = bf16[8,72,1024]{2,1,0:T(8,128)(2,1)} collective-permute-done((bf16[8,72,1024]{2,1,0:T(8,128)(2,1)}, bf16[8,72,1024]{2,1,0:T(8,128)(2,1)}, u32[]{:S(2)}, u32[]{:S(2)}) %collective-permute-start.6) | collective-permute-done | bytes 1179680 | tf_op jit(solution)/shard_map/ppermute | solution.py:991
  119.6 15.2 %all_gather.11 = f32[128,128]{1,0:T(8,128)S(1)} all-gather(f32[32,128]{1,0:T(8,128)S(1)} %fusion.54), channel_id=1, replica_groups=mesh['pipe'=4,'dp'=2,'tensor'=4] {'tensor'}, dimensions={0}, use_global_device_ids=true | all-gather | bytes 81920 | tf_op jit(solution)/shard_map/all_gather | solution.py:927
  183.0 52.8 %all-gather.3.cloned.1.call-done = bf16[24576,512]{1,0:T(8,128)(2,1)} async-done(((bf16[3072,512]{1,0:T(8,128)(2,1)}), bf16[24576,512]{1,0:T(8,128)(2,1)}) %all-gather.3.cloned.1.call-update) | async-done | bytes 25165840 | tf_op jit(solution)/shard_map/all_gather | solution.py:960
  237.6 23.7 %layer_forward.10 = (bf16[4,336,1024]{2,1,0:T(8,128)(2,1)}, bf16[4,336,3072]{2,1,0:T(8,128)(2,1)}, bf16[4,24,448,128]{3,2,1,0:T(8,128)(2,1)}, bf16[4,336,1024]{2...) custom-call(s32[5]{0:T(128)} %stack.431.flags, ...), custom_call_target="tpu_custom_call", output_to_operand_aliasing={{0}: (12, {}), {1}: (13, {}), {2}: (14, {}), {3}: (15, {}),... | custom-call | flops 8455716864 | bytes 41943040 | tf_op jit(solution)/shard_map/layer_forward/pallas_call | solution.py:735
  264.0 23.4 %layer_forward.11 = (bf16[4,336,1024]{2,1,0:T(8,128)(2,1)}, bf16[4,336,3072]{2,1,0:T(8,128)(2,1)}, bf16[4,24,448,128]{3,2,1,0:T(8,128)(2,1)}, bf16[4,336,1024]{2...) custom-call(s32[5]{0:T(128)} %stack.426.flags, ...), custom_call_target="tpu_custom_call", output_to_operand_aliasing={{0}: (12, {}), {1}: (13, {}), {2}: (14, {}), {3}: (15, {}),... | custom-call | flops 8455716864 | bytes 41943040 | tf_op jit(solution)/shard_map/layer_forward/pallas_call | solution.py:735
  290.8 23.7 %layer_forward.12 = (bf16[4,336,1024]{2,1,0:T(8,128)(2,1)}, bf16[4,336,3072]{2,1,0:T(8,128)(2,1)}, bf16[4,24,448,128]{3,2,1,0:T(8,128)(2,1)}, bf16[4,336,1024]{2...) custom-call(s32[5]{0:T(128)} %stack.395.flags, ...), custom_call_target="tpu_custom_call", output_to_operand_aliasing={{0}: (12, {}), {1}: (13, {}), {2}: (14, {}), {3}: (15, {}),... | custom-call | flops 8455716864 | bytes 41943040 | tf_op jit(solution)/shard_map/layer_forward/pallas_call | solution.py:735
  318.0 23.4 %layer_forward.13 = (bf16[4,336,1024]{2,1,0:T(8,128)(2,1)}, bf16[4,336,3072]{2,1,0:T(8,128)(2,1)}, bf16[4,24,448,128]{3,2,1,0:T(8,128)(2,1)}, bf16[4,336,1024]{2...) custom-call(s32[5]{0:T(128)} %stack.422.flags, ...), custom_call_target="tpu_custom_call", output_to_operand_aliasing={{0}: (12, {}), {1}: (13, {}), {2}: (14, {}), {3}: (15, {}),... | custom-call | flops 8455716864 | bytes 41943040 | tf_op jit(solution)/shard_map/layer_forward/pallas_call | solution.py:735
  352.2 11.0 %collective-permute-start.21 = (bf16[160,1024]{1,0:T(8,128)(2,1)}, bf16[160,1024]{1,0:T(8,128)(2,1)S(1)}, u32[]{:S(2)}, u32[]{:S(2)}) collective-permute-start(bf16[160,1024]{1,0:T(8,128)(2,1)} %get-tuple-element.350), channel_id=1, source_target_pairs={{0,8},{1,9},{2,10},{3,11},{8,17},{9,18},{10,19},{11,16},{16,24},{1... | collective-permute-start | bytes 983048 | tf_op jit(solution)/shard_map/ppermute | solution.py:886
  369.0 22.3 %collective-permute-start.19 = (bf16[160,1024]{1,0:T(8,128)(2,1)}, bf16[160,1024]{1,0:T(8,128)(2,1)S(1)}, u32[]{:S(2)}, u32[]{:S(2)}) collective-permute-start(bf16[160,1024]{1,0:T(8,128)(2,1)} %get-tuple-element.348), channel_id=1, source_target_pairs={{0,8},{1,9},{2,10},{3,11},{8,17},{9,18},{10,19},{11,16},{16,24},{1... | collective-permute-start | bytes 983048 | tf_op jit(solution)/shard_map/ppermute | solution.py:886
  415.6 24.2 %collective-permute-start.24 = (bf16[160,1024]{1,0:T(8,128)(2,1)}, bf16[160,1024]{1,0:T(8,128)(2,1)S(1)}, u32[]{:S(2)}, u32[]{:S(2)}) collective-permute-start(bf16[160,1024]{1,0:T(8,128)(2,1)} %get-tuple-element.375), channel_id=1, source_target_pairs={{0,11},{1,8},{2,9},{3,10},{8,16},{9,17},{10,18},{11,19},{16,27},{1... | collective-permute-start | bytes 983048 | tf_op jit(solution)/shard_map/ppermute | solution.py:887
  475.4 15.5 %collective-permute-done.30.recv_b = bf16[160,1024]{1,0:T(8,128)(2,1)S(1)} collective-permute-done((bf16[160,1024]{1,0:T(8,128)(2,1)}, bf16[160,1024]{1,0:T(8,128)(2,1)S(1)}, u32[]{:S(2)}, u32[]{:S(2)}) %collective-permute-start.30) | collective-permute-done | bytes 327712 | tf_op jit(solution)/shard_map/ppermute | solution.py:887
  511.7 16.9 %collective-permute-done.35.recv_b = bf16[160,1024]{1,0:T(8,128)(2,1)} collective-permute-done((bf16[160,1024]{1,0:T(8,128)(2,1)}, bf16[160,1024]{1,0:T(8,128)(2,1)}, u32[]{:S(2)}, u32[]{:S(2)}) %collective-permute-start.35) | collective-permute-done | bytes 327712 | tf_op jit(solution)/shard_map/ppermute | solution.py:887
  545.4 77.5 %collective-permute-done.38.recv_a = bf16[160,1024]{1,0:T(8,128)(2,1)S(1)} collective-permute-done((bf16[160,1024]{1,0:T(8,128)(2,1)}, bf16[160,1024]{1,0:T(8,128)(2,1)S(1)}, u32[]{:S(2)}, u32[]{:S(2)}) %collective-permute-start.38) | collective-permute-done | bytes 327712 | tf_op jit(solution)/shard_map/ppermute | solution.py:886
  631.7 32.9 %layer_backward.16 = (bf16[4,336,1024]{2,1,0:T(8,128)(2,1)}, bf16[4,336,3072]{2,1,0:T(8,128)(2,1)}, bf16[4,336,4096]{2,1,0:T(8,128)(2,1)}, bf16[4,336,1024]{2,1,...) custom-call(s32[5]{0:T(128)} %stack.469.flags, ...), custom_call_target="tpu_custom_call", output_to_operand_aliasing={{0}: (12, {}), {1}: (13, {}), {2}: (14, {}), {3}: (15, {}),... | custom-call | flops 8455716864 | bytes 52428800 | tf_op jit(solution)/shard_map/layer_backward/pallas_call | solution.py:786
  668.4 32.4 %layer_backward.17 = (bf16[4,336,1024]{2,1,0:T(8,128)(2,1)}, bf16[4,336,3072]{2,1,0:T(8,128)(2,1)}, bf16[4,336,4096]{2,1,0:T(8,128)(2,1)}, bf16[4,336,1024]{2,1,...) custom-call(s32[5]{0:T(128)} %stack.383.flags, ...), custom_call_target="tpu_custom_call", output_to_operand_aliasing={{0}: (12, {}), {1}: (13, {}), {2}: (14, {}), {3}: (15, {}),... | custom-call | flops 8455716864 | bytes 52428800 | tf_op jit(solution)/shard_map/layer_backward/pallas_call | solution.py:786
  707.2 33.0 %layer_backward.18 = (bf16[4,336,1024]{2,1,0:T(8,128)(2,1)}, bf16[4,336,3072]{2,1,0:T(8,128)(2,1)}, bf16[4,336,4096]{2,1,0:T(8,128)(2,1)}, bf16[4,336,1024]{2,1,...) custom-call(s32[5]{0:T(128)} %stack.473.flags, ...), custom_call_target="tpu_custom_call", output_to_operand_aliasing={{0}: (12, {}), {1}: (13, {}), {2}: (14, {}), {3}: (15, {}),... | custom-call | flops 8455716864 | bytes 52428800 | tf_op jit(solution)/shard_map/layer_backward/pallas_call | solution.py:786
  744.3 32.6 %layer_backward.19 = (bf16[4,336,1024]{2,1,0:T(8,128)(2,1)}, bf16[4,336,3072]{2,1,0:T(8,128)(2,1)}, bf16[4,336,4096]{2,1,0:T(8,128)(2,1)}, bf16[4,336,1024]{2,1,...) custom-call(s32[5]{0:T(128)} %stack.457.flags, ...), custom_call_target="tpu_custom_call", output_to_operand_aliasing={{0}: (12, {}), {1}: (13, {}), {2}: (14, {}), {3}: (15, {}),... | custom-call | flops 8455716864 | bytes 52428800 | tf_op jit(solution)/shard_map/layer_backward/pallas_call | solution.py:786
  776.9 10.4 convolution_convert_fusion.2
  830.6 10.2 add_convert_fusion.1
  847.2 13.9 %add_convert_fusion = bf16[4096,512]{1,0:T(8,128)(2,1)} fusion(bf16[4096,512]{1,0:T(8,128)(2,1)} %collective-permute-done.62, bf16[1344,4096]{1,0:T(8,128)(2,1)} %bitcast.297, bf16[1344,1024]{1,0:T(8,128)(2,1)S(1)} %bitcast.316, s32[]{:T(128)S(6)} %select_n.163), kind=kOutput, calls=%fused_computation.1 | convolution fusion | flops 5643436032 | bytes 20774916 | tf_op jit(solution)/shard_map/dot_general | solution.py:106
  933.9 12.7 %collective-permute-done.48 = bf16[1,2,160,1024]{3,2,1,0:T(8,128)(2,1)} collective-permute-done((bf16[1,2,160,1024]{3,2,1,0:T(8,128)(2,1)}, bf16[1,2,160,1024]{3,2,1,0:T(8,128)(2,1)}, u32[]{:S(2)}, u32[]{:S(2)}) %collective-permute-start.48) | collective-permute-done | bytes 655392 | tf_op jit(solution)/shard_map/ppermute | solution.py:1194
  982.5 11.0 %collective-permute-done.58 = f32[272,128]{1,0:T(8,128)S(1)} collective-permute-done((f32[272,128]{1,0:T(8,128)S(1)}, f32[272,128]{1,0:T(8,128)S(1)}, u32[]{:S(2)}, u32[]{:S(2)}) %collective-permute-start.58) | collective-permute-done | bytes 139296 | tf_op jit(solution)/shard_map/ppermute | solution.py:906
  1008.4 17.1 %collective-permute-done.60 = f32[48,128]{1,0:T(8,128)S(1)} collective-permute-done((f32[48,128]{1,0:T(8,128)S(1)}, f32[48,128]{1,0:T(8,128)S(1)}, u32[]{:S(2)}, u32[]{:S(2)}) %collective-permute-start.60) | collective-permute-done | bytes 24608 | tf_op jit(solution)/shard_map/ppermute | solution.py:906
  (484 shorter events, 474.5 us)
Async XLA Ops:
  7.2 228.7 %all-gather.3.cloned.1.call-start = ((), (), s32[]{:S(2)}) async-start(), calls=%async_computation.4 | async-start | bytes 28311552 | tf_op jit(solution)/shard_map/all_gather | solution.py:960
  15.4 1033.6 %reduce-scatter.3.cloned.1.call-start = ((), (), s32[]{:S(2)}) async-start(), calls=%async_computation.2 | async-start | bytes 5242880 | tf_op jit(solution)/shard_map/reduce_scatter | solution.py:1175
  50.2 52.7 %collective-permute-start.6 = (bf16[8,72,1024]{2,1,0:T(8,128)(2,1)}, bf16[8,72,1024]{2,1,0:T(8,128)(2,1)}, u32[]{:S(2)}, u32[]{:S(2)}) collective-permute-start(bf16[8,72,1024]{2,1,0:T(8,128)(2,1)} %bitcast.29), channel_id=1, source_target_pairs={{0,16},{8,24},{16,0},{24,8},{1,17},{9,25},{17,1},{25,9},{2,18},{10... | collective-permute-start | bytes 3538952 | tf_op jit(solution)/shard_map/ppermute | solution.py:991
  50.4 53.8 %collective-permute-start.7 = (bf16[8,72,1024]{2,1,0:T(8,128)(2,1)}, bf16[8,72,1024]{2,1,0:T(8,128)(2,1)}, u32[]{:S(2)}, u32[]{:S(2)}) collective-permute-start(bf16[8,72,1024]{2,1,0:T(8,128)(2,1)} %bitcast.29), channel_id=1, source_target_pairs={{0,8},{8,16},{16,24},{24,0},{1,9},{9,17},{17,25},{25,1},{2,10},{10... | collective-permute-start | bytes 3538952 | tf_op jit(solution)/shard_map/ppermute | solution.py:991
  134.9 44.7 %collective-permute-start.8 = (bf16[1,2,160,1024]{3,2,1,0:T(8,128)(2,1)S(1)}, bf16[1,2,160,1024]{3,2,1,0:T(8,128)(2,1)}, u32[]{:S(2)}, u32[]{:S(2)}) collective-permute-start(bf16[1,2,160,1024]{3,2,1,0:T(8,128)(2,1)S(1)} %pad.30), channel_id=1, source_target_pairs={{8,0},{9,1},{10,2},{11,3},{12,4},{13,5},{14,6},{15,7}} | collective-permute-start | bytes 1966088 | tf_op jit(solution)/shard_map/ppermute | solution.py:1029
  136.2 44.5 %collective-permute-start.9 = (bf16[1,2,160,1024]{3,2,1,0:T(8,128)(2,1)S(1)}, bf16[1,2,160,1024]{3,2,1,0:T(8,128)(2,1)}, u32[]{:S(2)}, u32[]{:S(2)}) collective-permute-start(bf16[1,2,160,1024]{3,2,1,0:T(8,128)(2,1)S(1)} %pad.30), channel_id=1, source_target_pairs={{16,0},{17,1},{18,2},{19,3},{20,4},{21,5},{22,6},{23,7}} | collective-permute-start | bytes 1966088 | tf_op jit(solution)/shard_map/ppermute | solution.py:1029
  137.5 44.4 %collective-permute-start.10 = (bf16[1,2,160,1024]{3,2,1,0:T(8,128)(2,1)S(1)}, bf16[1,2,160,1024]{3,2,1,0:T(8,128)(2,1)}, u32[]{:S(2)}, u32[]{:S(2)}) collective-permute-start(bf16[1,2,160,1024]{3,2,1,0:T(8,128)(2,1)S(1)} %pad.30), channel_id=1, source_target_pairs={{24,0},{25,1},{26,2},{27,3},{28,4},{29,5},{30,6},{31,7}} | collective-permute-start | bytes 1966088 | tf_op jit(solution)/shard_map/ppermute | solution.py:1029
  235.8 54.1 %collective-permute-start = (bf16[4,160,1024]{2,1,0:T(8,128)(2,1)}, bf16[4,160,1024]{2,1,0:T(8,128)(2,1)}, u32[]{:S(2)}, u32[]{:S(2)}) collective-permute-start(bf16[4,160,1024]{2,1,0:T(8,128)(2,1)} %slice_bitcast_fusion.2), channel_id=1, source_target_pairs={{8,11},{9,8},{10,9},{11,10},{24,27},{25,24},{26,25},{27,26},{12,15... | collective-permute-start | bytes 3932168 | tf_op jit(solution)/shard_map/ppermute | solution.py:1058
  352.2 42.3 %collective-permute-start.21 = (bf16[160,1024]{1,0:T(8,128)(2,1)}, bf16[160,1024]{1,0:T(8,128)(2,1)S(1)}, u32[]{:S(2)}, u32[]{:S(2)}) collective-permute-start(bf16[160,1024]{1,0:T(8,128)(2,1)} %get-tuple-element.350), channel_id=1, source_target_pairs={{0,8},{1,9},{2,10},{3,11},{8,17},{9,18},{10,19},{11,16},{16,24},{1... | collective-permute-start | bytes 983048 | tf_op jit(solution)/shard_map/ppermute | solution.py:886
  369.0 42.8 %collective-permute-start.19 = (bf16[160,1024]{1,0:T(8,128)(2,1)}, bf16[160,1024]{1,0:T(8,128)(2,1)S(1)}, u32[]{:S(2)}, u32[]{:S(2)}) collective-permute-start(bf16[160,1024]{1,0:T(8,128)(2,1)} %get-tuple-element.348), channel_id=1, source_target_pairs={{0,8},{1,9},{2,10},{3,11},{8,17},{9,18},{10,19},{11,16},{16,24},{1... | collective-permute-start | bytes 983048 | tf_op jit(solution)/shard_map/ppermute | solution.py:886
  402.9 37.0 %collective-permute-start.25 = (bf16[160,1024]{1,0:T(8,128)(2,1)}, bf16[160,1024]{1,0:T(8,128)(2,1)S(1)}, u32[]{:S(2)}, u32[]{:S(2)}) collective-permute-start(bf16[160,1024]{1,0:T(8,128)(2,1)} %get-tuple-element.376), channel_id=1, source_target_pairs={{0,8},{1,9},{2,10},{3,11},{8,17},{9,18},{10,19},{11,16},{16,24},{1... | collective-permute-start | bytes 983048 | tf_op jit(solution)/shard_map/ppermute | solution.py:886
  414.3 35.8 %collective-permute-start.23 = (bf16[160,1024]{1,0:T(8,128)(2,1)}, bf16[160,1024]{1,0:T(8,128)(2,1)S(1)}, u32[]{:S(2)}, u32[]{:S(2)}) collective-permute-start(bf16[160,1024]{1,0:T(8,128)(2,1)} %get-tuple-element.374), channel_id=1, source_target_pairs={{0,8},{1,9},{2,10},{3,11},{8,17},{9,18},{10,19},{11,16},{16,24},{1... | collective-permute-start | bytes 983048 | tf_op jit(solution)/shard_map/ppermute | solution.py:886
  466.9 37.5 %collective-permute-start.27 = (bf16[160,1024]{1,0:T(8,128)(2,1)}, bf16[160,1024]{1,0:T(8,128)(2,1)S(1)}, u32[]{:S(2)}, u32[]{:S(2)}) collective-permute-start(bf16[160,1024]{1,0:T(8,128)(2,1)} %get-tuple-element.417), channel_id=1, source_target_pairs={{8,1},{9,2},{10,3},{11,0},{16,8},{17,9},{18,10},{19,11},{24,17},{2... | collective-permute-start | bytes 983048 | tf_op jit(solution)/shard_map/ppermute | solution.py:886
  468.2 36.2 %collective-permute-start.28 = (bf16[160,1024]{1,0:T(8,128)(2,1)}, bf16[160,1024]{1,0:T(8,128)(2,1)S(1)}, u32[]{:S(2)}, u32[]{:S(2)}) collective-permute-start(bf16[160,1024]{1,0:T(8,128)(2,1)} %get-tuple-element.418), channel_id=1, source_target_pairs={{8,0},{9,1},{10,2},{11,3},{16,11},{17,8},{18,9},{19,10},{24,16},{2... | collective-permute-start | bytes 983048 | tf_op jit(solution)/shard_map/ppermute | solution.py:887
  509.6 157.6 %collective-permute-start.31 = (bf16[4,160,1024]{2,1,0:T(8,128)(2,1)S(1)}, bf16[4,160,1024]{2,1,0:T(8,128)(2,1)S(1)}, u32[]{:S(2)}, u32[]{:S(2)}) collective-permute-start(bf16[4,160,1024]{2,1,0:T(8,128)(2,1)S(1)} %slice_bitcast_fusion.1), channel_id=1, source_target_pairs={{8,9},{9,10},{10,11},{11,8},{24,25},{25,26},{26,27},{27,24},{12,13... | collective-permute-start | bytes 3932168 | tf_op jit(solution)/shard_map/ppermute | solution.py:1144
  538.6 84.3 %collective-permute-start.38 = (bf16[160,1024]{1,0:T(8,128)(2,1)}, bf16[160,1024]{1,0:T(8,128)(2,1)S(1)}, u32[]{:S(2)}, u32[]{:S(2)}) collective-permute-start(bf16[160,1024]{1,0:T(8,128)(2,1)} %get-tuple-element.462), channel_id=1, source_target_pairs={{8,1},{9,2},{10,3},{11,0},{16,8},{17,9},{18,10},{19,11},{24,17},{2... | collective-permute-start | bytes 983048 | tf_op jit(solution)/shard_map/ppermute | solution.py:886
  539.9 91.1 %collective-permute-start.39 = (bf16[160,1024]{1,0:T(8,128)(2,1)}, bf16[160,1024]{1,0:T(8,128)(2,1)S(1)}, u32[]{:S(2)}, u32[]{:S(2)}) collective-permute-start(bf16[160,1024]{1,0:T(8,128)(2,1)} %get-tuple-element.463), channel_id=1, source_target_pairs={{8,0},{9,1},{10,2},{11,3},{16,11},{17,8},{18,9},{19,10},{24,16},{2... | collective-permute-start | bytes 983048 | tf_op jit(solution)/shard_map/ppermute | solution.py:887
  542.8 124.5 %collective-permute-start.36 = (bf16[160,1024]{1,0:T(8,128)(2,1)}, bf16[160,1024]{1,0:T(8,128)(2,1)S(1)}, u32[]{:S(2)}, u32[]{:S(2)}) collective-permute-start(bf16[160,1024]{1,0:T(8,128)(2,1)} %get-tuple-element.460), channel_id=1, source_target_pairs={{8,1},{9,2},{10,3},{11,0},{16,8},{17,9},{18,10},{19,11},{24,17},{2... | collective-permute-start | bytes 983048 | tf_op jit(solution)/shard_map/ppermute | solution.py:886
  544.1 123.4 %collective-permute-start.37 = (bf16[160,1024]{1,0:T(8,128)(2,1)}, bf16[160,1024]{1,0:T(8,128)(2,1)S(1)}, u32[]{:S(2)}, u32[]{:S(2)}) collective-permute-start(bf16[160,1024]{1,0:T(8,128)(2,1)} %get-tuple-element.461), channel_id=1, source_target_pairs={{8,0},{9,1},{10,2},{11,3},{16,11},{17,8},{18,9},{19,10},{24,16},{2... | collective-permute-start | bytes 983048 | tf_op jit(solution)/shard_map/ppermute | solution.py:887
  664.7 38.8 %collective-permute-start.42 = (bf16[160,1024]{1,0:T(8,128)(2,1)}, bf16[160,1024]{1,0:T(8,128)(2,1)S(1)}, u32[]{:S(2)}, u32[]{:S(2)}) collective-permute-start(bf16[160,1024]{1,0:T(8,128)(2,1)} %get-tuple-element.480), channel_id=1, source_target_pairs={{8,1},{9,2},{10,3},{11,0},{16,8},{17,9},{18,10},{19,11},{24,17},{2... | collective-permute-start | bytes 983048 | tf_op jit(solution)/shard_map/ppermute | solution.py:886
  666.0 40.5 %collective-permute-start.43 = (bf16[160,1024]{1,0:T(8,128)(2,1)}, bf16[160,1024]{1,0:T(8,128)(2,1)S(1)}, u32[]{:S(2)}, u32[]{:S(2)}) collective-permute-start(bf16[160,1024]{1,0:T(8,128)(2,1)} %get-tuple-element.481), channel_id=1, source_target_pairs={{8,0},{9,1},{10,2},{11,3},{16,11},{17,8},{18,9},{19,10},{24,16},{2... | collective-permute-start | bytes 983048 | tf_op jit(solution)/shard_map/ppermute | solution.py:887
  700.8 39.4 %collective-permute-start.40 = (bf16[160,1024]{1,0:T(8,128)(2,1)}, bf16[160,1024]{1,0:T(8,128)(2,1)S(1)}, u32[]{:S(2)}, u32[]{:S(2)}) collective-permute-start(bf16[160,1024]{1,0:T(8,128)(2,1)} %get-tuple-element.478), channel_id=1, source_target_pairs={{8,1},{9,2},{10,3},{11,0},{16,8},{17,9},{18,10},{19,11},{24,17},{2... | collective-permute-start | bytes 983048 | tf_op jit(solution)/shard_map/ppermute | solution.py:886
  702.1 41.5 %collective-permute-start.41 = (bf16[160,1024]{1,0:T(8,128)(2,1)}, bf16[160,1024]{1,0:T(8,128)(2,1)S(1)}, u32[]{:S(2)}, u32[]{:S(2)}) collective-permute-start(bf16[160,1024]{1,0:T(8,128)(2,1)} %get-tuple-element.479), channel_id=1, source_target_pairs={{8,0},{9,1},{10,2},{11,3},{16,11},{17,8},{18,9},{19,10},{24,16},{2... | collective-permute-start | bytes 983048 | tf_op jit(solution)/shard_map/ppermute | solution.py:887
  810.8 242.1 %reduce-scatter.5.cloned.1.call-start = ((), (), s32[]{:S(2)}) async-start(), calls=%async_computation.3 | async-start | bytes 10485760 | tf_op jit(solution)/shard_map/reduce_scatter | solution.py:1175
  (124 other events, 1449.1 us)
Sparse Core Ops, SparseCore 0:
  15.5 220.3 all-gather.2
  810.9 74.0 reduce-scatter.2
  887.5 152.2 reduce-scatter.4

commit v5 on v4

--- a/solution.py
+++ b/solution.py
@@ -520,6 +520,8 @@
         w_copy(0, 0).start()
         load(5).start()
         w_copy(1, 0).start()
+        w_copy(0, 1).start()
+        w_copy(1, 1).start()
         for index in range(4):
             load(index).wait()
         sums[...] = jnp.zeros_like(sums)
@@ -566,12 +568,12 @@
             columns = lanes(block * FB, FB)
             w_copy(0, block).wait()
 
-            @pl.when(block < BLOCKS - 1)
+            @pl.when(block < BLOCKS - 2)
             def _():
-                w_copy(0, block + 1).start()
-                w_copy(1, block + 1).start()
-
-            @pl.when(block == BLOCKS - 1)
+                w_copy(0, block + 2).start()
+                w_copy(1, block + 2).start()
+
+            @pl.when(block == BLOCKS - 2)
             def _():
                 load(6).start()
                 proj_copy().start()
@@ -1195,10 +1197,12 @@
             dx_all[section * owned : (section + 1) * owned], "pipe", [(0, section)]
         )
         own_grads = jnp.where(section_now == section, moved, own_grads)
+    own_grads, g_proj, g_qkv = lax.optimization_barrier((own_grads, g_proj, g_qkv))
     grad_merged = own_part(from_halves(own_grads), 1).reshape(owned * rows_here, D)
-    g_merge = dot_tn(merged_in, grad_merged)
+    g_merge = dot_tn(merged_in, grad_merged).astype(BF16)
+    g_merge, dpos = lax.optimization_barrier((g_merge, dpos))
     g_merge = g_merge.reshape(section_count, dp_count, tensor_count, share, D)
-    g_merge = shares_summed(g_merge.transpose(1, 0, 2, 3, 4).astype(BF16), "dp")[0]
+    g_merge = shares_summed(g_merge.transpose(1, 0, 2, 3, 4), "dp")[0]
     g_merge = shares_summed(g_merge.astype(BF16), "pipe")[0]
     g_merge = shares_summed(g_merge.astype(BF16), "tensor")[0]
     grad_unit = dot_nt(grad_merged, merge_weight)

time: 1080 us -> 1070 us (level)
    unnamed x194 -> x187, local copies, waits for them, and re-layouts: 50.6 us -> 45.6 us
  transfers between devices with their start and end apart: 66 -> 66, of which waited for: 23 -> 23; matrix products, arithmetic and copies ran while one was open for 22% -> 23% of each run, Pallas kernels for 23% -> 23%
where the time goes in v5:
time: 1070 us; the launch traced here: 1050 us
  waiting for transfers between devices  298 us (28%)
  Pallas kernels  285 us (27%)
  local copies, waits for them, and re-layouts  163 us (15%)
  starting transfers between devices  151 us (14%)
  matrix products  91.3 us (9%)
  other arithmetic  33.9 us (3%)
  between operations  16.1 us (2%)
  blocking collectives  15.8 us (1%)
    pallas_call x10, Pallas kernels, layer_backward(): pl.pallas_call(backward_kernel, out_shape=shapes_of(stacks) + [jax.ShapeD...  161 us
    pallas_call x10, Pallas kernels, layer_forward(): pl.pallas_call(forward_kernel, out_shape=shapes_of(stacks) + [jax.ShapeDt...  123 us
    ppermute x16, waiting for transfers between devices, hop(): to_a = lax.ppermute(halves[1], axes, section_pairs(sections, step, (0, 1)))  81.2 us
    dot_general x9, matrix products, dot_tn(): lax.dot_general(left, right, (((0,), (0,)), ((), ())), preferred_element_...  74 us
    ppermute x16, starting transfers between devices, hop(): to_b = lax.ppermute(halves[0], axes, section_pairs(sections, step, (-1, 0)))  53.9 us
    all_gather x1, waiting for transfers between devices, on_device(): weights = lax.all_gather(block_rows(*shards), group_axes, axis=0)  52.8 us
    ppermute x16, starting transfers between devices, hop(): to_a = lax.ppermute(halves[1], axes, section_pairs(sections, step, (0, 1)))  51.4 us
    ppermute x16, waiting for transfers between devices, hop(): to_b = lax.ppermute(halves[0], axes, section_pairs(sections, step, (-1, 0)))  47.2 us
  transfers between devices with their start and end apart: 66, of which 23 were waited for; matrix products, arithmetic and copies ran while one was open for 23% of the time, Pallas kernels for 23%

profile of v5, /device:TPU:9, one launch (start us, length us, event | category | flops | bytes accessed | tf_op | source)
XLA Modules:
  0.0 1054.2 jit_solution(2232074829877145405)
XLA Ops:
  27.2 13.2 %collective-permute-done.3 = bf16[72,1024]{1,0:T(8,128)(2,1)S(1)} collective-permute-done((bf16[72,1024]{1,0:T(8,128)(2,1)S(1)}, bf16[72,1024]{1,0:T(8,128)(2,1)S(1)}, u32[]{:S(2)}, u32[]{:S(2)}) %collective-permute-start.3) | collective-permute-done | bytes 147488 | tf_op jit(solution)/shard_map/ppermute | solution.py:993
  76.7 26.3 %collective-permute-done.6 = bf16[8,72,1024]{2,1,0:T(8,128)(2,1)} collective-permute-done((bf16[8,72,1024]{2,1,0:T(8,128)(2,1)}, bf16[8,72,1024]{2,1,0:T(8,128)(2,1)}, u32[]{:S(2)}, u32[]{:S(2)}) %collective-permute-start.6) | collective-permute-done | bytes 1179680 | tf_op jit(solution)/shard_map/ppermute | solution.py:993
  119.2 15.8 %all_gather.11 = f32[128,128]{1,0:T(8,128)S(1)} all-gather(f32[32,128]{1,0:T(8,128)S(1)} %fusion.44), channel_id=1, replica_groups=mesh['pipe'=4,'dp'=2,'tensor'=4] {'tensor'}, dimensions={0}, use_global_device_ids=true | all-gather | bytes 81920 | tf_op jit(solution)/shard_map/all_gather | solution.py:929
  183.1 52.8 %all-gather.3.cloned.1.call-done = bf16[24576,512]{1,0:T(8,128)(2,1)} async-done(((bf16[3072,512]{1,0:T(8,128)(2,1)}), bf16[24576,512]{1,0:T(8,128)(2,1)}) %all-gather.3.cloned.1.call-update) | async-done | bytes 25165840 | tf_op jit(solution)/shard_map/all_gather | solution.py:962
  237.6 23.7 %layer_forward.10 = (bf16[4,336,1024]{2,1,0:T(8,128)(2,1)}, bf16[4,336,3072]{2,1,0:T(8,128)(2,1)}, bf16[4,24,448,128]{3,2,1,0:T(8,128)(2,1)}, bf16[4,336,1024]{2...) custom-call(s32[5]{0:T(128)} %stack.431.flags, ...), custom_call_target="tpu_custom_call", output_to_operand_aliasing={{0}: (12, {}), {1}: (13, {}), {2}: (14, {}), {3}: (15, {}),... | custom-call | flops 8455716864 | bytes 41943040 | tf_op jit(solution)/shard_map/layer_forward/pallas_call | solution.py:737
  264.0 23.4 %layer_forward.11 = (bf16[4,336,1024]{2,1,0:T(8,128)(2,1)}, bf16[4,336,3072]{2,1,0:T(8,128)(2,1)}, bf16[4,24,448,128]{3,2,1,0:T(8,128)(2,1)}, bf16[4,336,1024]{2...) custom-call(s32[5]{0:T(128)} %stack.426.flags, ...), custom_call_target="tpu_custom_call", output_to_operand_aliasing={{0}: (12, {}), {1}: (13, {}), {2}: (14, {}), {3}: (15, {}),... | custom-call | flops 8455716864 | bytes 41943040 | tf_op jit(solution)/shard_map/layer_forward/pallas_call | solution.py:737
  290.9 23.7 %layer_forward.12 = (bf16[4,336,1024]{2,1,0:T(8,128)(2,1)}, bf16[4,336,3072]{2,1,0:T(8,128)(2,1)}, bf16[4,24,448,128]{3,2,1,0:T(8,128)(2,1)}, bf16[4,336,1024]{2...) custom-call(s32[5]{0:T(128)} %stack.395.flags, ...), custom_call_target="tpu_custom_call", output_to_operand_aliasing={{0}: (12, {}), {1}: (13, {}), {2}: (14, {}), {3}: (15, {}),... | custom-call | flops 8455716864 | bytes 41943040 | tf_op jit(solution)/shard_map/layer_forward/pallas_call | solution.py:737
  318.1 23.4 %layer_forward.13 = (bf16[4,336,1024]{2,1,0:T(8,128)(2,1)}, bf16[4,336,3072]{2,1,0:T(8,128)(2,1)}, bf16[4,24,448,128]{3,2,1,0:T(8,128)(2,1)}, bf16[4,336,1024]{2...) custom-call(s32[5]{0:T(128)} %stack.422.flags, ...), custom_call_target="tpu_custom_call", output_to_operand_aliasing={{0}: (12, {}), {1}: (13, {}), {2}: (14, {}), {3}: (15, {}),... | custom-call | flops 8455716864 | bytes 41943040 | tf_op jit(solution)/shard_map/layer_forward/pallas_call | solution.py:737
  352.2 11.0 %collective-permute-start.21 = (bf16[160,1024]{1,0:T(8,128)(2,1)}, bf16[160,1024]{1,0:T(8,128)(2,1)S(1)}, u32[]{:S(2)}, u32[]{:S(2)}) collective-permute-start(bf16[160,1024]{1,0:T(8,128)(2,1)} %get-tuple-element.355), channel_id=1, source_target_pairs={{0,8},{1,9},{2,10},{3,11},{8,17},{9,18},{10,19},{11,16},{16,24},{1... | collective-permute-start | bytes 983048 | tf_op jit(solution)/shard_map/ppermute | solution.py:888
  369.0 22.3 %collective-permute-start.19 = (bf16[160,1024]{1,0:T(8,128)(2,1)}, bf16[160,1024]{1,0:T(8,128)(2,1)S(1)}, u32[]{:S(2)}, u32[]{:S(2)}) collective-permute-start(bf16[160,1024]{1,0:T(8,128)(2,1)} %get-tuple-element.353), channel_id=1, source_target_pairs={{0,8},{1,9},{2,10},{3,11},{8,17},{9,18},{10,19},{11,16},{16,24},{1... | collective-permute-start | bytes 983048 | tf_op jit(solution)/shard_map/ppermute | solution.py:888
  415.7 24.2 %collective-permute-start.24 = (bf16[160,1024]{1,0:T(8,128)(2,1)}, bf16[160,1024]{1,0:T(8,128)(2,1)S(1)}, u32[]{:S(2)}, u32[]{:S(2)}) collective-permute-start(bf16[160,1024]{1,0:T(8,128)(2,1)} %get-tuple-element.380), channel_id=1, source_target_pairs={{0,11},{1,8},{2,9},{3,10},{8,16},{9,17},{10,18},{11,19},{16,27},{1... | collective-permute-start | bytes 983048 | tf_op jit(solution)/shard_map/ppermute | solution.py:889
  475.4 15.5 %collective-permute-done.30.recv_b = bf16[160,1024]{1,0:T(8,128)(2,1)S(1)} collective-permute-done((bf16[160,1024]{1,0:T(8,128)(2,1)}, bf16[160,1024]{1,0:T(8,128)(2,1)S(1)}, u32[]{:S(2)}, u32[]{:S(2)}) %collective-permute-start.30) | collective-permute-done | bytes 327712 | tf_op jit(solution)/shard_map/ppermute | solution.py:889
  511.7 16.9 %collective-permute-done.35.recv_b = bf16[160,1024]{1,0:T(8,128)(2,1)} collective-permute-done((bf16[160,1024]{1,0:T(8,128)(2,1)}, bf16[160,1024]{1,0:T(8,128)(2,1)}, u32[]{:S(2)}, u32[]{:S(2)}) %collective-permute-start.35) | collective-permute-done | bytes 327712 | tf_op jit(solution)/shard_map/ppermute | solution.py:889
  545.4 73.9 %collective-permute-done.38.recv_a = bf16[160,1024]{1,0:T(8,128)(2,1)S(1)} collective-permute-done((bf16[160,1024]{1,0:T(8,128)(2,1)}, bf16[160,1024]{1,0:T(8,128)(2,1)S(1)}, u32[]{:S(2)}, u32[]{:S(2)}) %collective-permute-start.38) | collective-permute-done | bytes 327712 | tf_op jit(solution)/shard_map/ppermute | solution.py:888
  628.2 31.8 %layer_backward.16 = (bf16[4,336,1024]{2,1,0:T(8,128)(2,1)}, bf16[4,336,3072]{2,1,0:T(8,128)(2,1)}, bf16[4,336,4096]{2,1,0:T(8,128)(2,1)}, bf16[4,336,1024]{2,1,...) custom-call(s32[5]{0:T(128)} %stack.469.flags, ...), custom_call_target="tpu_custom_call", output_to_operand_aliasing={{0}: (12, {}), {1}: (13, {}), {2}: (14, {}), {3}: (15, {}),... | custom-call | flops 8455716864 | bytes 52428800 | tf_op jit(solution)/shard_map/layer_backward/pallas_call | solution.py:788
  663.8 31.2 %layer_backward.17 = (bf16[4,336,1024]{2,1,0:T(8,128)(2,1)}, bf16[4,336,3072]{2,1,0:T(8,128)(2,1)}, bf16[4,336,4096]{2,1,0:T(8,128)(2,1)}, bf16[4,336,1024]{2,1,...) custom-call(s32[5]{0:T(128)} %stack.383.flags, ...), custom_call_target="tpu_custom_call", output_to_operand_aliasing={{0}: (12, {}), {1}: (13, {}), {2}: (14, {}), {3}: (15, {}),... | custom-call | flops 8455716864 | bytes 52428800 | tf_op jit(solution)/shard_map/layer_backward/pallas_call | solution.py:788
  701.4 31.9 %layer_backward.18 = (bf16[4,336,1024]{2,1,0:T(8,128)(2,1)}, bf16[4,336,3072]{2,1,0:T(8,128)(2,1)}, bf16[4,336,4096]{2,1,0:T(8,128)(2,1)}, bf16[4,336,1024]{2,1,...) custom-call(s32[5]{0:T(128)} %stack.473.flags, ...), custom_call_target="tpu_custom_call", output_to_operand_aliasing={{0}: (12, {}), {1}: (13, {}), {2}: (14, {}), {3}: (15, {}),... | custom-call | flops 8455716864 | bytes 52428800 | tf_op jit(solution)/shard_map/layer_backward/pallas_call | solution.py:788
  737.4 31.4 %layer_backward.19 = (bf16[4,336,1024]{2,1,0:T(8,128)(2,1)}, bf16[4,336,3072]{2,1,0:T(8,128)(2,1)}, bf16[4,336,4096]{2,1,0:T(8,128)(2,1)}, bf16[4,336,1024]{2,1,...) custom-call(s32[5]{0:T(128)} %stack.457.flags, ...), custom_call_target="tpu_custom_call", output_to_operand_aliasing={{0}: (12, {}), {1}: (13, {}), {2}: (14, {}), {3}: (15, {}),... | custom-call | flops 8455716864 | bytes 52428800 | tf_op jit(solution)/shard_map/layer_backward/pallas_call | solution.py:788
  768.9 10.4 convolution_convert_fusion.2
  822.5 10.2 add_convert_fusion.1
  839.2 13.9 %add_convert_fusion = bf16[4096,512]{1,0:T(8,128)(2,1)} fusion(bf16[4096,512]{1,0:T(8,128)(2,1)} %collective-permute-done.62, bf16[1344,4096]{1,0:T(8,128)(2,1)} %bitcast.291, bf16[1344,1024]{1,0:T(8,128)(2,1)S(1)} %bitcast.310, s32[]{:T(128)S(6)} %select_n.163), kind=kOutput, calls=%fused_computation.1 | convolution fusion | flops 5643436032 | bytes 20774916 | tf_op jit(solution)/shard_map/dot_general | solution.py:106
  888.5 11.9 %collective-permute-done.48 = bf16[1,2,160,1024]{3,2,1,0:T(8,128)(2,1)} collective-permute-done((bf16[1,2,160,1024]{3,2,1,0:T(8,128)(2,1)}, bf16[1,2,160,1024]{3,2,1,0:T(8,128)(2,1)}, u32[]{:S(2)}, u32[]{:S(2)}) %collective-permute-start.48) | collective-permute-done | bytes 655392 | tf_op jit(solution)/shard_map/ppermute | solution.py:1196
  975.1 10.3 collective-permute-done.58
  998.8 18.0 %collective-permute-done.60 = f32[48,128]{1,0:T(8,128)S(1)} collective-permute-done((f32[48,128]{1,0:T(8,128)S(1)}, f32[48,128]{1,0:T(8,128)S(1)}, u32[]{:S(2)}, u32[]{:S(2)}) %collective-permute-start.60) | collective-permute-done | bytes 24608 | tf_op jit(solution)/shard_map/ppermute | solution.py:908
  (477 shorter events, 471.0 us)
Async XLA Ops:
  7.2 228.7 %all-gather.3.cloned.1.call-start = ((), (), s32[]{:S(2)}) async-start(), calls=%async_computation.4 | async-start | bytes 28311552 | tf_op jit(solution)/shard_map/all_gather | solution.py:962
  15.4 886.3 %reduce-scatter.3.cloned.1.call-start = ((), (), s32[]{:S(2)}) async-start(), calls=%async_computation.2 | async-start | bytes 5242880 | tf_op jit(solution)/shard_map/reduce_scatter | solution.py:1177
  50.2 52.7 %collective-permute-start.6 = (bf16[8,72,1024]{2,1,0:T(8,128)(2,1)}, bf16[8,72,1024]{2,1,0:T(8,128)(2,1)}, u32[]{:S(2)}, u32[]{:S(2)}) collective-permute-start(bf16[8,72,1024]{2,1,0:T(8,128)(2,1)} %bitcast.29), channel_id=1, source_target_pairs={{0,16},{8,24},{16,0},{24,8},{1,17},{9,25},{17,1},{25,9},{2,18},{10... | collective-permute-start | bytes 3538952 | tf_op jit(solution)/shard_map/ppermute | solution.py:993
  50.4 53.8 %collective-permute-start.7 = (bf16[8,72,1024]{2,1,0:T(8,128)(2,1)}, bf16[8,72,1024]{2,1,0:T(8,128)(2,1)}, u32[]{:S(2)}, u32[]{:S(2)}) collective-permute-start(bf16[8,72,1024]{2,1,0:T(8,128)(2,1)} %bitcast.29), channel_id=1, source_target_pairs={{0,8},{8,16},{16,24},{24,0},{1,9},{9,17},{17,25},{25,1},{2,10},{10... | collective-permute-start | bytes 3538952 | tf_op jit(solution)/shard_map/ppermute | solution.py:993
  135.0 44.6 %collective-permute-start.8 = (bf16[1,2,160,1024]{3,2,1,0:T(8,128)(2,1)S(1)}, bf16[1,2,160,1024]{3,2,1,0:T(8,128)(2,1)}, u32[]{:S(2)}, u32[]{:S(2)}) collective-permute-start(bf16[1,2,160,1024]{3,2,1,0:T(8,128)(2,1)S(1)} %pad.30), channel_id=1, source_target_pairs={{8,0},{9,1},{10,2},{11,3},{12,4},{13,5},{14,6},{15,7}} | collective-permute-start | bytes 1966088 | tf_op jit(solution)/shard_map/ppermute | solution.py:1031
  136.3 44.5 %collective-permute-start.9 = (bf16[1,2,160,1024]{3,2,1,0:T(8,128)(2,1)S(1)}, bf16[1,2,160,1024]{3,2,1,0:T(8,128)(2,1)}, u32[]{:S(2)}, u32[]{:S(2)}) collective-permute-start(bf16[1,2,160,1024]{3,2,1,0:T(8,128)(2,1)S(1)} %pad.30), channel_id=1, source_target_pairs={{16,0},{17,1},{18,2},{19,3},{20,4},{21,5},{22,6},{23,7}} | collective-permute-start | bytes 1966088 | tf_op jit(solution)/shard_map/ppermute | solution.py:1031
  137.6 44.3 %collective-permute-start.10 = (bf16[1,2,160,1024]{3,2,1,0:T(8,128)(2,1)S(1)}, bf16[1,2,160,1024]{3,2,1,0:T(8,128)(2,1)}, u32[]{:S(2)}, u32[]{:S(2)}) collective-permute-start(bf16[1,2,160,1024]{3,2,1,0:T(8,128)(2,1)S(1)} %pad.30), channel_id=1, source_target_pairs={{24,0},{25,1},{26,2},{27,3},{28,4},{29,5},{30,6},{31,7}} | collective-permute-start | bytes 1966088 | tf_op jit(solution)/shard_map/ppermute | solution.py:1031
  235.9 54.1 %collective-permute-start = (bf16[4,160,1024]{2,1,0:T(8,128)(2,1)}, bf16[4,160,1024]{2,1,0:T(8,128)(2,1)}, u32[]{:S(2)}, u32[]{:S(2)}) collective-permute-start(bf16[4,160,1024]{2,1,0:T(8,128)(2,1)} %slice_bitcast_fusion.2), channel_id=1, source_target_pairs={{8,11},{9,8},{10,9},{11,10},{24,27},{25,24},{26,25},{27,26},{12,15... | collective-permute-start | bytes 3932168 | tf_op jit(solution)/shard_map/ppermute | solution.py:1060
  352.2 42.3 %collective-permute-start.21 = (bf16[160,1024]{1,0:T(8,128)(2,1)}, bf16[160,1024]{1,0:T(8,128)(2,1)S(1)}, u32[]{:S(2)}, u32[]{:S(2)}) collective-permute-start(bf16[160,1024]{1,0:T(8,128)(2,1)} %get-tuple-element.355), channel_id=1, source_target_pairs={{0,8},{1,9},{2,10},{3,11},{8,17},{9,18},{10,19},{11,16},{16,24},{1... | collective-permute-start | bytes 983048 | tf_op jit(solution)/shard_map/ppermute | solution.py:888
  369.0 42.8 %collective-permute-start.19 = (bf16[160,1024]{1,0:T(8,128)(2,1)}, bf16[160,1024]{1,0:T(8,128)(2,1)S(1)}, u32[]{:S(2)}, u32[]{:S(2)}) collective-permute-start(bf16[160,1024]{1,0:T(8,128)(2,1)} %get-tuple-element.353), channel_id=1, source_target_pairs={{0,8},{1,9},{2,10},{3,11},{8,17},{9,18},{10,19},{11,16},{16,24},{1... | collective-permute-start | bytes 983048 | tf_op jit(solution)/shard_map/ppermute | solution.py:888
  402.9 37.0 %collective-permute-start.25 = (bf16[160,1024]{1,0:T(8,128)(2,1)}, bf16[160,1024]{1,0:T(8,128)(2,1)S(1)}, u32[]{:S(2)}, u32[]{:S(2)}) collective-permute-start(bf16[160,1024]{1,0:T(8,128)(2,1)} %get-tuple-element.381), channel_id=1, source_target_pairs={{0,8},{1,9},{2,10},{3,11},{8,17},{9,18},{10,19},{11,16},{16,24},{1... | collective-permute-start | bytes 983048 | tf_op jit(solution)/shard_map/ppermute | solution.py:888
  414.3 35.8 %collective-permute-start.23 = (bf16[160,1024]{1,0:T(8,128)(2,1)}, bf16[160,1024]{1,0:T(8,128)(2,1)S(1)}, u32[]{:S(2)}, u32[]{:S(2)}) collective-permute-start(bf16[160,1024]{1,0:T(8,128)(2,1)} %get-tuple-element.379), channel_id=1, source_target_pairs={{0,8},{1,9},{2,10},{3,11},{8,17},{9,18},{10,19},{11,16},{16,24},{1... | collective-permute-start | bytes 983048 | tf_op jit(solution)/shard_map/ppermute | solution.py:888
  466.9 37.5 %collective-permute-start.27 = (bf16[160,1024]{1,0:T(8,128)(2,1)}, bf16[160,1024]{1,0:T(8,128)(2,1)S(1)}, u32[]{:S(2)}, u32[]{:S(2)}) collective-permute-start(bf16[160,1024]{1,0:T(8,128)(2,1)} %get-tuple-element.422), channel_id=1, source_target_pairs={{8,1},{9,2},{10,3},{11,0},{16,8},{17,9},{18,10},{19,11},{24,17},{2... | collective-permute-start | bytes 983048 | tf_op jit(solution)/shard_map/ppermute | solution.py:888
  468.2 36.2 %collective-permute-start.28 = (bf16[160,1024]{1,0:T(8,128)(2,1)}, bf16[160,1024]{1,0:T(8,128)(2,1)S(1)}, u32[]{:S(2)}, u32[]{:S(2)}) collective-permute-start(bf16[160,1024]{1,0:T(8,128)(2,1)} %get-tuple-element.423), channel_id=1, source_target_pairs={{8,0},{9,1},{10,2},{11,3},{16,11},{17,8},{18,9},{19,10},{24,16},{2... | collective-permute-start | bytes 983048 | tf_op jit(solution)/shard_map/ppermute | solution.py:889
  509.7 153.0 %collective-permute-start.31 = (bf16[4,160,1024]{2,1,0:T(8,128)(2,1)S(1)}, bf16[4,160,1024]{2,1,0:T(8,128)(2,1)S(1)}, u32[]{:S(2)}, u32[]{:S(2)}) collective-permute-start(bf16[4,160,1024]{2,1,0:T(8,128)(2,1)S(1)} %slice_bitcast_fusion.1), channel_id=1, source_target_pairs={{8,9},{9,10},{10,11},{11,8},{24,25},{25,26},{26,27},{27,24},{12,13... | collective-permute-start | bytes 3932168 | tf_op jit(solution)/shard_map/ppermute | solution.py:1146
  538.6 80.7 %collective-permute-start.38 = (bf16[160,1024]{1,0:T(8,128)(2,1)}, bf16[160,1024]{1,0:T(8,128)(2,1)S(1)}, u32[]{:S(2)}, u32[]{:S(2)}) collective-permute-start(bf16[160,1024]{1,0:T(8,128)(2,1)} %get-tuple-element.467), channel_id=1, source_target_pairs={{8,1},{9,2},{10,3},{11,0},{16,8},{17,9},{18,10},{19,11},{24,17},{2... | collective-permute-start | bytes 983048 | tf_op jit(solution)/shard_map/ppermute | solution.py:888
  539.9 87.5 %collective-permute-start.39 = (bf16[160,1024]{1,0:T(8,128)(2,1)}, bf16[160,1024]{1,0:T(8,128)(2,1)S(1)}, u32[]{:S(2)}, u32[]{:S(2)}) collective-permute-start(bf16[160,1024]{1,0:T(8,128)(2,1)} %get-tuple-element.468), channel_id=1, source_target_pairs={{8,0},{9,1},{10,2},{11,3},{16,11},{17,8},{18,9},{19,10},{24,16},{2... | collective-permute-start | bytes 983048 | tf_op jit(solution)/shard_map/ppermute | solution.py:889
  542.8 119.8 %collective-permute-start.36 = (bf16[160,1024]{1,0:T(8,128)(2,1)}, bf16[160,1024]{1,0:T(8,128)(2,1)S(1)}, u32[]{:S(2)}, u32[]{:S(2)}) collective-permute-start(bf16[160,1024]{1,0:T(8,128)(2,1)} %get-tuple-element.465), channel_id=1, source_target_pairs={{8,1},{9,2},{10,3},{11,0},{16,8},{17,9},{18,10},{19,11},{24,17},{2... | collective-permute-start | bytes 983048 | tf_op jit(solution)/shard_map/ppermute | solution.py:888
  544.1 118.7 %collective-permute-start.37 = (bf16[160,1024]{1,0:T(8,128)(2,1)}, bf16[160,1024]{1,0:T(8,128)(2,1)S(1)}, u32[]{:S(2)}, u32[]{:S(2)}) collective-permute-start(bf16[160,1024]{1,0:T(8,128)(2,1)} %get-tuple-element.466), channel_id=1, source_target_pairs={{8,0},{9,1},{10,2},{11,3},{16,11},{17,8},{18,9},{19,10},{24,16},{2... | collective-permute-start | bytes 983048 | tf_op jit(solution)/shard_map/ppermute | solution.py:889
  660.0 37.6 %collective-permute-start.42 = (bf16[160,1024]{1,0:T(8,128)(2,1)}, bf16[160,1024]{1,0:T(8,128)(2,1)S(1)}, u32[]{:S(2)}, u32[]{:S(2)}) collective-permute-start(bf16[160,1024]{1,0:T(8,128)(2,1)} %get-tuple-element.485), channel_id=1, source_target_pairs={{8,1},{9,2},{10,3},{11,0},{16,8},{17,9},{18,10},{19,11},{24,17},{2... | collective-permute-start | bytes 983048 | tf_op jit(solution)/shard_map/ppermute | solution.py:888
  661.3 39.3 %collective-permute-start.43 = (bf16[160,1024]{1,0:T(8,128)(2,1)}, bf16[160,1024]{1,0:T(8,128)(2,1)S(1)}, u32[]{:S(2)}, u32[]{:S(2)}) collective-permute-start(bf16[160,1024]{1,0:T(8,128)(2,1)} %get-tuple-element.486), channel_id=1, source_target_pairs={{8,0},{9,1},{10,2},{11,3},{16,11},{17,8},{18,9},{19,10},{24,16},{2... | collective-permute-start | bytes 983048 | tf_op jit(solution)/shard_map/ppermute | solution.py:889
  695.0 38.2 %collective-permute-start.40 = (bf16[160,1024]{1,0:T(8,128)(2,1)}, bf16[160,1024]{1,0:T(8,128)(2,1)S(1)}, u32[]{:S(2)}, u32[]{:S(2)}) collective-permute-start(bf16[160,1024]{1,0:T(8,128)(2,1)} %get-tuple-element.483), channel_id=1, source_target_pairs={{8,1},{9,2},{10,3},{11,0},{16,8},{17,9},{18,10},{19,11},{24,17},{2... | collective-permute-start | bytes 983048 | tf_op jit(solution)/shard_map/ppermute | solution.py:888
  696.3 40.3 %collective-permute-start.41 = (bf16[160,1024]{1,0:T(8,128)(2,1)}, bf16[160,1024]{1,0:T(8,128)(2,1)S(1)}, u32[]{:S(2)}, u32[]{:S(2)}) collective-permute-start(bf16[160,1024]{1,0:T(8,128)(2,1)} %get-tuple-element.484), channel_id=1, source_target_pairs={{8,0},{9,1},{10,2},{11,3},{16,11},{17,8},{18,9},{19,10},{24,16},{2... | collective-permute-start | bytes 983048 | tf_op jit(solution)/shard_map/ppermute | solution.py:889
  802.7 238.3 %reduce-scatter.5.cloned.1.call-start = ((), (), s32[]{:S(2)}) async-start(), calls=%async_computation.3 | async-start | bytes 10485760 | tf_op jit(solution)/shard_map/reduce_scatter | solution.py:1177
  (121 other events, 1417.3 us)
Sparse Core Ops, SparseCore 0:
  15.5 220.3 all-gather.2
  802.8 74.0 reduce-scatter.2
  879.4 152.6 reduce-scatter.4

commit v6 on v5

--- a/solution.py
+++ b/solution.py
@@ -1200,10 +1200,10 @@
     own_grads, g_proj, g_qkv = lax.optimization_barrier((own_grads, g_proj, g_qkv))
     grad_merged = own_part(from_halves(own_grads), 1).reshape(owned * rows_here, D)
     g_merge = dot_tn(merged_in, grad_merged).astype(BF16)
+    g_merge = g_merge.reshape(section_count, dp_count, tensor_count, share, D)
+    g_merge = shares_summed(g_merge.transpose(1, 0, 2, 3, 4), "dp")[0].astype(BF16)
     g_merge, dpos = lax.optimization_barrier((g_merge, dpos))
-    g_merge = g_merge.reshape(section_count, dp_count, tensor_count, share, D)
-    g_merge = shares_summed(g_merge.transpose(1, 0, 2, 3, 4), "dp")[0]
-    g_merge = shares_summed(g_merge.astype(BF16), "pipe")[0]
+    g_merge = shares_summed(g_merge, "pipe")[0]
     g_merge = shares_summed(g_merge.astype(BF16), "tensor")[0]
     grad_unit = dot_nt(grad_merged, merge_weight)
     merge_sums = jnp.stack((jnp.sum(grad_unit * raw_hat, 0), jnp.sum(grad_unit, 0)))

time: 1070 us -> 1070 us (level)
    ppermute x5, waiting for transfers between devices: 36.6 us -> 18.5 us  [summed(): values = values + lax.ppermute(values, axis, pairs)]
    unnamed x187 -> x199, local copies, waits for them, and re-layouts: 45.6 us -> 50.3 us
  transfers between devices with their start and end apart: 66 -> 66, of which waited for: 23 -> 26; matrix products, arithmetic and copies ran while one was open for 23% -> 22% of each run, Pallas kernels for 23% -> 23%
where the time goes in v6:
time: 1070 us; the launch traced here: 1050 us
  waiting for transfers between devices  297 us (28%)
  Pallas kernels  285 us (27%)
  local copies, waits for them, and re-layouts  166 us (16%)
  starting transfers between devices  150 us (14%)
  matrix products  89.4 us (8%)
  other arithmetic  35.3 us (3%)
  between operations  16.1 us (2%)
  blocking collectives  15.8 us (1%)
    pallas_call x10, Pallas kernels, layer_backward(): pl.pallas_call(backward_kernel, out_shape=shapes_of(stacks) + [jax.ShapeD...  162 us
    pallas_call x10, Pallas kernels, layer_forward(): pl.pallas_call(forward_kernel, out_shape=shapes_of(stacks) + [jax.ShapeDt...  123 us
    ppermute x16, waiting for transfers between devices, hop(): to_a = lax.ppermute(halves[1], axes, section_pairs(sections, step, (0, 1)))  81.1 us
    dot_general x9, matrix products, dot_tn(): lax.dot_general(left, right, (((0,), (0,)), ((), ())), preferred_element_...  71.9 us
    ppermute x16, starting transfers between devices, hop(): to_b = lax.ppermute(halves[0], axes, section_pairs(sections, step, (-1, 0)))  53.8 us
    all_gather x1, waiting for transfers between devices, on_device(): weights = lax.all_gather(block_rows(*shards), group_axes, axis=0)  52.7 us
    ppermute x16, starting transfers between devices, hop(): to_a = lax.ppermute(halves[1], axes, section_pairs(sections, step, (0, 1)))  51.4 us
    unnamed x199, local copies, waits for them, and re-layouts  50.3 us
  transfers between devices with their start and end apart: 66, of which 26 were waited for; matrix products, arithmetic and copies ran while one was open for 22% of the time, Pallas kernels for 23%

profile of v6, /device:TPU:9, one launch (start us, length us, event | category | flops | bytes accessed | tf_op | source)
XLA Modules:
  0.0 1054.4 jit_solution(17680415009337908549)
XLA Ops:
  27.2 13.2 %collective-permute-done.3 = bf16[72,1024]{1,0:T(8,128)(2,1)S(1)} collective-permute-done((bf16[72,1024]{1,0:T(8,128)(2,1)S(1)}, bf16[72,1024]{1,0:T(8,128)(2,1)S(1)}, u32[]{:S(2)}, u32[]{:S(2)}) %collective-permute-start.3) | collective-permute-done | bytes 147488 | tf_op jit(solution)/shard_map/ppermute | solution.py:993
  76.8 26.0 %collective-permute-done.6 = bf16[8,72,1024]{2,1,0:T(8,128)(2,1)} collective-permute-done((bf16[8,72,1024]{2,1,0:T(8,128)(2,1)}, bf16[8,72,1024]{2,1,0:T(8,128)(2,1)}, u32[]{:S(2)}, u32[]{:S(2)}) %collective-permute-start.6) | collective-permute-done | bytes 1179680 | tf_op jit(solution)/shard_map/ppermute | solution.py:993
  119.1 15.8 %all_gather.11 = f32[128,128]{1,0:T(8,128)S(1)} all-gather(f32[32,128]{1,0:T(8,128)S(1)} %fusion.42), channel_id=1, replica_groups=mesh['pipe'=4,'dp'=2,'tensor'=4] {'tensor'}, dimensions={0}, use_global_device_ids=true | all-gather | bytes 81920 | tf_op jit(solution)/shard_map/all_gather | solution.py:929
  183.2 52.7 %all-gather.3.cloned.1.call-done = bf16[24576,512]{1,0:T(8,128)(2,1)} async-done(((bf16[3072,512]{1,0:T(8,128)(2,1)}), bf16[24576,512]{1,0:T(8,128)(2,1)}) %all-gather.3.cloned.1.call-update) | async-done | bytes 25165840 | tf_op jit(solution)/shard_map/all_gather | solution.py:962
  237.6 23.7 %layer_forward.10 = (bf16[4,336,1024]{2,1,0:T(8,128)(2,1)}, bf16[4,336,3072]{2,1,0:T(8,128)(2,1)}, bf16[4,24,448,128]{3,2,1,0:T(8,128)(2,1)}, bf16[4,336,1024]{2...) custom-call(s32[5]{0:T(128)} %stack.431.flags, ...), custom_call_target="tpu_custom_call", output_to_operand_aliasing={{0}: (12, {}), {1}: (13, {}), {2}: (14, {}), {3}: (15, {}),... | custom-call | flops 8455716864 | bytes 41943040 | tf_op jit(solution)/shard_map/layer_forward/pallas_call | solution.py:737
  264.0 23.4 %layer_forward.11 = (bf16[4,336,1024]{2,1,0:T(8,128)(2,1)}, bf16[4,336,3072]{2,1,0:T(8,128)(2,1)}, bf16[4,24,448,128]{3,2,1,0:T(8,128)(2,1)}, bf16[4,336,1024]{2...) custom-call(s32[5]{0:T(128)} %stack.426.flags, ...), custom_call_target="tpu_custom_call", output_to_operand_aliasing={{0}: (12, {}), {1}: (13, {}), {2}: (14, {}), {3}: (15, {}),... | custom-call | flops 8455716864 | bytes 41943040 | tf_op jit(solution)/shard_map/layer_forward/pallas_call | solution.py:737
  290.9 23.7 %layer_forward.12 = (bf16[4,336,1024]{2,1,0:T(8,128)(2,1)}, bf16[4,336,3072]{2,1,0:T(8,128)(2,1)}, bf16[4,24,448,128]{3,2,1,0:T(8,128)(2,1)}, bf16[4,336,1024]{2...) custom-call(s32[5]{0:T(128)} %stack.395.flags, ...), custom_call_target="tpu_custom_call", output_to_operand_aliasing={{0}: (12, {}), {1}: (13, {}), {2}: (14, {}), {3}: (15, {}),... | custom-call | flops 8455716864 | bytes 41943040 | tf_op jit(solution)/shard_map/layer_forward/pallas_call | solution.py:737
  318.0 23.4 %layer_forward.13 = (bf16[4,336,1024]{2,1,0:T(8,128)(2,1)}, bf16[4,336,3072]{2,1,0:T(8,128)(2,1)}, bf16[4,24,448,128]{3,2,1,0:T(8,128)(2,1)}, bf16[4,336,1024]{2...) custom-call(s32[5]{0:T(128)} %stack.422.flags, ...), custom_call_target="tpu_custom_call", output_to_operand_aliasing={{0}: (12, {}), {1}: (13, {}), {2}: (14, {}), {3}: (15, {}),... | custom-call | flops 8455716864 | bytes 41943040 | tf_op jit(solution)/shard_map/layer_forward/pallas_call | solution.py:737
  352.3 10.9 %collective-permute-start.21 = (bf16[160,1024]{1,0:T(8,128)(2,1)}, bf16[160,1024]{1,0:T(8,128)(2,1)S(1)}, u32[]{:S(2)}, u32[]{:S(2)}) collective-permute-start(bf16[160,1024]{1,0:T(8,128)(2,1)} %get-tuple-element.355), channel_id=1, source_target_pairs={{0,8},{1,9},{2,10},{3,11},{8,17},{9,18},{10,19},{11,16},{16,24},{1... | collective-permute-start | bytes 983048 | tf_op jit(solution)/shard_map/ppermute | solution.py:888
  369.0 22.3 %collective-permute-start.19 = (bf16[160,1024]{1,0:T(8,128)(2,1)}, bf16[160,1024]{1,0:T(8,128)(2,1)S(1)}, u32[]{:S(2)}, u32[]{:S(2)}) collective-permute-start(bf16[160,1024]{1,0:T(8,128)(2,1)} %get-tuple-element.353), channel_id=1, source_target_pairs={{0,8},{1,9},{2,10},{3,11},{8,17},{9,18},{10,19},{11,16},{16,24},{1... | collective-permute-start | bytes 983048 | tf_op jit(solution)/shard_map/ppermute | solution.py:888
  415.6 24.3 %collective-permute-start.24 = (bf16[160,1024]{1,0:T(8,128)(2,1)}, bf16[160,1024]{1,0:T(8,128)(2,1)S(1)}, u32[]{:S(2)}, u32[]{:S(2)}) collective-permute-start(bf16[160,1024]{1,0:T(8,128)(2,1)} %get-tuple-element.380), channel_id=1, source_target_pairs={{0,11},{1,8},{2,9},{3,10},{8,16},{9,17},{10,18},{11,19},{16,27},{1... | collective-permute-start | bytes 983048 | tf_op jit(solution)/shard_map/ppermute | solution.py:889
  475.4 15.5 %collective-permute-done.30.recv_b = bf16[160,1024]{1,0:T(8,128)(2,1)S(1)} collective-permute-done((bf16[160,1024]{1,0:T(8,128)(2,1)}, bf16[160,1024]{1,0:T(8,128)(2,1)S(1)}, u32[]{:S(2)}, u32[]{:S(2)}) %collective-permute-start.30) | collective-permute-done | bytes 327712 | tf_op jit(solution)/shard_map/ppermute | solution.py:889
  511.7 16.9 %collective-permute-done.35.recv_b = bf16[160,1024]{1,0:T(8,128)(2,1)} collective-permute-done((bf16[160,1024]{1,0:T(8,128)(2,1)}, bf16[160,1024]{1,0:T(8,128)(2,1)}, u32[]{:S(2)}, u32[]{:S(2)}) %collective-permute-start.35) | collective-permute-done | bytes 327712 | tf_op jit(solution)/shard_map/ppermute | solution.py:889
  545.4 73.9 %collective-permute-done.38.recv_a = bf16[160,1024]{1,0:T(8,128)(2,1)S(1)} collective-permute-done((bf16[160,1024]{1,0:T(8,128)(2,1)}, bf16[160,1024]{1,0:T(8,128)(2,1)S(1)}, u32[]{:S(2)}, u32[]{:S(2)}) %collective-permute-start.38) | collective-permute-done | bytes 327712 | tf_op jit(solution)/shard_map/ppermute | solution.py:888
  628.2 31.8 %layer_backward.16 = (bf16[4,336,1024]{2,1,0:T(8,128)(2,1)}, bf16[4,336,3072]{2,1,0:T(8,128)(2,1)}, bf16[4,336,4096]{2,1,0:T(8,128)(2,1)}, bf16[4,336,1024]{2,1,...) custom-call(s32[5]{0:T(128)} %stack.469.flags, ...), custom_call_target="tpu_custom_call", output_to_operand_aliasing={{0}: (12, {}), {1}: (13, {}), {2}: (14, {}), {3}: (15, {}),... | custom-call | flops 8455716864 | bytes 52428800 | tf_op jit(solution)/shard_map/layer_backward/pallas_call | solution.py:788
  663.9 31.3 %layer_backward.17 = (bf16[4,336,1024]{2,1,0:T(8,128)(2,1)}, bf16[4,336,3072]{2,1,0:T(8,128)(2,1)}, bf16[4,336,4096]{2,1,0:T(8,128)(2,1)}, bf16[4,336,1024]{2,1,...) custom-call(s32[5]{0:T(128)} %stack.383.flags, ...), custom_call_target="tpu_custom_call", output_to_operand_aliasing={{0}: (12, {}), {1}: (13, {}), {2}: (14, {}), {3}: (15, {}),... | custom-call | flops 8455716864 | bytes 52428800 | tf_op jit(solution)/shard_map/layer_backward/pallas_call | solution.py:788
  701.5 31.9 %layer_backward.18 = (bf16[4,336,1024]{2,1,0:T(8,128)(2,1)}, bf16[4,336,3072]{2,1,0:T(8,128)(2,1)}, bf16[4,336,4096]{2,1,0:T(8,128)(2,1)}, bf16[4,336,1024]{2,1,...) custom-call(s32[5]{0:T(128)} %stack.473.flags, ...), custom_call_target="tpu_custom_call", output_to_operand_aliasing={{0}: (12, {}), {1}: (13, {}), {2}: (14, {}), {3}: (15, {}),... | custom-call | flops 8455716864 | bytes 52428800 | tf_op jit(solution)/shard_map/layer_backward/pallas_call | solution.py:788
  737.6 31.5 %layer_backward.19 = (bf16[4,336,1024]{2,1,0:T(8,128)(2,1)}, bf16[4,336,3072]{2,1,0:T(8,128)(2,1)}, bf16[4,336,4096]{2,1,0:T(8,128)(2,1)}, bf16[4,336,1024]{2,1,...) custom-call(s32[5]{0:T(128)} %stack.457.flags, ...), custom_call_target="tpu_custom_call", output_to_operand_aliasing={{0}: (12, {}), {1}: (13, {}), {2}: (14, {}), {3}: (15, {}),... | custom-call | flops 8455716864 | bytes 52428800 | tf_op jit(solution)/shard_map/layer_backward/pallas_call | solution.py:788
  769.1 10.4 convolution_convert_fusion.2
  803.4 10.2 convolution_convert_fusion.1
  822.7 10.2 add_convert_fusion.1
  839.4 13.9 %add_convert_fusion = bf16[4096,512]{1,0:T(8,128)(2,1)} fusion(bf16[4096,512]{1,0:T(8,128)(2,1)} %collective-permute-done.62, bf16[1344,4096]{1,0:T(8,128)(2,1)} %bitcast.284, bf16[1344,1024]{1,0:T(8,128)(2,1)S(1)} %bitcast.303, s32[]{:T(128)S(6)} %select_n.163), kind=kOutput, calls=%fused_computation.1 | convolution fusion | flops 5643436032 | bytes 20774916 | tf_op jit(solution)/shard_map/dot_general | solution.py:106
  888.0 12.7 %collective-permute-done.48 = bf16[1,2,160,1024]{3,2,1,0:T(8,128)(2,1)} collective-permute-done((bf16[1,2,160,1024]{3,2,1,0:T(8,128)(2,1)}, bf16[1,2,160,1024]{3,2,1,0:T(8,128)(2,1)}, u32[]{:S(2)}, u32[]{:S(2)}) %collective-permute-start.48) | collective-permute-done | bytes 655392 | tf_op jit(solution)/shard_map/ppermute | solution.py:1196
  1022.3 16.2 %collective-permute-done.54 = bf16[1,64,1024]{2,1,0:T(8,128)(2,1)S(1)} collective-permute-done((bf16[1,64,1024]{2,1,0:T(8,128)(2,1)S(1)}, bf16[1,64,1024]{2,1,0:T(8,128)(2,1)S(1)}, u32[]{:S(2)}, u32[]{:S(2)}) %collective-permute-start.54) | collective-permute-done | bytes 131104 | tf_op jit(solution)/shard_map/ppermute | solution.py:900
  (489 shorter events, 472.3 us)
Async XLA Ops:
  7.2 228.7 %all-gather.3.cloned.1.call-start = ((), (), s32[]{:S(2)}) async-start(), calls=%async_computation.4 | async-start | bytes 28311552 | tf_op jit(solution)/shard_map/all_gather | solution.py:962
  15.4 885.5 %reduce-scatter.3.cloned.1.call-start = ((), (), s32[]{:S(2)}) async-start(), calls=%async_computation.2 | async-start | bytes 5242880 | tf_op jit(solution)/shard_map/reduce_scatter | solution.py:1177
  50.2 52.7 %collective-permute-start.6 = (bf16[8,72,1024]{2,1,0:T(8,128)(2,1)}, bf16[8,72,1024]{2,1,0:T(8,128)(2,1)}, u32[]{:S(2)}, u32[]{:S(2)}) collective-permute-start(bf16[8,72,1024]{2,1,0:T(8,128)(2,1)} %bitcast.29), channel_id=1, source_target_pairs={{0,16},{8,24},{16,0},{24,8},{1,17},{9,25},{17,1},{25,9},{2,18},{10... | collective-permute-start | bytes 3538952 | tf_op jit(solution)/shard_map/ppermute | solution.py:993
  50.4 53.8 %collective-permute-start.7 = (bf16[8,72,1024]{2,1,0:T(8,128)(2,1)}, bf16[8,72,1024]{2,1,0:T(8,128)(2,1)}, u32[]{:S(2)}, u32[]{:S(2)}) collective-permute-start(bf16[8,72,1024]{2,1,0:T(8,128)(2,1)} %bitcast.29), channel_id=1, source_target_pairs={{0,8},{8,16},{16,24},{24,0},{1,9},{9,17},{17,25},{25,1},{2,10},{10... | collective-permute-start | bytes 3538952 | tf_op jit(solution)/shard_map/ppermute | solution.py:993
  135.0 44.7 %collective-permute-start.8 = (bf16[1,2,160,1024]{3,2,1,0:T(8,128)(2,1)S(1)}, bf16[1,2,160,1024]{3,2,1,0:T(8,128)(2,1)}, u32[]{:S(2)}, u32[]{:S(2)}) collective-permute-start(bf16[1,2,160,1024]{3,2,1,0:T(8,128)(2,1)S(1)} %pad.30), channel_id=1, source_target_pairs={{8,0},{9,1},{10,2},{11,3},{12,4},{13,5},{14,6},{15,7}} | collective-permute-start | bytes 1966088 | tf_op jit(solution)/shard_map/ppermute | solution.py:1031
  136.3 44.6 %collective-permute-start.9 = (bf16[1,2,160,1024]{3,2,1,0:T(8,128)(2,1)S(1)}, bf16[1,2,160,1024]{3,2,1,0:T(8,128)(2,1)}, u32[]{:S(2)}, u32[]{:S(2)}) collective-permute-start(bf16[1,2,160,1024]{3,2,1,0:T(8,128)(2,1)S(1)} %pad.30), channel_id=1, source_target_pairs={{16,0},{17,1},{18,2},{19,3},{20,4},{21,5},{22,6},{23,7}} | collective-permute-start | bytes 1966088 | tf_op jit(solution)/shard_map/ppermute | solution.py:1031
  137.6 44.4 %collective-permute-start.10 = (bf16[1,2,160,1024]{3,2,1,0:T(8,128)(2,1)S(1)}, bf16[1,2,160,1024]{3,2,1,0:T(8,128)(2,1)}, u32[]{:S(2)}, u32[]{:S(2)}) collective-permute-start(bf16[1,2,160,1024]{3,2,1,0:T(8,128)(2,1)S(1)} %pad.30), channel_id=1, source_target_pairs={{24,0},{25,1},{26,2},{27,3},{28,4},{29,5},{30,6},{31,7}} | collective-permute-start | bytes 1966088 | tf_op jit(solution)/shard_map/ppermute | solution.py:1031
  235.9 54.1 %collective-permute-start = (bf16[4,160,1024]{2,1,0:T(8,128)(2,1)}, bf16[4,160,1024]{2,1,0:T(8,128)(2,1)}, u32[]{:S(2)}, u32[]{:S(2)}) collective-permute-start(bf16[4,160,1024]{2,1,0:T(8,128)(2,1)} %slice_bitcast_fusion.2), channel_id=1, source_target_pairs={{8,11},{9,8},{10,9},{11,10},{24,27},{25,24},{26,25},{27,26},{12,15... | collective-permute-start | bytes 3932168 | tf_op jit(solution)/shard_map/ppermute | solution.py:1060
  352.3 42.3 %collective-permute-start.21 = (bf16[160,1024]{1,0:T(8,128)(2,1)}, bf16[160,1024]{1,0:T(8,128)(2,1)S(1)}, u32[]{:S(2)}, u32[]{:S(2)}) collective-permute-start(bf16[160,1024]{1,0:T(8,128)(2,1)} %get-tuple-element.355), channel_id=1, source_target_pairs={{0,8},{1,9},{2,10},{3,11},{8,17},{9,18},{10,19},{11,16},{16,24},{1... | collective-permute-start | bytes 983048 | tf_op jit(solution)/shard_map/ppermute | solution.py:888
  369.0 42.8 %collective-permute-start.19 = (bf16[160,1024]{1,0:T(8,128)(2,1)}, bf16[160,1024]{1,0:T(8,128)(2,1)S(1)}, u32[]{:S(2)}, u32[]{:S(2)}) collective-permute-start(bf16[160,1024]{1,0:T(8,128)(2,1)} %get-tuple-element.353), channel_id=1, source_target_pairs={{0,8},{1,9},{2,10},{3,11},{8,17},{9,18},{10,19},{11,16},{16,24},{1... | collective-permute-start | bytes 983048 | tf_op jit(solution)/shard_map/ppermute | solution.py:888
  402.9 37.0 %collective-permute-start.25 = (bf16[160,1024]{1,0:T(8,128)(2,1)}, bf16[160,1024]{1,0:T(8,128)(2,1)S(1)}, u32[]{:S(2)}, u32[]{:S(2)}) collective-permute-start(bf16[160,1024]{1,0:T(8,128)(2,1)} %get-tuple-element.381), channel_id=1, source_target_pairs={{0,8},{1,9},{2,10},{3,11},{8,17},{9,18},{10,19},{11,16},{16,24},{1... | collective-permute-start | bytes 983048 | tf_op jit(solution)/shard_map/ppermute | solution.py:888
  414.3 35.8 %collective-permute-start.23 = (bf16[160,1024]{1,0:T(8,128)(2,1)}, bf16[160,1024]{1,0:T(8,128)(2,1)S(1)}, u32[]{:S(2)}, u32[]{:S(2)}) collective-permute-start(bf16[160,1024]{1,0:T(8,128)(2,1)} %get-tuple-element.379), channel_id=1, source_target_pairs={{0,8},{1,9},{2,10},{3,11},{8,17},{9,18},{10,19},{11,16},{16,24},{1... | collective-permute-start | bytes 983048 | tf_op jit(solution)/shard_map/ppermute | solution.py:888
  466.9 37.5 %collective-permute-start.27 = (bf16[160,1024]{1,0:T(8,128)(2,1)}, bf16[160,1024]{1,0:T(8,128)(2,1)S(1)}, u32[]{:S(2)}, u32[]{:S(2)}) collective-permute-start(bf16[160,1024]{1,0:T(8,128)(2,1)} %get-tuple-element.422), channel_id=1, source_target_pairs={{8,1},{9,2},{10,3},{11,0},{16,8},{17,9},{18,10},{19,11},{24,17},{2... | collective-permute-start | bytes 983048 | tf_op jit(solution)/shard_map/ppermute | solution.py:888
  468.2 36.2 %collective-permute-start.28 = (bf16[160,1024]{1,0:T(8,128)(2,1)}, bf16[160,1024]{1,0:T(8,128)(2,1)S(1)}, u32[]{:S(2)}, u32[]{:S(2)}) collective-permute-start(bf16[160,1024]{1,0:T(8,128)(2,1)} %get-tuple-element.423), channel_id=1, source_target_pairs={{8,0},{9,1},{10,2},{11,3},{16,11},{17,8},{18,9},{19,10},{24,16},{2... | collective-permute-start | bytes 983048 | tf_op jit(solution)/shard_map/ppermute | solution.py:889
  509.7 153.0 %collective-permute-start.31 = (bf16[4,160,1024]{2,1,0:T(8,128)(2,1)S(1)}, bf16[4,160,1024]{2,1,0:T(8,128)(2,1)S(1)}, u32[]{:S(2)}, u32[]{:S(2)}) collective-permute-start(bf16[4,160,1024]{2,1,0:T(8,128)(2,1)S(1)} %slice_bitcast_fusion.1), channel_id=1, source_target_pairs={{8,9},{9,10},{10,11},{11,8},{24,25},{25,26},{26,27},{27,24},{12,13... | collective-permute-start | bytes 3932168 | tf_op jit(solution)/shard_map/ppermute | solution.py:1146
  538.6 80.7 %collective-permute-start.38 = (bf16[160,1024]{1,0:T(8,128)(2,1)}, bf16[160,1024]{1,0:T(8,128)(2,1)S(1)}, u32[]{:S(2)}, u32[]{:S(2)}) collective-permute-start(bf16[160,1024]{1,0:T(8,128)(2,1)} %get-tuple-element.467), channel_id=1, source_target_pairs={{8,1},{9,2},{10,3},{11,0},{16,8},{17,9},{18,10},{19,11},{24,17},{2... | collective-permute-start | bytes 983048 | tf_op jit(solution)/shard_map/ppermute | solution.py:888
  539.9 87.5 %collective-permute-start.39 = (bf16[160,1024]{1,0:T(8,128)(2,1)}, bf16[160,1024]{1,0:T(8,128)(2,1)S(1)}, u32[]{:S(2)}, u32[]{:S(2)}) collective-permute-start(bf16[160,1024]{1,0:T(8,128)(2,1)} %get-tuple-element.468), channel_id=1, source_target_pairs={{8,0},{9,1},{10,2},{11,3},{16,11},{17,8},{18,9},{19,10},{24,16},{2... | collective-permute-start | bytes 983048 | tf_op jit(solution)/shard_map/ppermute | solution.py:889
  542.8 119.8 %collective-permute-start.36 = (bf16[160,1024]{1,0:T(8,128)(2,1)}, bf16[160,1024]{1,0:T(8,128)(2,1)S(1)}, u32[]{:S(2)}, u32[]{:S(2)}) collective-permute-start(bf16[160,1024]{1,0:T(8,128)(2,1)} %get-tuple-element.465), channel_id=1, source_target_pairs={{8,1},{9,2},{10,3},{11,0},{16,8},{17,9},{18,10},{19,11},{24,17},{2... | collective-permute-start | bytes 983048 | tf_op jit(solution)/shard_map/ppermute | solution.py:888
  544.1 118.8 %collective-permute-start.37 = (bf16[160,1024]{1,0:T(8,128)(2,1)}, bf16[160,1024]{1,0:T(8,128)(2,1)S(1)}, u32[]{:S(2)}, u32[]{:S(2)}) collective-permute-start(bf16[160,1024]{1,0:T(8,128)(2,1)} %get-tuple-element.466), channel_id=1, source_target_pairs={{8,0},{9,1},{10,2},{11,3},{16,11},{17,8},{18,9},{19,10},{24,16},{2... | collective-permute-start | bytes 983048 | tf_op jit(solution)/shard_map/ppermute | solution.py:889
  660.0 37.8 %collective-permute-start.42 = (bf16[160,1024]{1,0:T(8,128)(2,1)}, bf16[160,1024]{1,0:T(8,128)(2,1)S(1)}, u32[]{:S(2)}, u32[]{:S(2)}) collective-permute-start(bf16[160,1024]{1,0:T(8,128)(2,1)} %get-tuple-element.485), channel_id=1, source_target_pairs={{8,1},{9,2},{10,3},{11,0},{16,8},{17,9},{18,10},{19,11},{24,17},{2... | collective-permute-start | bytes 983048 | tf_op jit(solution)/shard_map/ppermute | solution.py:888
  661.3 39.5 %collective-permute-start.43 = (bf16[160,1024]{1,0:T(8,128)(2,1)}, bf16[160,1024]{1,0:T(8,128)(2,1)S(1)}, u32[]{:S(2)}, u32[]{:S(2)}) collective-permute-start(bf16[160,1024]{1,0:T(8,128)(2,1)} %get-tuple-element.486), channel_id=1, source_target_pairs={{8,0},{9,1},{10,2},{11,3},{16,11},{17,8},{18,9},{19,10},{24,16},{2... | collective-permute-start | bytes 983048 | tf_op jit(solution)/shard_map/ppermute | solution.py:889
  695.2 38.3 %collective-permute-start.40 = (bf16[160,1024]{1,0:T(8,128)(2,1)}, bf16[160,1024]{1,0:T(8,128)(2,1)S(1)}, u32[]{:S(2)}, u32[]{:S(2)}) collective-permute-start(bf16[160,1024]{1,0:T(8,128)(2,1)} %get-tuple-element.483), channel_id=1, source_target_pairs={{8,1},{9,2},{10,3},{11,0},{16,8},{17,9},{18,10},{19,11},{24,17},{2... | collective-permute-start | bytes 983048 | tf_op jit(solution)/shard_map/ppermute | solution.py:888
  696.5 40.4 %collective-permute-start.41 = (bf16[160,1024]{1,0:T(8,128)(2,1)}, bf16[160,1024]{1,0:T(8,128)(2,1)S(1)}, u32[]{:S(2)}, u32[]{:S(2)}) collective-permute-start(bf16[160,1024]{1,0:T(8,128)(2,1)} %get-tuple-element.484), channel_id=1, source_target_pairs={{8,0},{9,1},{10,2},{11,3},{16,11},{17,8},{18,9},{19,10},{24,16},{2... | collective-permute-start | bytes 983048 | tf_op jit(solution)/shard_map/ppermute | solution.py:889
  802.9 238.2 %reduce-scatter.5.cloned.1.call-start = ((), (), s32[]{:S(2)}) async-start(), calls=%async_computation.3 | async-start | bytes 10485760 | tf_op jit(solution)/shard_map/reduce_scatter | solution.py:1177
  (127 other events, 1392.0 us)
Sparse Core Ops, SparseCore 0:
  15.5 220.3 all-gather.2
  803.1 74.0 reduce-scatter.2
  879.7 161.3 reduce-scatter.4
